TPU v7x, 32 devices: a whole 2x2x4 slice. The times are simulated.
32 devices in a mesh: groups: 2 (over x), ctx: 4 (over y, core), tp: 4 (over z).
Axes of the slice: x: 2, y: 2, z: 4, core: 2. Of those that a mesh axis runs over, the one named last changes fastest.
Arguments:
- queries: bfloat16 [3072, 8192], P(('groups', 'ctx'), 'tp'), parts along dimension 0, may hold values from -6 to 6
- key_states: bfloat16 [3072, 1024], P(('groups', 'ctx'), 'tp'), parts along dimension 0, may hold values from -6 to 6
- value_tensor: bfloat16 [3072, 1024], P(('groups', 'ctx'), 'tp'), parts along dimension 0, may hold values from -6 to 6
- output_gradient: bfloat16 [3072, 8192], P(('groups', 'ctx'), 'tp'), parts along dimension 0, may hold values from -6 to 6
- parent: int32 [24], P('groups'), parts along dimension 0, may hold values from -1 to 8, as said below
- block_owner: int32 [24], P('groups'), parts along dimension 0, may hold values from 0 to 11, as said below
Outputs:
- attn_out: bfloat16 [3072, 8192], P(('groups', 'ctx'), 'tp'), parts along dimension 0
- d_queries: bfloat16 [3072, 8192], P(('groups', 'ctx'), 'tp'), parts along dimension 0
- d_keys: bfloat16 [3072, 1024], P(('groups', 'ctx'), 'tp'), parts along dimension 0
- d_values: bfloat16 [3072, 1024], P(('groups', 'ctx'), 'tp'), parts along dimension 0
There are 2 independent parts, one for each index of `groups`. A program takes and returns all parts, laid end to end along the dimension named above; each array names one. Nothing has to cross between parts.
Inputs may be any that keep to these rules, and one draw needn't show every extreme that they name: Tree block ids are ordered so that a parent comes before its children. All blocks of one stored shard (3 blocks in a row) lie at one depth of the tree, and their parents lie on one other shard, so a block's ancestors are never on its own shard. A path from a root holds at most 16 blocks; some path reaches 16 where the group has 16 shards or more. The blocks of one shard have ancestors among at most 2 blocks of any other one shard, and every shard that is not at depth 0 reaches 2 with its parent shard. `block_owner`: A permutation of the stored blocks that keeps each shard's blocks together.
All inputs are finite; a program needn't handle non-finite values.
Results may differ from a plain program's by a relative error of at most 0.015.
Values may be sent and summed in bfloat16 or wider, within the bound.
No kernel may reach another device: no remote copies, remote signals or barrier semaphores. Data moves between devices by JAX's collectives and lax.ppermute only.
A program may use at most 192 MiB of HBM per device.

v0:
```python
import math

import jax
import jax.numpy as jnp
from jax import lax
from jax.sharding import PartitionSpec as P

QUERY_HEADS = 64
KEY_VALUE_HEADS = 8
HEAD_SIZE = 128
TREE_BLOCK_SIZE = 128
PATH_DEPTH_MAX = 16


def lookup_table(lookup_values, index):
    places = jnp.arange(lookup_values.shape[0], dtype=jnp.int32)
    matches = index[..., None] == places
    return jnp.sum(jnp.where(matches, lookup_values, 0), axis=-1)


def ancestor_table(parent, block_owner, chain_depth):
    places = jnp.arange(block_owner.shape[0], dtype=jnp.int32)
    holder = jnp.sum(jnp.where(block_owner[None, :] == places[:, None], places[None, :], 0), axis=1)
    current = holder
    columns = [places]
    for hop_index in range(chain_depth - 1):
        current = jnp.where(current >= 0, lookup_table(parent, jnp.maximum(current, 0)), -1)
        columns.append(
            jnp.where(current >= 0, lookup_table(block_owner, jnp.maximum(current, 0)), -1)
        )
    return jnp.stack(columns, axis=1)


def visible_mask(ancestry, block_len):
    row_index = jnp.arange(block_len)[:, None]
    key_index = jnp.arange(ancestry.shape[0] * block_len)[None, :]
    live_slot = jnp.repeat(ancestry >= 0, block_len)[None, :]
    return jnp.where(key_index // block_len == 0, key_index % block_len <= row_index, live_slot)


def attend_block(query_block, grad_block, key_row_list, value_row_list, visible, score_scale):
    scores = (
        jnp.einsum("qhgd,khd->hgqk", query_block, key_row_list, preferred_element_type=jnp.float32)
        * score_scale
    )
    scores = jnp.where(visible, scores, -jnp.inf)
    highest = jnp.max(scores, axis=-1, keepdims=True)
    totals = jnp.sum(jnp.exp(scores - highest), axis=-1, keepdims=True)
    probabilities = jnp.exp(scores - (highest + jnp.log(totals)))
    weights = probabilities.astype(jnp.bfloat16)
    attended = jnp.einsum(
        "hgqk,khd->qhgd", weights, value_row_list, preferred_element_type=jnp.float32
    ).astype(jnp.bfloat16)
    row_inner = jnp.transpose(
        jnp.sum(grad_block.astype(jnp.float32) * attended.astype(jnp.float32), axis=-1), (1, 2, 0)
    )
    dprobs = jnp.einsum(
        "qhgd,khd->hgqk", grad_block, value_row_list, preferred_element_type=jnp.float32
    )
    dscores = (probabilities * (dprobs - row_inner[..., None])).astype(jnp.bfloat16)
    dquery = (
        jnp.einsum("hgqk,khd->qhgd", dscores, key_row_list, preferred_element_type=jnp.float32)
        * score_scale
    ).astype(jnp.bfloat16)
    key_grad = (
        jnp.einsum("hgqk,qhgd->khd", dscores, query_block, preferred_element_type=jnp.float32)
        * score_scale
    )
    dvalues = jnp.einsum("hgqk,qhgd->khd", weights, grad_block, preferred_element_type=jnp.float32)
    return (attended, dquery, key_grad, dvalues)


def body(queries, key_states, value_tensor, output_gradient, parent, block_owner):
    block_len = TREE_BLOCK_SIZE
    chain_depth = PATH_DEPTH_MAX
    head_dim = HEAD_SIZE
    groups_each_split = QUERY_HEADS // KEY_VALUE_HEADS
    score_scale = 1.0 / math.sqrt(head_dim)
    tok_dev = queries.shape[0]
    per_shard = tok_dev // block_len
    row_span_width = key_states.shape[1]
    kv_heads = row_span_width // head_dim
    myself = lax.axis_index("ctx")
    ancestry_all = ancestor_table(parent, block_owner, chain_depth)
    my_ancestry = lax.dynamic_slice_in_dim(ancestry_all, myself * per_shard, per_shard, 0)
    ancestry_flat = my_ancestry.reshape(-1)
    slot_count = per_shard * chain_depth
    piece_keys = lax.all_gather(key_states, "ctx", axis=0, tiled=True)
    piece_values = lax.all_gather(value_tensor, "ctx", axis=0, tiled=True)
    piece_blocks = piece_keys.shape[0] // block_len
    hit_table = (ancestry_flat[:, None] == jnp.arange(piece_blocks)[None, :]).astype(jnp.bfloat16)
    new_keys = jnp.einsum(
        "sn,nbx->sbx",
        hit_table,
        piece_keys.reshape(piece_blocks, block_len, row_span_width),
        preferred_element_type=jnp.float32,
    )
    new_values = jnp.einsum(
        "sn,nbx->sbx",
        hit_table,
        piece_values.reshape(piece_blocks, block_len, row_span_width),
        preferred_element_type=jnp.float32,
    )
    slot_keys = new_keys.astype(jnp.bfloat16)
    slot_values = new_values.astype(jnp.bfloat16)
    query_block_list = queries.reshape(per_shard, block_len, kv_heads, groups_each_split, head_dim)
    gradient_block_list = output_gradient.reshape(
        per_shard, block_len, kv_heads, groups_each_split, head_dim
    )
    key_block_list = slot_keys.reshape(per_shard, chain_depth * block_len, kv_heads, head_dim)
    value_block_list = slot_values.reshape(per_shard, chain_depth * block_len, kv_heads, head_dim)
    masks = jax.vmap(lambda ancestry: visible_mask(ancestry, block_len))(my_ancestry)

    def one_block(block_items):
        return attend_block(*block_items, score_scale)

    attended, dquery, key_grad, dvalues = lax.map(
        one_block, (query_block_list, gradient_block_list, key_block_list, value_block_list, masks)
    )
    slot_grads = jnp.concatenate(
        [
            key_grad.reshape(slot_count, block_len, row_span_width),
            dvalues.reshape(slot_count, block_len, row_span_width),
        ],
        axis=-1,
    )
    term_blocks = tok_dev * lax.axis_size("ctx") // block_len
    inside = (ancestry_flat >= 0) & (ancestry_flat >= 0) & (ancestry_flat < term_blocks)
    targets = jnp.where(inside, ancestry_flat, term_blocks)
    partial_sums = jax.ops.segment_sum(slot_grads, targets, num_segments=term_blocks + 1)[
        :term_blocks
    ]
    summed = lax.psum_scatter(
        partial_sums.reshape(tok_dev * lax.axis_size("ctx"), 2 * row_span_width),
        "ctx",
        scatter_dimension=0,
        tiled=True,
    )
    attn_out = attended.reshape(tok_dev, -1)
    d_queries = dquery.reshape(tok_dev, -1)
    d_keys = summed[:, :row_span_width].astype(jnp.bfloat16)
    d_values = summed[:, row_span_width:].astype(jnp.bfloat16)
    return (attn_out, d_queries, d_keys, d_values)


def solution(mesh):
    placed = (
        P(("groups", "ctx"), "tp"),
        P(("groups", "ctx"), "tp"),
        P(("groups", "ctx"), "tp"),
        P(("groups", "ctx"), "tp"),
        P("groups"),
        P("groups"),
    )
    return jax.shard_map(
        body,
        mesh=mesh,
        in_specs=placed,
        out_specs=(
            P(("groups", "ctx"), "tp"),
            P(("groups", "ctx"), "tp"),
            P(("groups", "ctx"), "tp"),
            P(("groups", "ctx"), "tp"),
        ),
        check_vma=False,
    )
```

profile of v0, /device:TPU:0, one launch (start us, length us, event | category | flops | bytes accessed | tf_op | source)
XLA Modules:
  0.0 398.2 jit_solution(4142831048781948340)
XLA Ops:
  25.0 10.3 %all_gather.6 = bf16[1536,256]{1,0:T(8,128)(2,1)S(1)} all-gather(bf16[384,256]{1,0:T(8,128)(2,1)} %param.10), channel_id=1, replica_groups=mesh['groups'=2,'ctx'=4,'tp'=4] {'ctx'}, dimensions={0}, use_global_device_ids=true | all-gather | bytes 983040 | tf_op jit(solution)/shard_map/all_gather | solution.py:89
  37.4 3.0 reshape.1172
  40.8 8.9 %all_gather.7 = bf16[1536,256]{1,0:T(8,128)(2,1)S(1)} all-gather(bf16[384,256]{1,0:T(8,128)(2,1)} %param.9), channel_id=1, replica_groups=mesh['groups'=2,'ctx'=4,'tp'=4] {'ctx'}, dimensions={0}, use_global_device_ids=true | all-gather | bytes 983040 | tf_op jit(solution)/shard_map/all_gather | solution.py:88
  51.9 3.0 reshape.1174
  54.9 3.0 copy.141
  57.9 3.0 copy.142
  60.9 3.4 broadcast_select_fusion
  64.3 237.0 %while.16 = (s32[]{:T(128)}, bf16[3,128,2,8,128]{4,3,2,1,0:T(8,128)(2,1)}, bf16[3,128,2,8,128]{4,3,2,1,0:T(8,128)(2,1)}, f32[3,2048,2,128]{3,2,1,0:T(2,128)}, f3...) while((s32[]{:T(128)}, ...), condition=%wide.region_35.36_spmd, body=%wide.region_31.35_spmd.sunk | while | flops 6532886528 | bytes 193290480 | solution.py:117
  68.2 7.1 %fusion.63 = (f32[2,8,128]{2,1,0:T(8,128)S(1)}, f32[2,2048,128,8]{2,1,3,0:T(8,128)}) fusion(pred[128,2048]{0,1:T(8,128)(4,1)S(1)} %dynamic-slice_bitcast_fusion.2, bf16[1,128,2,8,128]{4,3,2,1,0:T(8,128)(2,1)S(1)} %constant_dynamic-slice_fusion.10, bf16[1,2048,2,128]{3,2,1,0:T(2,128)(2,1)S(1)} %constant_dynamic-slice_fusion.11), kind=kOutput, calls=%fused_computation.8.clone.1 | convolution fusion | flops 1086322688 | bytes 18620416 | tf_op jit(solution)/shard_map/while/body/eval_jaxpr/qhgd,khd->hgqk/dot_general | solution.py:43
  76.8 9.1 %exponential_reduce_fusion.2 = f32[2,8,128]{2,1,0:T(8,128)S(1)} fusion(f32[2,2048,128,8]{2,1,3,0:T(8,128)} %get-tuple-element.248, f32[2,8,128]{2,1,0:T(8,128)S(1)} %get-tuple-element.249, pred[128,2048]{0,1:T(8,128)(4,1)S(1)} %dynamic-slice_bitcast_fusion.2), kind=kLoop, calls=%fused_computation.6.clone.1 | loop fusion | flops 16775168 | bytes 17055744 | tf_op jit(solution)/shard_map/while/body/eval_jaxpr/reduce_sum | solution.py:48
  87.8 2.1 copy.174
  89.9 10.9 %multiply_reduce_fusion.2 = (f32[128,2,8]{0,2,1:T(8,128)S(1)}, bf16[2,128,8,128]{3,1,2,0:T(8,128)(2,1)}) fusion(bf16[1,128,2,8,128]{1,4,3,2,0:T(8,128)(2,1)S(1)} %copy.173, f32[2,2048,128,8]{2,1,3,0:T(8,128)} %get-tuple-element.248, f32[2,8,128]{2,1,0:T(8,128)S(1)} %log_add_fusion.2, pred[128,2048]{0,1:T(8,128)(4,1)S(1)} %dynamic-slice_bitcast_fusion.2, ...), kind=kOutput, calls=%fused_computation.20.clone.1 | convolution fusion | flops 1091827712 | bytes 19152896 | tf_op jit(solution)/shard_map/while/body/eval_jaxpr/hgqk,khd->qhgd/dot_general | solution.py:51
  100.8 8.7 %fusion.64 = bf16[2,8,128,2048]{2,3,1,0:T(8,128)(2,1)S(1)} fusion(f32[2,2048,128,8]{2,1,3,0:T(8,128)} %get-tuple-element.248, f32[2,8,128]{2,1,0:T(8,128)S(1)} %bitcast.218, f32[2,8,128]{2,1,0:T(8,128)S(1)} %log_add_fusion.2, pred[128,2048]{0,1:T(8,128)(4,1)S(1)} %dynamic-slice_bitcast_fusion.2, bf16[1,2048,2,128]{1,3,2,0:T(8,128)(2,1)S(1)} %copy-done.1, ...), kind=kOutput, calls=%fused_computation.3.clone.1 | convolution fusion | flops 1098907648 | bytes 27017216 | tf_op jit(solution)/shard_map/while/body/eval_jaxpr/qhgd,khd->hgqk/dot_general | solution.py:57
  109.5 3.2 copy-done
  116.1 9.3 %convolution_bitcast_fusion.3 = f32[1,2048,2,128]{1,3,2,0:T(8,128)} fusion(bf16[1,128,2,8,128]{1,4,3,2,0:T(8,128)(2,1)S(1)} %copy.173, f32[2,2048,128,8]{2,1,3,0:T(8,128)} %get-tuple-element.248, f32[2,8,128]{2,1,0:T(8,128)S(1)} %log_add_fusion.2, pred[128,2048]{0,1:T(8,128)(4,1)S(1)} %dynamic-slice_bitcast_fusion.2), kind=kOutput, calls=%fused_computation.9.clone.1 | convolution fusion | flops 1090519040 | bytes 19668992 | tf_op jit(solution)/shard_map/while/body/eval_jaxpr/hgqk,qhgd->khd/dot_general | solution.py:69
  125.4 2.8 copy.177
  128.3 7.5 %fusion.66 = f32[1,2048,2,128]{1,3,2,0:T(8,128)} fusion(bf16[2,8,128,2048]{2,3,1,0:T(8,128)(2,1)} %copy-done, bf16[1,128,2,8,128]{4,3,2,1,0:T(8,128)(2,1)S(1)} %constant_dynamic-slice_fusion.10), kind=kOutput, calls=%fused_computation.12.clone.1 | convolution fusion | flops 1074266112 | bytes 11010048 | tf_op jit(solution)/shard_map/while/body/eval_jaxpr/hgqk,qhgd->khd/dot_general | solution.py:66
  135.8 4.1 %copy.178 = f32[1,2048,2,128]{3,2,1,0:T(2,128)} copy(f32[1,2048,2,128]{1,3,2,0:T(8,128)} %fusion.66) | data formatting | bytes 4194304 | tf_op jit(solution)/shard_map/while/body/jit(dynamic_update_index_in_dim)/dynamic_update_slice | solution.py:117
  139.9 3.5 constant_dynamic-update-slice_fusion.7
  147.3 7.1 %fusion.63 = (f32[2,8,128]{2,1,0:T(8,128)S(1)}, f32[2,2048,128,8]{2,1,3,0:T(8,128)}) fusion(pred[128,2048]{0,1:T(8,128)(4,1)S(1)} %dynamic-slice_bitcast_fusion.2, bf16[1,128,2,8,128]{4,3,2,1,0:T(8,128)(2,1)S(1)} %constant_dynamic-slice_fusion.10, bf16[1,2048,2,128]{3,2,1,0:T(2,128)(2,1)S(1)} %constant_dynamic-slice_fusion.11), kind=kOutput, calls=%fused_computation.8.clone.1 | convolution fusion | flops 1086322688 | bytes 18620416 | tf_op jit(solution)/shard_map/while/body/eval_jaxpr/qhgd,khd->hgqk/dot_general | solution.py:43
  155.9 9.1 %exponential_reduce_fusion.2 = f32[2,8,128]{2,1,0:T(8,128)S(1)} fusion(f32[2,2048,128,8]{2,1,3,0:T(8,128)} %get-tuple-element.248, f32[2,8,128]{2,1,0:T(8,128)S(1)} %get-tuple-element.249, pred[128,2048]{0,1:T(8,128)(4,1)S(1)} %dynamic-slice_bitcast_fusion.2), kind=kLoop, calls=%fused_computation.6.clone.1 | loop fusion | flops 16775168 | bytes 17055744 | tf_op jit(solution)/shard_map/while/body/eval_jaxpr/reduce_sum | solution.py:48
  166.9 2.1 copy.174
  169.0 10.9 %multiply_reduce_fusion.2 = (f32[128,2,8]{0,2,1:T(8,128)S(1)}, bf16[2,128,8,128]{3,1,2,0:T(8,128)(2,1)}) fusion(bf16[1,128,2,8,128]{1,4,3,2,0:T(8,128)(2,1)S(1)} %copy.173, f32[2,2048,128,8]{2,1,3,0:T(8,128)} %get-tuple-element.248, f32[2,8,128]{2,1,0:T(8,128)S(1)} %log_add_fusion.2, pred[128,2048]{0,1:T(8,128)(4,1)S(1)} %dynamic-slice_bitcast_fusion.2, ...), kind=kOutput, calls=%fused_computation.20.clone.1 | convolution fusion | flops 1091827712 | bytes 19152896 | tf_op jit(solution)/shard_map/while/body/eval_jaxpr/hgqk,khd->qhgd/dot_general | solution.py:51
  179.9 8.7 %fusion.64 = bf16[2,8,128,2048]{2,3,1,0:T(8,128)(2,1)S(1)} fusion(f32[2,2048,128,8]{2,1,3,0:T(8,128)} %get-tuple-element.248, f32[2,8,128]{2,1,0:T(8,128)S(1)} %bitcast.218, f32[2,8,128]{2,1,0:T(8,128)S(1)} %log_add_fusion.2, pred[128,2048]{0,1:T(8,128)(4,1)S(1)} %dynamic-slice_bitcast_fusion.2, bf16[1,2048,2,128]{1,3,2,0:T(8,128)(2,1)S(1)} %copy-done.1, ...), kind=kOutput, calls=%fused_computation.3.clone.1 | convolution fusion | flops 1098907648 | bytes 27017216 | tf_op jit(solution)/shard_map/while/body/eval_jaxpr/qhgd,khd->hgqk/dot_general | solution.py:57
  188.6 3.2 copy-done
  195.2 9.3 %convolution_bitcast_fusion.3 = f32[1,2048,2,128]{1,3,2,0:T(8,128)} fusion(bf16[1,128,2,8,128]{1,4,3,2,0:T(8,128)(2,1)S(1)} %copy.173, f32[2,2048,128,8]{2,1,3,0:T(8,128)} %get-tuple-element.248, f32[2,8,128]{2,1,0:T(8,128)S(1)} %log_add_fusion.2, pred[128,2048]{0,1:T(8,128)(4,1)S(1)} %dynamic-slice_bitcast_fusion.2), kind=kOutput, calls=%fused_computation.9.clone.1 | convolution fusion | flops 1090519040 | bytes 19668992 | tf_op jit(solution)/shard_map/while/body/eval_jaxpr/hgqk,qhgd->khd/dot_general | solution.py:69
  204.5 2.8 copy.177
  207.4 7.5 %fusion.66 = f32[1,2048,2,128]{1,3,2,0:T(8,128)} fusion(bf16[2,8,128,2048]{2,3,1,0:T(8,128)(2,1)} %copy-done, bf16[1,128,2,8,128]{4,3,2,1,0:T(8,128)(2,1)S(1)} %constant_dynamic-slice_fusion.10), kind=kOutput, calls=%fused_computation.12.clone.1 | convolution fusion | flops 1074266112 | bytes 11010048 | tf_op jit(solution)/shard_map/while/body/eval_jaxpr/hgqk,qhgd->khd/dot_general | solution.py:66
  214.9 4.1 %copy.178 = f32[1,2048,2,128]{3,2,1,0:T(2,128)} copy(f32[1,2048,2,128]{1,3,2,0:T(8,128)} %fusion.66) | data formatting | bytes 4194304 | tf_op jit(solution)/shard_map/while/body/jit(dynamic_update_index_in_dim)/dynamic_update_slice | solution.py:117
  219.0 3.3 constant_dynamic-update-slice_fusion.7
  226.2 7.1 %fusion.63 = (f32[2,8,128]{2,1,0:T(8,128)S(1)}, f32[2,2048,128,8]{2,1,3,0:T(8,128)}) fusion(pred[128,2048]{0,1:T(8,128)(4,1)S(1)} %dynamic-slice_bitcast_fusion.2, bf16[1,128,2,8,128]{4,3,2,1,0:T(8,128)(2,1)S(1)} %constant_dynamic-slice_fusion.10, bf16[1,2048,2,128]{3,2,1,0:T(2,128)(2,1)S(1)} %constant_dynamic-slice_fusion.11), kind=kOutput, calls=%fused_computation.8.clone.1 | convolution fusion | flops 1086322688 | bytes 18620416 | tf_op jit(solution)/shard_map/while/body/eval_jaxpr/qhgd,khd->hgqk/dot_general | solution.py:43
  234.8 9.1 %exponential_reduce_fusion.2 = f32[2,8,128]{2,1,0:T(8,128)S(1)} fusion(f32[2,2048,128,8]{2,1,3,0:T(8,128)} %get-tuple-element.248, f32[2,8,128]{2,1,0:T(8,128)S(1)} %get-tuple-element.249, pred[128,2048]{0,1:T(8,128)(4,1)S(1)} %dynamic-slice_bitcast_fusion.2), kind=kLoop, calls=%fused_computation.6.clone.1 | loop fusion | flops 16775168 | bytes 17055744 | tf_op jit(solution)/shard_map/while/body/eval_jaxpr/reduce_sum | solution.py:48
  245.8 2.1 copy.174
  247.9 10.9 %multiply_reduce_fusion.2 = (f32[128,2,8]{0,2,1:T(8,128)S(1)}, bf16[2,128,8,128]{3,1,2,0:T(8,128)(2,1)}) fusion(bf16[1,128,2,8,128]{1,4,3,2,0:T(8,128)(2,1)S(1)} %copy.173, f32[2,2048,128,8]{2,1,3,0:T(8,128)} %get-tuple-element.248, f32[2,8,128]{2,1,0:T(8,128)S(1)} %log_add_fusion.2, pred[128,2048]{0,1:T(8,128)(4,1)S(1)} %dynamic-slice_bitcast_fusion.2, ...), kind=kOutput, calls=%fused_computation.20.clone.1 | convolution fusion | flops 1091827712 | bytes 19152896 | tf_op jit(solution)/shard_map/while/body/eval_jaxpr/hgqk,khd->qhgd/dot_general | solution.py:51
  258.8 8.7 %fusion.64 = bf16[2,8,128,2048]{2,3,1,0:T(8,128)(2,1)S(1)} fusion(f32[2,2048,128,8]{2,1,3,0:T(8,128)} %get-tuple-element.248, f32[2,8,128]{2,1,0:T(8,128)S(1)} %bitcast.218, f32[2,8,128]{2,1,0:T(8,128)S(1)} %log_add_fusion.2, pred[128,2048]{0,1:T(8,128)(4,1)S(1)} %dynamic-slice_bitcast_fusion.2, bf16[1,2048,2,128]{1,3,2,0:T(8,128)(2,1)S(1)} %copy-done.1, ...), kind=kOutput, calls=%fused_computation.3.clone.1 | convolution fusion | flops 1098907648 | bytes 27017216 | tf_op jit(solution)/shard_map/while/body/eval_jaxpr/qhgd,khd->hgqk/dot_general | solution.py:57
  267.5 3.2 copy-done
  274.1 9.3 %convolution_bitcast_fusion.3 = f32[1,2048,2,128]{1,3,2,0:T(8,128)} fusion(bf16[1,128,2,8,128]{1,4,3,2,0:T(8,128)(2,1)S(1)} %copy.173, f32[2,2048,128,8]{2,1,3,0:T(8,128)} %get-tuple-element.248, f32[2,8,128]{2,1,0:T(8,128)S(1)} %log_add_fusion.2, pred[128,2048]{0,1:T(8,128)(4,1)S(1)} %dynamic-slice_bitcast_fusion.2), kind=kOutput, calls=%fused_computation.9.clone.1 | convolution fusion | flops 1090519040 | bytes 19668992 | tf_op jit(solution)/shard_map/while/body/eval_jaxpr/hgqk,qhgd->khd/dot_general | solution.py:69
  283.4 2.8 copy.177
  286.3 7.5 %fusion.66 = f32[1,2048,2,128]{1,3,2,0:T(8,128)} fusion(bf16[2,8,128,2048]{2,3,1,0:T(8,128)(2,1)} %copy-done, bf16[1,128,2,8,128]{4,3,2,1,0:T(8,128)(2,1)S(1)} %constant_dynamic-slice_fusion.10), kind=kOutput, calls=%fused_computation.12.clone.1 | convolution fusion | flops 1074266112 | bytes 11010048 | tf_op jit(solution)/shard_map/while/body/eval_jaxpr/hgqk,qhgd->khd/dot_general | solution.py:66
  293.8 4.1 %copy.178 = f32[1,2048,2,128]{3,2,1,0:T(2,128)} copy(f32[1,2048,2,128]{1,3,2,0:T(8,128)} %fusion.66) | data formatting | bytes 4194304 | tf_op jit(solution)/shard_map/while/body/jit(dynamic_update_index_in_dim)/dynamic_update_slice | solution.py:117
  297.9 3.3 constant_dynamic-update-slice_fusion.7
  301.3 9.0 %reshape.1181 = f32[48,128,256]{2,1,0:T(8,128)} reshape(f32[3,2048,2,128]{3,2,1,0:T(2,128)} %get-tuple-element.62) | data formatting | bytes 12582912 | tf_op jit(solution)/shard_map/reshape | solution.py:123
  310.3 9.0 %reshape.1180 = f32[48,128,256]{2,1,0:T(8,128)} reshape(f32[3,2048,2,128]{3,2,1,0:T(2,128)} %get-tuple-element.61) | data formatting | bytes 12582912 | tf_op jit(solution)/shard_map/reshape | solution.py:122
  319.2 11.4 %pad_maximum_fusion = f32[48,128,512]{2,1,0:T(8,128)} fusion(f32[48,128,256]{2,1,0:T(8,128)} %reshape.1181, f32[48,128,256]{2,1,0:T(8,128)} %reshape.1180), kind=kLoop, calls=%fused_computation.39 | loop fusion | flops 3145728 | bytes 25165824 | tf_op jit(solution)/shard_map/concatenate | solution.py:120
  331.0 17.2 %scatter_fusion = f32[13,128,512]{2,1,0:T(8,128)S(1)} fusion(f32[13,128,512]{2,1,0:T(8,128)S(1)} %broadcast_in_dim.291, s32[48]{0:T(128)S(1)} %fusion.43, f32[48,128,512]{2,1,0:T(8,128)} %pad_maximum_fusion), kind=kCustom, calls=%fused_computation | custom fusion | flops 3145728 | bytes 37748928 | tf_op jit(solution)/shard_map/scatter-add | solution.py:130
  348.2 2.2 slice.14
  350.5 3.8 reshape.1177
  356.3 33.1 %reduce-scatter.2.cloned.1.call-done = f32[384,512]{1,0:T(8,128)} async-done(((f32[1536,512]{1,0:T(8,128)}), f32[384,512]{1,0:T(8,128)}) %reduce-scatter.2.cloned.1.call-update) | async-done | bytes 786448 | tf_op jit(solution)/shard_map/reduce_scatter | solution.py:133
  (140 shorter events, 58.7 us)
Async XLA Ops:
  7.2 382.3 %reduce-scatter.2.cloned.1.call-start = ((), (), s32[]{:S(2)}) async-start(), calls=%async_computation.1 | async-start | bytes 3932160 | tf_op jit(solution)/shard_map/reduce_scatter | solution.py:133
  64.3 237.0 %copy-start.4 = (s32[48,1]{0,1:T(1,128)S(1)}, s32[48,1]{0,1:T(1,128)}, u32[]{:S(2)}) copy-start(s32[48,1]{0,1:T(1,128)} %reshape.1179) | copy-start | bytes 580
  89.9 10.9 %copy-start.1 = (bf16[1,2048,2,128]{1,3,2,0:T(8,128)(2,1)S(1)}, bf16[1,2048,2,128]{1,3,2,0:T(8,128)(2,1)}, u32[]{:S(2)}) copy-start(bf16[1,2048,2,128]{1,3,2,0:T(8,128)(2,1)} %copy.174) | copy-start | bytes 3145732 | tf_op jit(solution)/shard_map/while
  109.5 3.2 copy-start
  112.7 1.9 copy-start.2
  169.0 10.9 %copy-start.1 = (bf16[1,2048,2,128]{1,3,2,0:T(8,128)(2,1)S(1)}, bf16[1,2048,2,128]{1,3,2,0:T(8,128)(2,1)}, u32[]{:S(2)}) copy-start(bf16[1,2048,2,128]{1,3,2,0:T(8,128)(2,1)} %copy.174) | copy-start | bytes 3145732 | tf_op jit(solution)/shard_map/while
  188.6 3.2 copy-start
  191.8 1.9 copy-start.2
  247.9 10.9 %copy-start.1 = (bf16[1,2048,2,128]{1,3,2,0:T(8,128)(2,1)S(1)}, bf16[1,2048,2,128]{1,3,2,0:T(8,128)(2,1)}, u32[]{:S(2)}) copy-start(bf16[1,2048,2,128]{1,3,2,0:T(8,128)(2,1)} %copy.174) | copy-start | bytes 3145732 | tf_op jit(solution)/shard_map/while
  267.5 3.2 copy-start
  270.7 1.9 copy-start.2
  350.5 3.8 copy-start.3
Sparse Core Ops, SparseCore 0:
  350.6 38.7 reduce-scatter.1
where the time goes:
time: 400 us; the launch traced here: 398 us
  matrix products  137 us (34%)
  local copies, waits for them, and re-layouts  119 us (30%)
  other arithmetic  75.5 us (19%)
  waiting for transfers between devices  33.1 us (8%)
  blocking collectives  19.2 us (5%)
  between operations  14.2 us (4%)
    dynamic_update_slice x18, local copies, waits for them, and re-layouts, body(): lax.map(one_block, (query_block_list, gradient_block_list, key_block_list...  37 us
    reduce_scatter x1, waiting for transfers between devices, body(): lax.psum_scatter(partial_sums.reshape(tok_dev * lax.axis_size('ctx'), 2 *...  33.1 us
    dot_general x3, matrix products, attend_block(): jnp.einsum('hgqk,khd->qhgd', weights, value_row_list, preferred_element_t...  32.8 us
    dot_general x3, matrix products, attend_block(): jnp.einsum('hgqk,qhgd->khd', weights, grad_block, preferred_element_type=...  27.8 us
    reduce_sum x3, other arithmetic, attend_block(): totals = jnp.sum(jnp.exp(scores - highest), axis=-1, keepdims=True)  27.3 us
    dot_general x3, matrix products, attend_block(): jnp.einsum('qhgd,khd->hgqk', grad_block, value_row_list, preferred_elemen...  26 us
    dynamic_slice x18, local copies, waits for them, and re-layouts, body(): lax.map(one_block, (query_block_list, gradient_block_list, key_block_list...  25 us
    dot_general x3, matrix products, attend_block(): jnp.einsum('hgqk,qhgd->khd', dscores, query_block, preferred_element_type...  22.6 us
  transfers between devices with their start and end apart: 1, of which 1 were waited for; matrix products, arithmetic and copies ran while one was open for 1% of the time, Pallas kernels for 0%

commit v1 on v0

v1 whole, which is shorter than its diff:
```python
import functools
import math

import jax
import jax.numpy as jnp
from jax import lax
import jax.experimental.pallas as pl
import jax.experimental.pallas.tpu as pltpu
from jax.sharding import PartitionSpec as P

HEAD_SIZE = 128
TREE_BLOCK_SIZE = 128
PATH_DEPTH_MAX = 16
QUERY_HEADS = 64
KEY_VALUE_HEADS = 8

D = HEAD_SIZE
T = TREE_BLOCK_SIZE
NT = (((1,), (1,)), ((), ()))
TN = (((0,), (0,)), ((), ()))
BF = jnp.bfloat16
F32 = jnp.float32
SCALE = 1.0 / math.sqrt(D)
LOG2E = math.log2(math.e)


def fill_table(info, table, me, blocks, group_blocks, depth, pairwise):
    for b in range(blocks):
        mine = me * blocks + b

        def find(t, found):
            return jnp.where(info[1 + group_blocks + t] == mine, t, found)

        current = lax.fori_loop(0, group_blocks, find, jnp.int32(0))
        for d in range(depth):
            if d:
                current = jnp.where(current >= 0, info[1 + jnp.maximum(current, 0)], -1)
            owner = info[1 + group_blocks + jnp.maximum(current, 0)]
            if pairwise:
                shard = lax.div(owner, jnp.int32(blocks))
                place = (shard ^ me) * blocks + owner - shard * blocks
            else:
                place = owner
            table[b * depth + d] = jnp.where(current >= 0, place, -1)


def attend_kernel(*refs, head, blocks, group_blocks, depth, groups, shards, pairwise, chained):
    source_count = shards if pairwise else 1
    info, q_ref, do_ref = refs[:3]
    sources = refs[3 : 3 + source_count]
    at = 3 + source_count + (2 if chained else 0)
    o_out, dq_out, sum_ref = refs[at : at + 3]
    at += 3
    if pairwise:
        core_ref, far_ref = refs[at : at + 2]
        at += 2
    kv, acc, kb, vb, pt, dst, o_buf, dq_buf, table, kv_sem, out_sem = refs[at:]
    rows_each = blocks * T
    part_rows = kv.shape[0] // source_count

    def source_copy(i):
        return pltpu.make_async_copy(sources[i], kv.at[pl.ds(i * part_rows, part_rows)], kv_sem.at[i])

    for i in range(source_count):
        source_copy(i).start()
    me = info[0]
    fill_table(info, table, me, blocks, group_blocks, depth, pairwise)
    acc[...] = jnp.zeros_like(acc)
    for i in range(source_count):
        source_copy(i).wait()

    tri = lax.broadcasted_iota(jnp.int32, (T, T), 0) <= lax.broadcasted_iota(jnp.int32, (T, T), 1)

    def place(b, d):
        return pl.ds(pl.multiple_of(jnp.maximum(table[b * depth + d], 0) * T, T), T)

    def out_copies(b):
        rows = pl.ds(pl.multiple_of(b * T, T), T)
        columns = pl.ds(head * groups * D, groups * D)
        return (
            pltpu.make_async_copy(o_buf.at[b], o_out.at[rows, columns], out_sem.at[0, b]),
            pltpu.make_async_copy(dq_buf.at[b], dq_out.at[rows, columns], out_sem.at[1, b]),
        )

    def block(b, carry):
        rows = pl.ds(pl.multiple_of(b * T, T), T)
        for d in range(depth):
            kb[pl.ds(d * T, T), :] = kv[place(b, d), :D]
            vb[pl.ds(d * T, T), :] = kv[place(b, d), D:]
        bias = [
            jnp.where(table[b * depth + d] >= 0, 0.0, -jnp.inf).astype(F32) for d in range(depth)
        ]
        for g in range(groups):
            col = pl.ds(g * T, T)
            head_col = pl.ds((head * groups + g) * D, D)
            scores = lax.dot_general(kb[...], q_ref[rows, head_col], NT, preferred_element_type=F32)
            dprobs = lax.dot_general(vb[...], do_ref[rows, head_col], NT, preferred_element_type=F32)
            parts = [scores[d * T : (d + 1) * T] * (SCALE * LOG2E) for d in range(depth)]
            parts[0] = jnp.where(tri, parts[0], -jnp.inf)
            highs = [jnp.max(x, axis=0, keepdims=True) + bias[d] for d, x in enumerate(parts)]
            high = functools.reduce(jnp.maximum, highs)
            exps = [jnp.exp2(x - (high - bias[d])) for d, x in enumerate(parts)]
            total = functools.reduce(
                jnp.add, [jnp.sum(x, axis=0, keepdims=True) for x in exps]
            )
            inverse = 1.0 / total
            dparts = [dprobs[d * T : (d + 1) * T] for d in range(depth)]
            inner = inverse * functools.reduce(
                jnp.add,
                [jnp.sum(x * y, axis=0, keepdims=True) for x, y in zip(exps, dparts)],
            )
            for d in range(depth):
                weights = exps[d] * inverse
                pt[pl.ds(d * T, T), col] = weights.astype(BF)
                dst[pl.ds(d * T, T), col] = (weights * (dparts[d] - inner)).astype(BF)
        q_rows = jnp.concatenate(
            [q_ref[rows, (head * groups + g) * D : (head * groups + g + 1) * D] for g in range(groups)], 0
        )
        do_rows = jnp.concatenate(
            [do_ref[rows, (head * groups + g) * D : (head * groups + g + 1) * D] for g in range(groups)], 0
        )
        dv = jnp.dot(pt[...], do_rows, preferred_element_type=F32)
        dk = jnp.dot(dst[...], q_rows, preferred_element_type=F32) * SCALE
        for d in range(depth):
            acc[place(b, d), :D] += dk[d * T : (d + 1) * T]
            acc[place(b, d), D:] += dv[d * T : (d + 1) * T]
        out_t = lax.dot_general(vb[...], pt[...], TN, preferred_element_type=F32)
        dq_t = lax.dot_general(kb[...], dst[...], TN, preferred_element_type=F32) * SCALE
        for g in range(groups):
            col = pl.ds(g * T, T)
            o_buf[b, :, col] = out_t[:, g * T : (g + 1) * T].T.astype(BF)
            dq_buf[b, :, col] = dq_t[:, g * T : (g + 1) * T].T.astype(BF)
        for copy in out_copies(b):
            copy.start()
        return carry

    lax.fori_loop(0, blocks, block, 0)
    if pairwise:
        sum_ref[...] = acc[:rows_each]
        core_ref[:rows_each] = acc[rows_each : 2 * rows_each].astype(BF)
        core_ref[rows_each:] = acc[3 * rows_each :].astype(BF)
        far_ref[...] = acc[2 * rows_each : 3 * rows_each].astype(BF)
    else:
        sum_ref[...] = acc[...]
    for b in range(blocks):
        for copy in out_copies(b):
            copy.wait()


def attend(info, queries, output_gradient, sources, outputs, head, shards, pairwise):
    tokens = queries.shape[0]
    blocks = tokens // T
    group_blocks = blocks * shards
    depth = min(PATH_DEPTH_MAX, shards)
    groups = QUERY_HEADS // KEY_VALUE_HEADS
    vmem = pl.BlockSpec(memory_space=pltpu.VMEM)
    hbm = pl.BlockSpec(memory_space=pl.ANY)
    chained = outputs is not None
    operands = [
        info,
        pltpu.with_memory_space_constraint(queries, pltpu.VMEM),
        pltpu.with_memory_space_constraint(output_gradient, pltpu.VMEM),
        *sources,
        *(outputs if chained else ()),
    ]
    in_specs = [pl.BlockSpec(memory_space=pltpu.SMEM), vmem, vmem]
    in_specs += [hbm] * (len(operands) - 3)
    full = jax.ShapeDtypeStruct(queries.shape, BF)
    total_rows = tokens * shards
    if pairwise:
        sums = [
            jax.ShapeDtypeStruct((tokens, 2 * D), F32),
            jax.ShapeDtypeStruct((2 * tokens, 2 * D), BF),
            jax.ShapeDtypeStruct((tokens, 2 * D), BF),
        ]
    else:
        sums = [jax.ShapeDtypeStruct((total_rows, 2 * D), F32)]
    first = 3 + len(sources)
    kernel = functools.partial(
        attend_kernel,
        head=head,
        blocks=blocks,
        group_blocks=group_blocks,
        depth=depth,
        groups=groups,
        shards=shards,
        pairwise=pairwise,
        chained=chained,
    )
    flops = 12 * blocks * groups * depth * T * T * D
    return pl.pallas_call(
        kernel,
        in_specs=in_specs,
        out_specs=[hbm, hbm] + [vmem] * len(sums),
        out_shape=[full, full] + sums,
        input_output_aliases={first: 0, first + 1: 1} if chained else {},
        scratch_shapes=[
            pltpu.VMEM((total_rows, 2 * D), BF),
            pltpu.VMEM((total_rows, 2 * D), F32),
            pltpu.VMEM((depth * T, D), BF),
            pltpu.VMEM((depth * T, D), BF),
            pltpu.VMEM((depth * T, groups * T), BF),
            pltpu.VMEM((depth * T, groups * T), BF),
            pltpu.VMEM((blocks, T, groups * D), BF),
            pltpu.VMEM((blocks, T, groups * D), BF),
            pltpu.SMEM((blocks * depth,), jnp.int32),
            pltpu.SemaphoreType.DMA((len(sources),)),
            pltpu.SemaphoreType.DMA((2, blocks)),
        ],
        compiler_params=pltpu.CompilerParams(vmem_limit_bytes=40 * 2**20),
        cost_estimate=pl.CostEstimate(
            flops=2 * flops, bytes_accessed=8 * tokens * groups * D, transcendentals=0
        ),
        name="attend",
    )(*operands)


def body(queries, key_states, value_tensor, output_gradient, parent, block_owner, shards):
    tokens = queries.shape[0]
    kv_heads = key_states.shape[1] // D
    pairwise = shards == 4
    me = lax.axis_index("ctx").astype(jnp.int32)
    info = jnp.concatenate([me[None], parent, block_owner])
    core = [(i, i ^ 1) for i in range(shards)]
    across = [(i, i ^ 2) for i in range(shards)]
    packed = [
        jnp.concatenate([key_states[:, h * D : (h + 1) * D], value_tensor[:, h * D : (h + 1) * D]], 1)
        for h in range(kv_heads)
    ]
    gathered = []
    for own in packed:
        if pairwise:
            far = lax.ppermute(own, "ctx", across)
            near = lax.ppermute(own, "ctx", core)
            gathered.append([own, near, far, lax.ppermute(far, "ctx", core)])
        else:
            gathered.append([lax.all_gather(own, "ctx", axis=0, tiled=True)])
    outputs = None
    summed = []
    for h in range(kv_heads):
        done = attend(info, queries, output_gradient, gathered[h], outputs, h, shards, pairwise)
        outputs = done[:2]
        if pairwise:
            sums, to_core, to_far = done[2:]
            from_core = lax.ppermute(to_core, "ctx", core)
            onward = (to_far.astype(F32) + from_core[tokens:].astype(F32)).astype(BF)
            from_far = lax.ppermute(onward, "ctx", across)
            summed.append(sums + from_core[:tokens].astype(F32) + from_far.astype(F32))
        else:
            summed.append(lax.psum_scatter(done[2], "ctx", scatter_dimension=0, tiled=True))
    d_keys = jnp.concatenate([s[:, :D] for s in summed], 1).astype(BF)
    d_values = jnp.concatenate([s[:, D:] for s in summed], 1).astype(BF)
    return (outputs[0], outputs[1], d_keys, d_values)


def solution(mesh):
    tokens_split = P(("groups", "ctx"), "tp")
    return jax.shard_map(
        functools.partial(body, shards=mesh.shape["ctx"]),
        mesh=mesh,
        in_specs=(tokens_split,) * 4 + (P("groups"),) * 2,
        out_specs=(tokens_split,) * 4,
        check_vma=False,
    )
```

time: 400 us -> 50.2 us (0.13)
  matrix products: 137 us -> 0 us
  local copies, waits for them, and re-layouts: 119 us -> 2.63 us
  other arithmetic: 75.5 us -> 1.77 us
  Pallas kernels: 0 us -> 20.8 us
  blocking collectives: 19.2 us -> 0 us
  waiting for transfers between devices: 33.1 us -> 16.3 us
  between operations: 14.2 us -> 0.76 us
  starting transfers between devices: 0.04 us -> 7.79 us
    dot_general x20 -> x0, matrix products: 137 us -> none  [the longest x3 32.8 us: attend_block(): jnp.einsum('hgqk,khd->qhgd', weights, value_row_list, preferred_element_t...]
    reduce_sum x20 -> x0, other arithmetic: 41.8 us -> none  [the longest x3 27.3 us: attend_block(): totals = jnp.sum(jnp.exp(scores - highest), axis=-1, keepdims=True)]
    dynamic_update_slice x18 -> x0, local copies, waits for them, and re-layouts: 37 us -> none  [body(): lax.map(one_block, (query_block_list, gradient_block_list, key_block_list...]
    reduce_scatter x1 -> x0, waiting for transfers between devices: 33.1 us -> none  [body(): lax.psum_scatter(partial_sums.reshape(tok_dev * lax.axis_size('ctx'), 2 *...]
    reshape x7 -> x0, local copies, waits for them, and re-layouts: 30.4 us -> none  [the longest x1 9.01 us: body(): dvalues.reshape(slot_count, block_len, row_span_width)]
    dynamic_slice x18 -> x0, local copies, waits for them, and re-layouts: 25 us -> none  [body(): lax.map(one_block, (query_block_list, gradient_block_list, key_block_list...]
    pallas_call x0 -> x2, Pallas kernels: none -> 20.8 us  [attend(): pl.pallas_call(kernel, in_specs=in_specs, out_specs=[hbm, hbm] + [vmem] *...]
    all_gather x2 -> x0, blocking collectives: 19.2 us -> none  [the longest x1 10.3 us: body(): piece_values = lax.all_gather(value_tensor, 'ctx', axis=0, tiled=True)]
  transfers between devices with their start and end apart: 1 -> 10, of which waited for: 1 -> 4; matrix products, arithmetic and copies ran while one was open for 1% -> 1% of each run, Pallas kernels for 0% -> 42%
where the time goes in v1:
time: 50.2 us; the launch traced here: 50.1 us
  Pallas kernels  20.8 us (41%)
  waiting for transfers between devices  16.3 us (32%)
  starting transfers between devices  7.79 us (16%)
  local copies, waits for them, and re-layouts  2.63 us (5%)
  other arithmetic  1.77 us (4%)
  between operations  0.76 us (2%)
    pallas_call x2, Pallas kernels, attend(): pl.pallas_call(kernel, in_specs=in_specs, out_specs=[hbm, hbm] + [vmem] *...  20.8 us
    ppermute x2, waiting for transfers between devices, body(): far = lax.ppermute(own, 'ctx', across)  8.34 us
    ppermute x2, waiting for transfers between devices, body(): from_far = lax.ppermute(onward, 'ctx', across)  7.98 us
    ppermute x2, starting transfers between devices, body(): from_far = lax.ppermute(onward, 'ctx', across)  3.43 us
    ppermute x2, starting transfers between devices, body(): far = lax.ppermute(own, 'ctx', across)  3.12 us
    unnamed x8, local copies, waits for them, and re-layouts  1.42 us
    slice x1, local copies, waits for them, and re-layouts, body(): key_states[:, h * D:(h + 1) * D]  1.18 us
  transfers between devices with their start and end apart: 10, of which 4 were waited for; matrix products, arithmetic and copies ran while one was open for 1% of the time, Pallas kernels for 42%

profile of v1, /device:TPU:0, one launch (start us, length us, event | category | flops | bytes accessed | tf_op | source)
XLA Modules:
  0.0 50.1 jit_solution(12646784282614164053)
XLA Ops:
  0.6 0.0 copy-start.3
  0.6 0.0 copy-start.2
  0.7 0.0 copy-start
  0.7 1.2 %fusion.2 = (bf16[384,128]{1,0:T(8,128)(2,1)S(1)}, bf16[384,128]{1,0:T(8,128)(2,1)S(1)}, bf16[384,128]{1,0:T(8,128)(2,1)S(1)}, bf16[384,128]{1,0:T(8,128)(2,1)S(1)}) fusion(bf16[384,256]{1,0:T(8,128)(2,1)} %param.7, bf16[384,256]{1,0:T(8,128)(2,1)} %param.8), kind=kLoop, calls=%fused_computation.11 | loop fusion | bytes 786432 | tf_op jit(solution)/shard_map/slice | solution.py:227
  1.9 3.0 %collective-permute-start.4 = (bf16[384,256]{1,0:T(8,128)(2,1)S(1)}, bf16[384,256]{1,0:T(8,128)(2,1)S(1)}, u32[]{:S(2)}, u32[]{:S(2)}) collective-permute-start(bf16[384,256]{1,0:T(8,128)(2,1)S(1)} %pad_maximum_fusion.1.refs_3_), channel_id=1, source_target_pairs={{0,8},{4,12},{8,0},{12,4},{1,9},{5,13},{9,1},{13,5},{2,10},{6,14},... | collective-permute-start | bytes 589832 | tf_op jit(solution)/shard_map/ppermute | solution.py:233
  4.9 0.1 collective-permute-start.1
  5.0 0.1 collective-permute-start.3
  5.1 5.5 %collective-permute-done.4.refs_5_ = bf16[384,256]{1,0:T(8,128)(2,1)S(1)} collective-permute-done((bf16[384,256]{1,0:T(8,128)(2,1)S(1)}, bf16[384,256]{1,0:T(8,128)(2,1)S(1)}, u32[]{:S(2)}, u32[]{:S(2)}) %collective-permute-start.4) | collective-permute-done | bytes 196640 | tf_op jit(solution)/shard_map/ppermute | solution.py:233
  10.6 0.0 collective-permute-start.5
  10.6 0.5 %collective-permute-start = (bf16[384,256]{1,0:T(8,128)(2,1)S(1)}, bf16[384,256]{1,0:T(8,128)(2,1)S(1)}, u32[]{:S(2)}, u32[]{:S(2)}) collective-permute-start(bf16[384,256]{1,0:T(8,128)(2,1)S(1)} %pad_maximum_fusion.refs_3_), channel_id=1, source_target_pairs={{0,4},{4,0},{8,12},{12,8},{1,5},{5,1},{9,13},{13,9},{2,6},{6,2},{1... | collective-permute-start | bytes 589832 | tf_op jit(solution)/shard_map/ppermute | solution.py:234
  11.2 0.0 copy-done.3
  11.2 0.0 copy-done.2
  11.2 0.1 pad_add_fusion.refs_0_
  11.2 2.8 %collective-permute-done.1.refs_5_ = bf16[384,256]{1,0:T(8,128)(2,1)S(1)} collective-permute-done((bf16[384,256]{1,0:T(8,128)(2,1)S(1)}, bf16[384,256]{1,0:T(8,128)(2,1)S(1)}, u32[]{:S(2)}, u32[]{:S(2)}) %collective-permute-start.1) | collective-permute-done | bytes 196640 | tf_op jit(solution)/shard_map/ppermute | solution.py:233
  14.0 0.0 collective-permute-start.2
  14.0 0.0 collective-permute-done.3.refs_4_
  14.0 0.0 collective-permute-done.5.refs_6_
  14.0 0.0 copy-done
  14.1 0.0 copy-start.1
  14.1 1.4 %copy-done.1 = bf16[384,2048]{1,0:T(8,128)(2,1)S(1)} copy-done((bf16[384,2048]{1,0:T(8,128)(2,1)S(1)}, bf16[384,2048]{1,0:T(8,128)(2,1)}, u32[]{:S(2)}) %copy-start.1) | copy-done | bytes 1572888
  15.5 10.4 %attend.2 = (bf16[384,2048]{1,0:T(8,128)(2,1)}, bf16[384,2048]{1,0:T(8,128)(2,1)}, f32[384,256]{1,0:T(8,128)S(1)}, bf16[768,256]{1,0:T(8,128)(2,1)S(1)}, bf16[384,256]{1,0:T(8,128)(2,1)S(1)}) custom-call(s32[25]{0:T(128)S(1)} %pad_add_fusion.refs_0_, bf16[384,2048]{1,0:T(8,128)(2,1)S(1)} %copy-done, bf16[384,2048]{1,0:T(8,128)(2,1)S(1)} %copy-done.1, ...), custom_call_target="tpu_custom_call" | custom-call | flops 4831838208 | bytes 3145728 | tf_op jit(solution)/shard_map/attend/pallas_call | solution.py:191
  25.9 0.6 %collective-permute-start.6 = (bf16[768,256]{1,0:T(8,128)(2,1)S(1)}, bf16[768,256]{1,0:T(8,128)(2,1)S(1)}, u32[]{:S(2)}, u32[]{:S(2)}) collective-permute-start(bf16[768,256]{1,0:T(8,128)(2,1)S(1)} %get-tuple-element.19), channel_id=1, source_target_pairs={{0,4},{4,0},{8,12},{12,8},{1,5},{5,1},{9,13},{13,9},{2,6},{6,2},{1... | collective-permute-start | bytes 1179656 | tf_op jit(solution)/shard_map/ppermute | solution.py:245
  26.4 0.0 collective-permute-done.refs_4_
  26.4 0.0 collective-permute-done.2.refs_6_
  26.4 10.4 %attend.3 = (bf16[384,2048]{1,0:T(8,128)(2,1)}, bf16[384,2048]{1,0:T(8,128)(2,1)}, f32[384,256]{1,0:T(8,128)S(1)}, bf16[768,256]{1,0:T(8,128)(2,1)S(1)}, bf16[384,256]{1,0:T(8,128)(2,1)S(1)}) custom-call(s32[25]{0:T(128)S(1)} %pad_add_fusion.refs_0_, bf16[384,2048]{1,0:T(8,128)(2,1)S(1)} %copy-done, ...), custom_call_target="tpu_custom_call", output_to_operand_aliasing={{0}: (7, {}), {1}: (8, {})} | custom-call | flops 4831838208 | bytes 3145728 | tf_op jit(solution)/shard_map/attend/pallas_call | solution.py:191
  36.9 0.1 collective-permute-start.8
  37.0 0.0 collective-permute-done.6
  37.0 1.8 %collective-permute-start.7 = (bf16[384,256]{1,0:T(8,128)(2,1)S(1)}, bf16[384,256]{1,0:T(8,128)(2,1)S(1)}, u32[]{:S(2)}, u32[]{:S(2)}) collective-permute-start(bf16[384,256]{1,0:T(8,128)(2,1)S(1)} %add_convert_fusion.3), channel_id=1, source_target_pairs={{0,8},{4,12},{8,0},{12,4},{1,9},{5,13},{9,1},{13,5},{2,10},{6,14},... | collective-permute-start | bytes 589832 | tf_op jit(solution)/shard_map/ppermute | solution.py:247
  38.8 0.0 collective-permute-done.8
  38.8 0.1 add_convert_fusion.1
  38.9 1.6 %collective-permute-start.9 = (bf16[384,256]{1,0:T(8,128)(2,1)S(1)}, bf16[384,256]{1,0:T(8,128)(2,1)S(1)}, u32[]{:S(2)}, u32[]{:S(2)}) collective-permute-start(bf16[384,256]{1,0:T(8,128)(2,1)S(1)} %add_convert_fusion.1), channel_id=1, source_target_pairs={{0,8},{4,12},{8,0},{12,4},{1,9},{5,13},{9,1},{13,5},{2,10},{6,14},... | collective-permute-start | bytes 589832 | tf_op jit(solution)/shard_map/ppermute | solution.py:247
  40.5 4.3 %collective-permute-done.7 = bf16[384,256]{1,0:T(8,128)(2,1)S(1)} collective-permute-done((bf16[384,256]{1,0:T(8,128)(2,1)S(1)}, bf16[384,256]{1,0:T(8,128)(2,1)S(1)}, u32[]{:S(2)}, u32[]{:S(2)}) %collective-permute-start.7) | collective-permute-done | bytes 196640 | tf_op jit(solution)/shard_map/ppermute | solution.py:247
  44.8 0.1 add_convert_fusion.2
  44.9 3.7 %collective-permute-done.9 = bf16[384,256]{1,0:T(8,128)(2,1)S(1)} collective-permute-done((bf16[384,256]{1,0:T(8,128)(2,1)S(1)}, bf16[384,256]{1,0:T(8,128)(2,1)S(1)}, u32[]{:S(2)}, u32[]{:S(2)}) %collective-permute-start.9) | collective-permute-done | bytes 196640 | tf_op jit(solution)/shard_map/ppermute | solution.py:247
  48.6 0.1 add_convert_fusion
  48.7 0.7 %pad_maximum_fusion.3 = bf16[384,256]{1,0:T(8,128)(2,1)} fusion(bf16[384,128]{1,0:T(8,128)(2,1)S(1)} %get-tuple-element.26, bf16[384,128]{1,0:T(8,128)(2,1)S(1)} %get-tuple-element.24), kind=kLoop, calls=%fused_computation.7 | loop fusion | flops 393216 | bytes 393216 | tf_op jit(solution)/shard_map/concatenate | solution.py:252
  49.4 0.7 %pad_maximum_fusion.2 = bf16[384,256]{1,0:T(8,128)(2,1)} fusion(bf16[384,128]{1,0:T(8,128)(2,1)S(1)} %get-tuple-element.27, bf16[384,128]{1,0:T(8,128)(2,1)S(1)} %get-tuple-element.25), kind=kLoop, calls=%fused_computation.6 | loop fusion | flops 393216 | bytes 393216 | tf_op jit(solution)/shard_map/concatenate | solution.py:251
  (5 shorter events, 0.1 us)
Async XLA Ops:
  0.6 10.5 %copy-start.3 = (s32[12]{0:T(128)S(1)}, s32[12]{0:T(128)}, u32[]{:S(2)}) copy-start(s32[12]{0:T(128)} %param.10) | copy-start | bytes 148
  0.6 10.5 %copy-start.2 = (s32[12]{0:T(128)S(1)}, s32[12]{0:T(128)}, u32[]{:S(2)}) copy-start(s32[12]{0:T(128)} %param.11) | copy-start | bytes 148
  0.7 13.4 %copy-start = (bf16[384,2048]{1,0:T(8,128)(2,1)S(1)}, bf16[384,2048]{1,0:T(8,128)(2,1)}, u32[]{:S(2)}) copy-start(bf16[384,2048]{1,0:T(8,128)(2,1)} %refs_1_.3) | copy-start | bytes 4718596
  1.9 8.8 %collective-permute-start.4 = (bf16[384,256]{1,0:T(8,128)(2,1)S(1)}, bf16[384,256]{1,0:T(8,128)(2,1)S(1)}, u32[]{:S(2)}, u32[]{:S(2)}) collective-permute-start(bf16[384,256]{1,0:T(8,128)(2,1)S(1)} %pad_maximum_fusion.1.refs_3_), channel_id=1, source_target_pairs={{0,8},{4,12},{8,0},{12,4},{1,9},{5,13},{9,1},{13,5},{2,10},{6,14},... | collective-permute-start | bytes 589832 | tf_op jit(solution)/shard_map/ppermute | solution.py:233
  4.9 9.1 %collective-permute-start.1 = (bf16[384,256]{1,0:T(8,128)(2,1)S(1)}, bf16[384,256]{1,0:T(8,128)(2,1)S(1)}, u32[]{:S(2)}, u32[]{:S(2)}) collective-permute-start(bf16[384,256]{1,0:T(8,128)(2,1)S(1)} %pad_maximum_fusion.refs_3_), channel_id=1, source_target_pairs={{0,8},{4,12},{8,0},{12,4},{1,9},{5,13},{9,1},{13,5},{2,10},{6,14},... | collective-permute-start | bytes 589832 | tf_op jit(solution)/shard_map/ppermute | solution.py:233
  5.0 9.0 %collective-permute-start.3 = (bf16[384,256]{1,0:T(8,128)(2,1)S(1)}, bf16[384,256]{1,0:T(8,128)(2,1)S(1)}, u32[]{:S(2)}, u32[]{:S(2)}) collective-permute-start(bf16[384,256]{1,0:T(8,128)(2,1)S(1)} %pad_maximum_fusion.1.refs_3_), channel_id=1, source_target_pairs={{0,4},{4,0},{8,12},{12,8},{1,5},{5,1},{9,13},{13,9},{2,6},{6,2},{1... | collective-permute-start | bytes 589832 | tf_op jit(solution)/shard_map/ppermute | solution.py:234
  10.6 3.4 %collective-permute-start.5 = (bf16[384,256]{1,0:T(8,128)(2,1)S(1)}, bf16[384,256]{1,0:T(8,128)(2,1)S(1)}, u32[]{:S(2)}, u32[]{:S(2)}) collective-permute-start(bf16[384,256]{1,0:T(8,128)(2,1)S(1)} %collective-permute-done.4.refs_5_), channel_id=1, source_target_pairs={{0,4},{4,0},{8,12},{12,8},{1,5},{5,1},{9,13},{13,9},{2,6},{6,2},{1... | collective-permute-start | bytes 589832 | tf_op jit(solution)/shard_map/ppermute | solution.py:235
  10.6 15.8 %collective-permute-start = (bf16[384,256]{1,0:T(8,128)(2,1)S(1)}, bf16[384,256]{1,0:T(8,128)(2,1)S(1)}, u32[]{:S(2)}, u32[]{:S(2)}) collective-permute-start(bf16[384,256]{1,0:T(8,128)(2,1)S(1)} %pad_maximum_fusion.refs_3_), channel_id=1, source_target_pairs={{0,4},{4,0},{8,12},{12,8},{1,5},{5,1},{9,13},{13,9},{2,6},{6,2},{1... | collective-permute-start | bytes 589832 | tf_op jit(solution)/shard_map/ppermute | solution.py:234
  14.0 12.4 %collective-permute-start.2 = (bf16[384,256]{1,0:T(8,128)(2,1)S(1)}, bf16[384,256]{1,0:T(8,128)(2,1)S(1)}, u32[]{:S(2)}, u32[]{:S(2)}) collective-permute-start(bf16[384,256]{1,0:T(8,128)(2,1)S(1)} %collective-permute-done.1.refs_5_), channel_id=1, source_target_pairs={{0,4},{4,0},{8,12},{12,8},{1,5},{5,1},{9,13},{13,9},{2,6},{6,2},{1... | collective-permute-start | bytes 589832 | tf_op jit(solution)/shard_map/ppermute | solution.py:235
  14.1 1.4 %copy-start.1 = (bf16[384,2048]{1,0:T(8,128)(2,1)S(1)}, bf16[384,2048]{1,0:T(8,128)(2,1)}, u32[]{:S(2)}) copy-start(bf16[384,2048]{1,0:T(8,128)(2,1)} %refs_2_.3) | copy-start | bytes 4718596
  25.9 11.1 %collective-permute-start.6 = (bf16[768,256]{1,0:T(8,128)(2,1)S(1)}, bf16[768,256]{1,0:T(8,128)(2,1)S(1)}, u32[]{:S(2)}, u32[]{:S(2)}) collective-permute-start(bf16[768,256]{1,0:T(8,128)(2,1)S(1)} %get-tuple-element.19), channel_id=1, source_target_pairs={{0,4},{4,0},{8,12},{12,8},{1,5},{5,1},{9,13},{13,9},{2,6},{6,2},{1... | collective-permute-start | bytes 1179656 | tf_op jit(solution)/shard_map/ppermute | solution.py:245
  36.9 2.0 %collective-permute-start.8 = (bf16[768,256]{1,0:T(8,128)(2,1)S(1)}, bf16[768,256]{1,0:T(8,128)(2,1)S(1)}, u32[]{:S(2)}, u32[]{:S(2)}) collective-permute-start(bf16[768,256]{1,0:T(8,128)(2,1)S(1)} %get-tuple-element.22), channel_id=1, source_target_pairs={{0,4},{4,0},{8,12},{12,8},{1,5},{5,1},{9,13},{13,9},{2,6},{6,2},{1... | collective-permute-start | bytes 1179656 | tf_op jit(solution)/shard_map/ppermute | solution.py:245
  37.0 7.8 %collective-permute-start.7 = (bf16[384,256]{1,0:T(8,128)(2,1)S(1)}, bf16[384,256]{1,0:T(8,128)(2,1)S(1)}, u32[]{:S(2)}, u32[]{:S(2)}) collective-permute-start(bf16[384,256]{1,0:T(8,128)(2,1)S(1)} %add_convert_fusion.3), channel_id=1, source_target_pairs={{0,8},{4,12},{8,0},{12,4},{1,9},{5,13},{9,1},{13,5},{2,10},{6,14},... | collective-permute-start | bytes 589832 | tf_op jit(solution)/shard_map/ppermute | solution.py:247
  38.9 9.7 %collective-permute-start.9 = (bf16[384,256]{1,0:T(8,128)(2,1)S(1)}, bf16[384,256]{1,0:T(8,128)(2,1)S(1)}, u32[]{:S(2)}, u32[]{:S(2)}) collective-permute-start(bf16[384,256]{1,0:T(8,128)(2,1)S(1)} %add_convert_fusion.1), channel_id=1, source_target_pairs={{0,8},{4,12},{8,0},{12,4},{1,9},{5,13},{9,1},{13,5},{2,10},{6,14},... | collective-permute-start | bytes 589832 | tf_op jit(solution)/shard_map/ppermute | solution.py:247

commit v2 on v1

--- a/solution.py
+++ b/solution.py
@@ -22,9 +22,13 @@
 F32 = jnp.float32
 SCALE = 1.0 / math.sqrt(D)
 LOG2E = math.log2(math.e)
-
-
-def fill_table(info, table, me, blocks, group_blocks, depth, pairwise):
+LINKED = 4
+WIDE = 2
+ONES = 16
+SAFE_EXPONENT = 96.0
+
+
+def fill_table(info, table, me, blocks, group_blocks, depth):
     for b in range(blocks):
         mine = me * blocks + b
 
@@ -36,38 +40,19 @@
             if d:
                 current = jnp.where(current >= 0, info[1 + jnp.maximum(current, 0)], -1)
             owner = info[1 + group_blocks + jnp.maximum(current, 0)]
-            if pairwise:
-                shard = lax.div(owner, jnp.int32(blocks))
-                place = (shard ^ me) * blocks + owner - shard * blocks
-            else:
-                place = owner
-            table[b * depth + d] = jnp.where(current >= 0, place, -1)
-
-
-def attend_kernel(*refs, head, blocks, group_blocks, depth, groups, shards, pairwise, chained):
-    source_count = shards if pairwise else 1
-    info, q_ref, do_ref = refs[:3]
-    sources = refs[3 : 3 + source_count]
-    at = 3 + source_count + (2 if chained else 0)
+            table[b * depth + d] = jnp.where(current >= 0, owner, -1)
+
+
+def attend_kernel(*refs, head, blocks, group_blocks, depth, groups, chained):
+    info, q_ref, do_ref, gathered = refs[:4]
+    at = 6 if chained else 4
     o_out, dq_out, sum_ref = refs[at : at + 3]
-    at += 3
-    if pairwise:
-        core_ref, far_ref = refs[at : at + 2]
-        at += 2
-    kv, acc, kb, vb, pt, dst, o_buf, dq_buf, table, kv_sem, out_sem = refs[at:]
-    rows_each = blocks * T
-    part_rows = kv.shape[0] // source_count
-
-    def source_copy(i):
-        return pltpu.make_async_copy(sources[i], kv.at[pl.ds(i * part_rows, part_rows)], kv_sem.at[i])
-
-    for i in range(source_count):
-        source_copy(i).start()
-    me = info[0]
-    fill_table(info, table, me, blocks, group_blocks, depth, pairwise)
+    kv, acc, kb, vb, pt, dst, o_buf, dq_buf, table, kv_sem, out_sem = refs[at + 3 :]
+    source_copy = pltpu.make_async_copy(gathered, kv, kv_sem)
+    source_copy.start()
+    fill_table(info, table, info[0], blocks, group_blocks, depth)
     acc[...] = jnp.zeros_like(acc)
-    for i in range(source_count):
-        source_copy(i).wait()
+    source_copy.wait()
 
     tri = lax.broadcasted_iota(jnp.int32, (T, T), 0) <= lax.broadcasted_iota(jnp.int32, (T, T), 1)
 
@@ -135,19 +120,13 @@
         return carry
 
     lax.fori_loop(0, blocks, block, 0)
-    if pairwise:
-        sum_ref[...] = acc[:rows_each]
-        core_ref[:rows_each] = acc[rows_each : 2 * rows_each].astype(BF)
-        core_ref[rows_each:] = acc[3 * rows_each :].astype(BF)
-        far_ref[...] = acc[2 * rows_each : 3 * rows_each].astype(BF)
-    else:
-        sum_ref[...] = acc[...]
+    sum_ref[...] = acc[...]
     for b in range(blocks):
         for copy in out_copies(b):
             copy.wait()
 
 
-def attend(info, queries, output_gradient, sources, outputs, head, shards, pairwise):
+def attend(info, queries, output_gradient, gathered, outputs, head, shards):
     tokens = queries.shape[0]
     blocks = tokens // T
     group_blocks = blocks * shards
@@ -160,22 +139,14 @@
         info,
         pltpu.with_memory_space_constraint(queries, pltpu.VMEM),
         pltpu.with_memory_space_constraint(output_gradient, pltpu.VMEM),
-        *sources,
+        gathered,
         *(outputs if chained else ()),
     ]
     in_specs = [pl.BlockSpec(memory_space=pltpu.SMEM), vmem, vmem]
     in_specs += [hbm] * (len(operands) - 3)
     full = jax.ShapeDtypeStruct(queries.shape, BF)
     total_rows = tokens * shards
-    if pairwise:
-        sums = [
-            jax.ShapeDtypeStruct((tokens, 2 * D), F32),
-            jax.ShapeDtypeStruct((2 * tokens, 2 * D), BF),
-            jax.ShapeDtypeStruct((tokens, 2 * D), BF),
-        ]
-    else:
-        sums = [jax.ShapeDtypeStruct((total_rows, 2 * D), F32)]
-    first = 3 + len(sources)
+    sums = [jax.ShapeDtypeStruct((total_rows, 2 * D), F32)]
     kernel = functools.partial(
         attend_kernel,
         head=head,
@@ -183,8 +154,6 @@
         group_blocks=group_blocks,
         depth=depth,
         groups=groups,
-        shards=shards,
-        pairwise=pairwise,
         chained=chained,
     )
     flops = 12 * blocks * groups * depth * T * T * D
@@ -193,7 +162,7 @@
         in_specs=in_specs,
         out_specs=[hbm, hbm] + [vmem] * len(sums),
         out_shape=[full, full] + sums,
-        input_output_aliases={first: 0, first + 1: 1} if chained else {},
+        input_output_aliases={4: 0, 5: 1} if chained else {},
         scratch_shapes=[
             pltpu.VMEM((total_rows, 2 * D), BF),
             pltpu.VMEM((total_rows, 2 * D), F32),
@@ -204,7 +173,7 @@
             pltpu.VMEM((blocks, T, groups * D), BF),
             pltpu.VMEM((blocks, T, groups * D), BF),
             pltpu.SMEM((blocks * depth,), jnp.int32),
-            pltpu.SemaphoreType.DMA((len(sources),)),
+            pltpu.SemaphoreType.DMA,
             pltpu.SemaphoreType.DMA((2, blocks)),
         ],
         compiler_params=pltpu.CompilerParams(vmem_limit_bytes=40 * 2**20),
@@ -215,39 +184,413 @@
     )(*operands)
 
 
+def relation_table(info, table, blocks, depth):
+    me = info[0]
+    group_blocks = blocks * LINKED
+    for b in range(blocks):
+        for r in range(LINKED):
+            table[b * LINKED + r] = -1
+        current = jnp.int32(0)
+        for t in range(group_blocks):
+            current = jnp.where(info[1 + group_blocks + t] == me * blocks + b, t, current)
+        for d in range(depth):
+            if d:
+                current = jnp.where(current >= 0, info[1 + jnp.maximum(current, 0)], -1)
+            owner = info[1 + group_blocks + jnp.maximum(current, 0)]
+            shard = lax.div(owner, jnp.int32(blocks))
+            slot = b * LINKED + (shard ^ me)
+            table[slot] = jnp.where(current >= 0, owner - shard * blocks, table[slot])
+
+
+def row_span(index):
+    return pl.ds(pl.multiple_of(jnp.maximum(index, 0) * T, T), T)
+
+
+def live_factor(index):
+    return jnp.where(index >= 0, 1.0, 0.0).astype(BF)
+
+
+def norm_top(rows):
+    wide = rows.astype(F32)
+    return jnp.max(jnp.sum(wide * wide, axis=1, keepdims=True))
+
+
+def causal(width):
+    keys = lax.broadcasted_iota(jnp.int32, (T, T), 0)
+    queries = lax.broadcasted_iota(jnp.int32, (T, T), 1)
+    return jnp.concatenate([keys <= queries] * width, 1)
+
+
+def near_kernel(*refs, blocks, heads, groups, depth):
+    info, q_in, do_in = refs[:3]
+    own = refs[3 : 3 + heads]
+    near = refs[3 + heads : 3 + 2 * heads]
+    table, top, q_v, do_v, qt, dt, kbn, vtn, pn, dpn, on = refs[3 + 2 * heads : 14 + 2 * heads]
+    kv, vb, row_sem, kv_sem = refs[14 + 2 * heads :]
+
+    def row_copies(b):
+        rows = pl.ds(b * T, T)
+        return (
+            pltpu.make_async_copy(q_in.at[rows], q_v.at[rows], row_sem.at[0, b]),
+            pltpu.make_async_copy(do_in.at[rows], do_v.at[rows], row_sem.at[1, b]),
+        )
+
+    kv_copies = [
+        pltpu.make_async_copy(source, kv.at[i], kv_sem.at[i]) for i, source in enumerate(own + near)
+    ]
+    for copy in kv_copies:
+        copy.start()
+    for b in range(blocks):
+        for copy in row_copies(b):
+            copy.start()
+    relation_table(info, table, blocks, depth)
+    for copy in kv_copies:
+        copy.wait()
+    for h in range(heads):
+        top[1 + h] = jnp.maximum(norm_top(kv[h, :, :D]), norm_top(kv[heads + h, :, :D]))
+    highest = jnp.zeros((1, heads * groups * T), F32)
+    for b in range(blocks):
+        for copy in row_copies(b):
+            copy.wait()
+        for g in range(heads * groups):
+            col = pl.ds(g * D, D)
+            qt[b, :, col] = q_v[pl.ds(b * T, T), col].T
+            dt[b, :, col] = do_v[pl.ds(b * T, T), col].T
+        wide = qt[b].astype(F32)
+        highest = jnp.maximum(highest, jnp.sum(wide * wide, axis=0, keepdims=True))
+    top[0] = jnp.max(highest)
+    tri = causal(WIDE)
+    for h in range(heads):
+        for b in range(blocks):
+            for r in range(2):
+                index = table[b * LINKED + r]
+                here = pl.ds(r * T, T)
+                source = kv.at[r * heads + h]
+                kbn[h, b, here, :] = source[row_span(index), :D] * live_factor(index)
+                values = source[row_span(index), D:] * live_factor(index)
+                vb[here, :] = values
+                vtn[h, b, :D, here] = values.T
+                vtn[h, b, D:, here] = jnp.full((ONES, T), live_factor(index), BF)
+            for j in range(0, groups, WIDE):
+                col = pl.ds(j * T, WIDE * T)
+                head_col = pl.ds((h * groups + j) * D, WIDE * D)
+                scores = jnp.dot(kbn[h, b], qt[b, :, head_col], preferred_element_type=F32)
+                exps = jnp.exp2(scores * (SCALE * LOG2E))
+                pn[h, b, :T, col] = jnp.where(tri, exps[:T], 0.0).astype(BF)
+                pn[h, b, T:, col] = exps[T:].astype(BF)
+                dpn[h, b, :, col] = jnp.dot(vb[...], dt[b, :, head_col], preferred_element_type=F32)
+                on[h, b, :, col] = jnp.dot(
+                    vtn[h, b], pn[h, b, :, col], preferred_element_type=F32
+                )[: D + 8]
+
+
+def far_kernel(*refs, head, blocks, groups, chained):
+    table, top, q_v, do_v, qt, dt, kbn, vtn, pn, dpn, on = refs[:11]
+    sources = refs[11:13]
+    at = 14 if chained else 13
+    o_out, pt, dst, kb, far_ref, diagonal_ref = refs[at : at + 6]
+    kv, vb, vt, acc, o_buf, kv_sem, out_sem = refs[at + 6 :]
+    tokens = blocks * T
+    kv_copies = [
+        pltpu.make_async_copy(source, kv.at[i], kv_sem.at[i]) for i, source in enumerate(sources)
+    ]
+    for copy in kv_copies:
+        copy.start()
+    acc[...] = jnp.zeros_like(acc)
+    for b in range(blocks):
+        kb[b, : 2 * T, :] = kbn[head, b]
+    for copy in kv_copies:
+        copy.wait()
+    for b in range(blocks):
+        for r in range(2):
+            index = table[b * LINKED + 2 + r]
+            here = pl.ds(r * T, T)
+            kb[b, pl.ds((2 + r) * T, T), :] = kv[r, row_span(index), :D] * live_factor(index)
+            values = kv[r, row_span(index), D:] * live_factor(index)
+            vb[b, here, :] = values
+            vt[b, :D, here] = values.T
+            vt[b, D:, here] = jnp.full((ONES, T), live_factor(index), BF)
+
+    def out_copy(b):
+        rows = pl.ds(pl.multiple_of(b * T, T), T)
+        columns = pl.ds(head * groups * D, groups * D)
+        return pltpu.make_async_copy(o_buf.at[b], o_out.at[rows, columns], out_sem.at[b])
+
+    keys_top = jnp.maximum(norm_top(kv[0, :, :D]), norm_top(kv[1, :, :D]))
+    keys_top = jnp.maximum(keys_top, top[1 + head])
+    safe = top[0] * keys_top <= (SAFE_EXPONENT / (SCALE * LOG2E)) ** 2
+
+    @pl.when(safe)
+    def _():
+        for b in range(blocks):
+            for j in range(0, groups, WIDE):
+                col = pl.ds(j * T, WIDE * T)
+                head_col = pl.ds((head * groups + j) * D, WIDE * D)
+                scores = jnp.dot(kb[b, 2 * T :], qt[b, :, head_col], preferred_element_type=F32)
+                exps = jnp.exp2(scores * (SCALE * LOG2E)).astype(BF)
+                pt[b, 2 * T :, col] = exps
+                sums = jnp.dot(vt[b], pt[b, 2 * T :, col], preferred_element_type=F32)
+                sums = sums[: D + 8] + on[head, b, :, col]
+                inverse = 1.0 / sums[D : D + 1]
+                out_t = sums[:D] * inverse
+                inner = jnp.sum(out_t * dt[b, :, head_col].astype(F32), axis=0, keepdims=True)
+                for w in range(WIDE):
+                    o_buf[b, :, pl.ds((j + w) * D, D)] = out_t[:, w * T : (w + 1) * T].astype(BF).T
+                dprobs = jnp.dot(vb[b], dt[b, :, head_col], preferred_element_type=F32)
+                weights = pn[head, b, :, col].astype(F32) * inverse
+                pt[b, : 2 * T, col] = weights.astype(BF)
+                dst[b, : 2 * T, col] = (weights * (dpn[head, b, :, col] - inner)).astype(BF)
+                weights = pt[b, 2 * T :, col].astype(F32) * inverse
+                pt[b, 2 * T :, col] = weights.astype(BF)
+                dst[b, 2 * T :, col] = (weights * (dprobs - inner)).astype(BF)
+            out_copy(b).start()
+
+    @pl.when(jnp.logical_not(safe))
+    def _():
+        tri = causal(1)
+
+        def block(b, carry):
+            bias = [
+                jnp.where(table[b * LINKED + r] >= 0, 0.0, -jnp.inf).astype(F32)
+                for r in range(LINKED)
+            ]
+            for g in range(groups):
+                col = pl.ds(g * T, T)
+                head_col = pl.ds((head * groups + g) * D, D)
+                scores = jnp.dot(kb[b], qt[b, :, head_col], preferred_element_type=F32)
+                dprobs = jnp.dot(vb[b], dt[b, :, head_col], preferred_element_type=F32)
+                dparts = [dpn[head, b, pl.ds(r * T, T), col] for r in range(2)]
+                dparts += [dprobs[:T], dprobs[T:]]
+                parts = [scores[r * T : (r + 1) * T] * (SCALE * LOG2E) for r in range(LINKED)]
+                parts[0] = jnp.where(tri, parts[0], -jnp.inf)
+                highs = [jnp.max(x, axis=0, keepdims=True) + bias[r] for r, x in enumerate(parts)]
+                high = functools.reduce(jnp.maximum, highs)
+                exps = [jnp.exp2(x - (high - bias[r])) for r, x in enumerate(parts)]
+                total = functools.reduce(
+                    jnp.add, [jnp.sum(x, axis=0, keepdims=True) for x in exps]
+                )
+                inverse = 1.0 / total
+                inner = inverse * functools.reduce(
+                    jnp.add,
+                    [jnp.sum(x * y, axis=0, keepdims=True) for x, y in zip(exps, dparts)],
+                )
+                for r in range(LINKED):
+                    weights = exps[r] * inverse
+                    here = pl.ds(r * T, T)
+                    pt[b, here, col] = weights.astype(BF)
+                    dst[b, here, col] = (weights * (dparts[r] - inner)).astype(BF)
+                out_t = jnp.dot(
+                    vtn[head, b], pt[b, : 2 * T, col], preferred_element_type=F32
+                ) + jnp.dot(vt[b], pt[b, 2 * T :, col], preferred_element_type=F32)
+                o_buf[b, :, pl.ds(g * D, D)] = out_t[:D].astype(BF).T
+            out_copy(b).start()
+            return carry
+
+        lax.fori_loop(0, blocks, block, 0)
+
+    for b in range(blocks):
+        rows = pl.ds(b * T, T)
+        q_rows, do_rows = (
+            jnp.concatenate(
+                [ref[rows, pl.ds((head * groups + g) * D, D)] for g in range(groups)], 0
+            )
+            for ref in (q_v, do_v)
+        )
+        dv = jnp.dot(pt[b, 2 * T :], do_rows, preferred_element_type=F32)
+        dk = jnp.dot(dst[b, 2 * T :], q_rows, preferred_element_type=F32) * SCALE
+        for r in range(2):
+            index = table[b * LINKED + 2 + r]
+            here = row_span(jnp.where(index >= 0, index + r * blocks, 2 * blocks))
+            acc[here, :D] += dk[r * T : (r + 1) * T]
+            acc[here, D:] += dv[r * T : (r + 1) * T]
+    far_ref[...] = acc[:tokens].astype(BF)
+    diagonal_ref[...] = acc[tokens : 2 * tokens].astype(BF)
+    for b in range(blocks):
+        out_copy(b).wait()
+
+
+def tail_kernel(*refs, blocks, heads, groups):
+    table, q_v, do_v = refs[:3]
+    probs = refs[3 : 3 + 3 * heads]
+    dq_out, own_ref, core_ref = refs[3 + 3 * heads : 6 + 3 * heads]
+    acc, dq_buf, out_sem = refs[6 + 3 * heads :]
+    tokens = blocks * T
+
+    def out_copy(h, b):
+        rows = pl.ds(b * T, T)
+        columns = pl.ds(h * groups * D, groups * D)
+        return pltpu.make_async_copy(dq_buf.at[h, b], dq_out.at[rows, columns], out_sem.at[h, b])
+
+    acc[...] = jnp.zeros_like(acc)
+    for h in range(heads):
+        pt, dst, kb = probs[3 * h : 3 * h + 3]
+        key_col = pl.ds(h * D, D)
+        value_col = pl.ds((heads + h) * D, D)
+        for b in range(blocks):
+            rows = pl.ds(b * T, T)
+            q_rows, do_rows = (
+                jnp.concatenate(
+                    [ref[rows, pl.ds((h * groups + g) * D, D)] for g in range(groups)], 0
+                )
+                for ref in (q_v, do_v)
+            )
+            dv = jnp.dot(pt[b, : 2 * T], do_rows, preferred_element_type=F32)
+            dk = jnp.dot(dst[b, : 2 * T], q_rows, preferred_element_type=F32) * SCALE
+            own_ref[rows, key_col] = dk[:T]
+            own_ref[rows, value_col] = dv[:T]
+            index = table[b * LINKED + 1]
+            here = row_span(jnp.where(index >= 0, index, blocks))
+            acc[here, key_col] += dk[T:]
+            acc[here, value_col] += dv[T:]
+        core_ref[:, key_col] = acc[:tokens, key_col].astype(BF)
+        core_ref[:, value_col] = acc[:tokens, value_col].astype(BF)
+        for b in range(blocks):
+            for j in range(0, groups, WIDE):
+                dq_t = SCALE * lax.dot_general(
+                    kb[b], dst[b, :, pl.ds(j * T, WIDE * T)], TN, preferred_element_type=F32
+                )
+                for w in range(WIDE):
+                    dq_buf[h, b, :, pl.ds((j + w) * D, D)] = (
+                        dq_t[:, w * T : (w + 1) * T].astype(BF).T
+                    )
+            out_copy(h, b).start()
+    for h in range(heads):
+        for b in range(blocks):
+            out_copy(h, b).wait()
+
+
+def linked_body(info, queries, output_gradient, packed):
+    tokens = queries.shape[0]
+    heads = len(packed)
+    blocks = tokens // T
+    groups = QUERY_HEADS // KEY_VALUE_HEADS
+    width = groups * T
+    depth = min(PATH_DEPTH_MAX, LINKED)
+    core = [(i, i ^ 1) for i in range(LINKED)]
+    across = [(i, i ^ 2) for i in range(LINKED)]
+    far = [lax.ppermute(own, "ctx", across) for own in packed]
+    near = [lax.ppermute(own, "ctx", core) for own in packed]
+    diagonal = [lax.ppermute(x, "ctx", core) for x in far]
+
+    vmem = pl.BlockSpec(memory_space=pltpu.VMEM)
+    smem = pl.BlockSpec(memory_space=pltpu.SMEM)
+    hbm = pl.BlockSpec(memory_space=pl.ANY)
+    kept = pltpu.VMEM
+
+    def keep(x):
+        return pltpu.with_memory_space_constraint(x, pltpu.VMEM)
+
+    shared = pl.pallas_call(
+        functools.partial(near_kernel, blocks=blocks, heads=heads, groups=groups, depth=depth),
+        in_specs=[smem] + [hbm] * (2 + 2 * heads),
+        out_specs=[smem, smem] + [vmem] * 9,
+        out_shape=[
+            jax.ShapeDtypeStruct((blocks * LINKED,), jnp.int32),
+            jax.ShapeDtypeStruct((1 + heads,), F32),
+            kept(queries.shape, BF),
+            kept(queries.shape, BF),
+            kept((blocks, D, heads * width), BF),
+            kept((blocks, D, heads * width), BF),
+            kept((heads, blocks, 2 * T, D), BF),
+            kept((heads, blocks, D + ONES, 2 * T), BF),
+            kept((heads, blocks, 2 * T, width), BF),
+            kept((heads, blocks, 2 * T, width), F32),
+            kept((heads, blocks, D + 8, width), F32),
+        ],
+        scratch_shapes=[
+            pltpu.VMEM((2 * heads, tokens, 2 * D), BF),
+            pltpu.VMEM((2 * T, D), BF),
+            pltpu.SemaphoreType.DMA((2, blocks)),
+            pltpu.SemaphoreType.DMA((2 * heads,)),
+        ],
+        compiler_params=pltpu.CompilerParams(vmem_limit_bytes=12 * 2**20),
+        name="near",
+    )(info, queries, output_gradient, *packed, *near)
+    table, top = shared[:2]
+    local = [keep(x) for x in shared[2:]]
+
+    attended = None
+    probs = []
+    far_sums = []
+    for h in range(heads):
+        chained = attended is not None
+        operands = [table, top, *local, far[h], diagonal[h]]
+        done = pl.pallas_call(
+            functools.partial(far_kernel, head=h, blocks=blocks, groups=groups, chained=chained),
+            in_specs=[smem, smem] + [vmem] * 9 + [hbm] * (3 if chained else 2),
+            out_specs=[hbm] + [vmem] * 5,
+            out_shape=[
+                jax.ShapeDtypeStruct(queries.shape, BF),
+                kept((blocks, LINKED * T, width), BF),
+                kept((blocks, LINKED * T, width), BF),
+                kept((blocks, LINKED * T, D), BF),
+                jax.ShapeDtypeStruct((tokens, 2 * D), BF),
+                jax.ShapeDtypeStruct((tokens, 2 * D), BF),
+            ],
+            input_output_aliases={len(operands): 0} if chained else {},
+            scratch_shapes=[
+                pltpu.VMEM((2, tokens, 2 * D), BF),
+                pltpu.VMEM((blocks, 2 * T, D), BF),
+                pltpu.VMEM((blocks, D + ONES, 2 * T), BF),
+                pltpu.VMEM((2 * tokens + T, 2 * D), F32),
+                pltpu.VMEM((blocks, T, groups * D), BF),
+                pltpu.SemaphoreType.DMA((2,)),
+                pltpu.SemaphoreType.DMA((blocks,)),
+            ],
+            compiler_params=pltpu.CompilerParams(vmem_limit_bytes=12 * 2**20),
+            name="far",
+        )(*operands, *([attended] if chained else []))
+        attended = done[0]
+        probs += [keep(x) for x in done[1:4]]
+        to_far, to_diagonal = done[4:]
+        onward = lax.ppermute(to_diagonal, "ctx", core)
+        onward = (to_far.astype(F32) + onward.astype(F32)).astype(BF)
+        far_sums.append(lax.ppermute(onward, "ctx", across))
+
+    d_queries, own_sums, to_core = pl.pallas_call(
+        functools.partial(tail_kernel, blocks=blocks, heads=heads, groups=groups),
+        in_specs=[smem] + [vmem] * (2 + 3 * heads),
+        out_specs=[hbm, vmem, vmem],
+        out_shape=[
+            jax.ShapeDtypeStruct(queries.shape, BF),
+            jax.ShapeDtypeStruct((tokens, 2 * heads * D), F32),
+            jax.ShapeDtypeStruct((tokens, 2 * heads * D), BF),
+        ],
+        scratch_shapes=[
+            pltpu.VMEM((tokens + T, 2 * heads * D), F32),
+            pltpu.VMEM((heads, blocks, T, groups * D), BF),
+            pltpu.SemaphoreType.DMA((heads, blocks)),
+        ],
+        compiler_params=pltpu.CompilerParams(vmem_limit_bytes=12 * 2**20),
+        name="tail",
+    )(table, local[0], local[1], *probs)
+    near_sums = own_sums + lax.ppermute(to_core, "ctx", core).astype(F32)
+    d_keys = near_sums[:, : heads * D] + jnp.concatenate(
+        [x[:, :D].astype(F32) for x in far_sums], 1
+    )
+    d_values = near_sums[:, heads * D :] + jnp.concatenate(
+        [x[:, D:].astype(F32) for x in far_sums], 1
+    )
+    return attended, d_queries, d_keys.astype(BF), d_values.astype(BF)
+
+
 def body(queries, key_states, value_tensor, output_gradient, parent, block_owner, shards):
-    tokens = queries.shape[0]
-    kv_heads = key_states.shape[1] // D
-    pairwise = shards == 4
+    heads = key_states.shape[1] // D
     me = lax.axis_index("ctx").astype(jnp.int32)
     info = jnp.concatenate([me[None], parent, block_owner])
-    core = [(i, i ^ 1) for i in range(shards)]
-    across = [(i, i ^ 2) for i in range(shards)]
     packed = [
         jnp.concatenate([key_states[:, h * D : (h + 1) * D], value_tensor[:, h * D : (h + 1) * D]], 1)
-        for h in range(kv_heads)
+        for h in range(heads)
     ]
-    gathered = []
-    for own in packed:
-        if pairwise:
-            far = lax.ppermute(own, "ctx", across)
-            near = lax.ppermute(own, "ctx", core)
-            gathered.append([own, near, far, lax.ppermute(far, "ctx", core)])
-        else:
-            gathered.append([lax.all_gather(own, "ctx", axis=0, tiled=True)])
+    if shards == LINKED:
+        return linked_body(info, queries, output_gradient, packed)
     outputs = None
     summed = []
-    for h in range(kv_heads):
-        done = attend(info, queries, output_gradient, gathered[h], outputs, h, shards, pairwise)
+    for h in range(heads):
+        gathered = lax.all_gather(packed[h], "ctx", axis=0, tiled=True)
+        done = attend(info, queries, output_gradient, gathered, outputs, h, shards)
         outputs = done[:2]
-        if pairwise:
-            sums, to_core, to_far = done[2:]
-            from_core = lax.ppermute(to_core, "ctx", core)
-            onward = (to_far.astype(F32) + from_core[tokens:].astype(F32)).astype(BF)
-            from_far = lax.ppermute(onward, "ctx", across)
-            summed.append(sums + from_core[:tokens].astype(F32) + from_far.astype(F32))
-        else:
-            summed.append(lax.psum_scatter(done[2], "ctx", scatter_dimension=0, tiled=True))
+        summed.append(lax.psum_scatter(done[2], "ctx", scatter_dimension=0, tiled=True))
     d_keys = jnp.concatenate([s[:, :D] for s in summed], 1).astype(BF)
     d_values = jnp.concatenate([s[:, D:] for s in summed], 1).astype(BF)
     return (outputs[0], outputs[1], d_keys, d_values)

time: 50.2 us -> 67.3 us (1.34)
  Pallas kernels: 20.8 us -> 38.3 us
  waiting for transfers between devices: 16.3 us -> 17.3 us
  starting transfers between devices: 7.79 us -> 7.04 us
    pallas_call x2 -> x4, Pallas kernels: 20.8 us -> 38.3 us  [the longest x2 26.4 us: linked_body(): pl.pallas_call(functools.partial(far_kernel, head=h, blocks=blocks, group...]
    concatenate x2 -> x0, other arithmetic: 1.4 us -> none  [the longest x1 0.7 us: body(): d_values = jnp.concatenate([s[:, D:] for s in summed], 1).astype(BF)]
    ppermute x10 -> x11, waiting for transfers between devices: 16.3 us -> 17.3 us  [the longest x2 8.89 us: linked_body(): far_sums.append(lax.ppermute(onward, 'ctx', across))]
    convert_element_type x2 -> x3, other arithmetic: 0.1 us -> 0.93 us  [the longest x1 0.83 us: linked_body(): return (attended, d_queries, d_keys.astype(BF), d_values.astype(BF))]
    ppermute x10 -> x11, starting transfers between devices: 7.79 us -> 7.04 us  [the longest x2 3.12 us: linked_body(): far = [lax.ppermute(own, 'ctx', across) for own in packed]]
  transfers between devices with their start and end apart: 10 -> 11, of which waited for: 4 -> 4; matrix products, arithmetic and copies ran while one was open for 1% -> 0% of each run, Pallas kernels for 42% -> 57%
where the time goes in v2:
time: 67.3 us; the launch traced here: 67.1 us
  Pallas kernels  38.3 us (57%)
  waiting for transfers between devices  17.3 us (26%)
  starting transfers between devices  7.04 us (10%)
  local copies, waits for them, and re-layouts  2.63 us (4%)
  other arithmetic  1.17 us (2%)
  between operations  0.78 us (1%)
    pallas_call x2, Pallas kernels, linked_body(): pl.pallas_call(functools.partial(far_kernel, head=h, blocks=blocks, group...  26.4 us
    ppermute x2, waiting for transfers between devices, linked_body(): far_sums.append(lax.ppermute(onward, 'ctx', across))  8.89 us
    ppermute x2, waiting for transfers between devices, linked_body(): far = [lax.ppermute(own, 'ctx', across) for own in packed]  8.34 us
    pallas_call x1, Pallas kernels, linked_body(): pl.pallas_call(functools.partial(near_kernel, blocks=blocks, heads=heads,...  7.49 us
    pallas_call x1, Pallas kernels, linked_body(): pl.pallas_call(functools.partial(tail_kernel, blocks=blocks, heads=heads,...  4.4 us
    ppermute x2, starting transfers between devices, linked_body(): far = [lax.ppermute(own, 'ctx', across) for own in packed]  3.12 us
    ppermute x2, starting transfers between devices, linked_body(): far_sums.append(lax.ppermute(onward, 'ctx', across))  2.16 us
    unnamed x8, local copies, waits for them, and re-layouts  1.42 us
  transfers between devices with their start and end apart: 11, of which 4 were waited for; matrix products, arithmetic and copies ran while one was open for 0% of the time, Pallas kernels for 57%

profile of v2, /device:TPU:0, one launch (start us, length us, event | category | flops | bytes accessed | tf_op | source)
XLA Modules:
  0.0 67.1 jit_solution(15471415913057237288)
XLA Ops:
  0.6 0.0 copy-start.3
  0.6 0.0 copy-start.2
  0.7 0.0 copy-start
  0.7 1.2 %fusion.4 = (bf16[384,128]{1,0:T(8,128)(2,1)S(1)}, bf16[384,128]{1,0:T(8,128)(2,1)S(1)}, bf16[384,128]{1,0:T(8,128)(2,1)S(1)}, bf16[384,128]{1,0:T(8,128)(2,1)S(1)}) fusion(bf16[384,256]{1,0:T(8,128)(2,1)} %param.7, bf16[384,256]{1,0:T(8,128)(2,1)} %param.8), kind=kLoop, calls=%fused_computation.12 | loop fusion | bytes 786432 | tf_op jit(solution)/shard_map/slice | solution.py:582
  1.9 3.0 %collective-permute-start.4 = (bf16[384,256]{1,0:T(8,128)(2,1)S(1)}, bf16[384,256]{1,0:T(8,128)(2,1)S(1)}, u32[]{:S(2)}, u32[]{:S(2)}) collective-permute-start(bf16[384,256]{1,0:T(8,128)(2,1)S(1)} %pad_maximum_fusion.refs_3_), channel_id=1, source_target_pairs={{0,8},{4,12},{8,0},{12,4},{1,9},{5,13},{9,1},{13,5},{2,10},{6,14},... | collective-permute-start | bytes 589832 | tf_op jit(solution)/shard_map/ppermute | solution.py:471
  4.9 0.1 collective-permute-start.2
  5.0 0.1 collective-permute-start.1
  5.1 0.5 collective-permute-start
  5.6 5.0 %collective-permute-done.4.refs_11_ = bf16[384,256]{1,0:T(8,128)(2,1)S(1)} collective-permute-done((bf16[384,256]{1,0:T(8,128)(2,1)S(1)}, bf16[384,256]{1,0:T(8,128)(2,1)S(1)}, u32[]{:S(2)}, u32[]{:S(2)}) %collective-permute-start.4) | collective-permute-done | bytes 196640 | tf_op jit(solution)/shard_map/ppermute | solution.py:471
  10.6 0.0 collective-permute-start.5
  10.6 0.0 copy-done.3
  10.7 0.0 copy-done.2
  10.7 0.1 pad_add_fusion.refs_0_
  10.7 3.3 %collective-permute-done.2.refs_11_ = bf16[384,256]{1,0:T(8,128)(2,1)S(1)} collective-permute-done((bf16[384,256]{1,0:T(8,128)(2,1)S(1)}, bf16[384,256]{1,0:T(8,128)(2,1)S(1)}, u32[]{:S(2)}, u32[]{:S(2)}) %collective-permute-start.2) | collective-permute-done | bytes 196640 | tf_op jit(solution)/shard_map/ppermute | solution.py:471
  14.0 0.0 collective-permute-start.3
  14.0 0.0 collective-permute-done.1.refs_6_
  14.0 0.0 collective-permute-done.refs_5_
  14.0 0.0 copy-done
  14.1 0.0 copy-start.1
  14.1 1.4 %copy-done.1 = bf16[384,2048]{1,0:T(8,128)(2,1)S(1)} copy-done((bf16[384,2048]{1,0:T(8,128)(2,1)S(1)}, bf16[384,2048]{1,0:T(8,128)(2,1)}, u32[]{:S(2)}) %copy-start.1) | copy-done | bytes 1572888
  15.5 7.5 %near.1 = (s32[12]{0:T(128)S(1)}, f32[3]{0:T(128)S(1)}, bf16[384,2048]{1,0:T(8,128)(2,1)S(1)}, bf16[384,2048]{1,0:T(8,128)(2,1)S(1)}, bf16[3,128,2048]{2,1,0:T(8...) custom-call(s32[25]{0:T(128)S(1)} %pad_add_fusion.refs_0_, ...), custom_call_target="tpu_custom_call" | custom-call | tf_op jit(solution)/shard_map/near/pallas_call | solution.py:483
  23.0 0.0 collective-permute-done.5.refs_12_
  23.0 13.3 %far.2 = (bf16[384,2048]{1,0:T(8,128)(2,1)}, bf16[3,512,1024]{2,1,0:T(8,128)(2,1)S(1)}, bf16[3,512,1024]{2,1,0:T(8,128)(2,1)S(1)}, bf16[3,512,128]{2,1,0:T(8,128...) custom-call(s32[12]{0:T(128)S(1)} %get-tuple-element.30.refs_0_, f32[3]{0:T(128)S(1)} %get-tuple-element.31.refs_1_, ...), custom_call_target="tpu_custom_call" | custom-call | tf_op jit(solution)/shard_map/far/pallas_call | solution.py:518
  36.2 0.6 collective-permute-start.7
  36.8 0.0 collective-permute-done.3.refs_12_
  36.8 13.1 %far.3 = (bf16[384,2048]{1,0:T(8,128)(2,1)}, bf16[3,512,1024]{2,1,0:T(8,128)(2,1)S(1)}, bf16[3,512,1024]{2,1,0:T(8,128)(2,1)S(1)}, bf16[3,512,128]{2,1,0:T(8,128...) custom-call(s32[12]{0:T(128)S(1)} %get-tuple-element.30.refs_0_, ...), custom_call_target="tpu_custom_call", output_to_operand_aliasing={{0}: (13, {})} | custom-call | tf_op jit(solution)/shard_map/far/pallas_call | solution.py:518
  49.9 0.1 collective-permute-start.9
  50.0 4.4 %tail.1 = (bf16[384,2048]{1,0:T(8,128)(2,1)}, f32[384,512]{1,0:T(8,128)S(1)}, bf16[384,512]{1,0:T(8,128)(2,1)S(1)}) custom-call(s32[12]{0:T(128)S(1)} %get-tuple-element.30.refs_0_, bf16[384,2048]{1,0:T(8,128)(2,1)S(1)} %get-tuple-element.32.refs_2_.refs_1_, bf16[384,2048]{1,0:T(8,128)(2,1)S(1)} %get-tuple-element.33.refs_3_.refs_2_, ...), custom_call_target="tpu_custom_call" | custom-call | tf_op jit(solution)/shard_map/tail/pallas_call | solution.py:550
  54.4 0.5 collective-permute-start.6
  55.0 0.0 collective-permute-done.7
  55.0 1.8 %collective-permute-start.8 = (bf16[384,256]{1,0:T(8,128)(2,1)S(1)}, bf16[384,256]{1,0:T(8,128)(2,1)S(1)}, u32[]{:S(2)}, u32[]{:S(2)}) collective-permute-start(bf16[384,256]{1,0:T(8,128)(2,1)S(1)} %add_convert_fusion.1), channel_id=1, source_target_pairs={{0,8},{4,12},{8,0},{12,4},{1,9},{5,13},{9,1},{13,5},{2,10},{6,14},... | collective-permute-start | bytes 589832 | tf_op jit(solution)/shard_map/ppermute | solution.py:548
  56.8 0.0 collective-permute-done.9
  56.8 0.1 add_convert_fusion
  56.9 0.4 collective-permute-start.10
  57.2 5.6 %collective-permute-done.8 = bf16[384,256]{1,0:T(8,128)(2,1)S(1)} collective-permute-done((bf16[384,256]{1,0:T(8,128)(2,1)S(1)}, bf16[384,256]{1,0:T(8,128)(2,1)S(1)}, u32[]{:S(2)}, u32[]{:S(2)}) %collective-permute-start.8) | collective-permute-done | bytes 196640 | tf_op jit(solution)/shard_map/ppermute | solution.py:548
  62.9 3.3 %collective-permute-done.10 = bf16[384,256]{1,0:T(8,128)(2,1)S(1)} collective-permute-done((bf16[384,256]{1,0:T(8,128)(2,1)S(1)}, bf16[384,256]{1,0:T(8,128)(2,1)S(1)}, u32[]{:S(2)}, u32[]{:S(2)}) %collective-permute-start.10) | collective-permute-done | bytes 196640 | tf_op jit(solution)/shard_map/ppermute | solution.py:548
  66.2 0.0 collective-permute-done.6
  66.2 0.1 convert_add_fusion
  66.3 0.8 %fusion = (bf16[384,256]{1,0:T(8,128)(2,1)}, bf16[384,256]{1,0:T(8,128)(2,1)}) fusion(f32[384,512]{1,0:T(8,128)S(1)} %convert_add_fusion, bf16[384,128]{1,0:T(8,128)(2,1)S(1)} %get-tuple-element.60, bf16[384,128]{1,0:T(8,128)(2,1)S(1)} %get-tuple-element.58, bf16[384,128]{1,0:T(8,128)(2,1)S(1)} %get-tuple-element.61, bf16[384,128]{1,0:T(8,128)(2,1)S(1)} %get-tuple-element.59), kind=kLoop, calls=%fused_computation.2 | loop fusion | flops 1179648 | bytes 1572864 | tf_op jit(solution)/shard_map/convert_element_type | solution.py:574
  (5 shorter events, 0.1 us)
Async XLA Ops:
  0.6 10.0 %copy-start.3 = (s32[12]{0:T(128)S(1)}, s32[12]{0:T(128)}, u32[]{:S(2)}) copy-start(s32[12]{0:T(128)} %param.10) | copy-start | bytes 148
  0.6 10.0 %copy-start.2 = (s32[12]{0:T(128)S(1)}, s32[12]{0:T(128)}, u32[]{:S(2)}) copy-start(s32[12]{0:T(128)} %param.11) | copy-start | bytes 148
  0.7 13.4 %copy-start = (bf16[384,2048]{1,0:T(8,128)(2,1)S(1)}, bf16[384,2048]{1,0:T(8,128)(2,1)}, u32[]{:S(2)}) copy-start(bf16[384,2048]{1,0:T(8,128)(2,1)} %refs_1_.1) | copy-start | bytes 4718596
  1.9 8.8 %collective-permute-start.4 = (bf16[384,256]{1,0:T(8,128)(2,1)S(1)}, bf16[384,256]{1,0:T(8,128)(2,1)S(1)}, u32[]{:S(2)}, u32[]{:S(2)}) collective-permute-start(bf16[384,256]{1,0:T(8,128)(2,1)S(1)} %pad_maximum_fusion.refs_3_), channel_id=1, source_target_pairs={{0,8},{4,12},{8,0},{12,4},{1,9},{5,13},{9,1},{13,5},{2,10},{6,14},... | collective-permute-start | bytes 589832 | tf_op jit(solution)/shard_map/ppermute | solution.py:471
  4.9 9.1 %collective-permute-start.2 = (bf16[384,256]{1,0:T(8,128)(2,1)S(1)}, bf16[384,256]{1,0:T(8,128)(2,1)S(1)}, u32[]{:S(2)}, u32[]{:S(2)}) collective-permute-start(bf16[384,256]{1,0:T(8,128)(2,1)S(1)} %pad_maximum_fusion.1.refs_4_), channel_id=1, source_target_pairs={{0,8},{4,12},{8,0},{12,4},{1,9},{5,13},{9,1},{13,5},{2,10},{6,14},... | collective-permute-start | bytes 589832 | tf_op jit(solution)/shard_map/ppermute | solution.py:471
  5.0 9.0 %collective-permute-start.1 = (bf16[384,256]{1,0:T(8,128)(2,1)S(1)}, bf16[384,256]{1,0:T(8,128)(2,1)S(1)}, u32[]{:S(2)}, u32[]{:S(2)}) collective-permute-start(bf16[384,256]{1,0:T(8,128)(2,1)S(1)} %pad_maximum_fusion.1.refs_4_), channel_id=1, source_target_pairs={{0,4},{4,0},{8,12},{12,8},{1,5},{5,1},{9,13},{13,9},{2,6},{6,2},{1... | collective-permute-start | bytes 589832 | tf_op jit(solution)/shard_map/ppermute | solution.py:472
  5.1 8.9 %collective-permute-start = (bf16[384,256]{1,0:T(8,128)(2,1)S(1)}, bf16[384,256]{1,0:T(8,128)(2,1)S(1)}, u32[]{:S(2)}, u32[]{:S(2)}) collective-permute-start(bf16[384,256]{1,0:T(8,128)(2,1)S(1)} %pad_maximum_fusion.refs_3_), channel_id=1, source_target_pairs={{0,4},{4,0},{8,12},{12,8},{1,5},{5,1},{9,13},{13,9},{2,6},{6,2},{1... | collective-permute-start | bytes 589832 | tf_op jit(solution)/shard_map/ppermute | solution.py:472
  10.6 12.3 %collective-permute-start.5 = (bf16[384,256]{1,0:T(8,128)(2,1)S(1)}, bf16[384,256]{1,0:T(8,128)(2,1)S(1)}, u32[]{:S(2)}, u32[]{:S(2)}) collective-permute-start(bf16[384,256]{1,0:T(8,128)(2,1)S(1)} %collective-permute-done.4.refs_11_), channel_id=1, source_target_pairs={{0,4},{4,0},{8,12},{12,8},{1,5},{5,1},{9,13},{13,9},{2,6},{6,2},{1... | collective-permute-start | bytes 589832 | tf_op jit(solution)/shard_map/ppermute | solution.py:473
  14.0 22.8 %collective-permute-start.3 = (bf16[384,256]{1,0:T(8,128)(2,1)S(1)}, bf16[384,256]{1,0:T(8,128)(2,1)S(1)}, u32[]{:S(2)}, u32[]{:S(2)}) collective-permute-start(bf16[384,256]{1,0:T(8,128)(2,1)S(1)} %collective-permute-done.2.refs_11_), channel_id=1, source_target_pairs={{0,4},{4,0},{8,12},{12,8},{1,5},{5,1},{9,13},{13,9},{2,6},{6,2},{1... | collective-permute-start | bytes 589832 | tf_op jit(solution)/shard_map/ppermute | solution.py:473
  14.1 1.4 %copy-start.1 = (bf16[384,2048]{1,0:T(8,128)(2,1)S(1)}, bf16[384,2048]{1,0:T(8,128)(2,1)}, u32[]{:S(2)}) copy-start(bf16[384,2048]{1,0:T(8,128)(2,1)} %refs_2_.1) | copy-start | bytes 4718596
  36.2 18.7 %collective-permute-start.7 = (bf16[384,256]{1,0:T(8,128)(2,1)S(1)}, bf16[384,256]{1,0:T(8,128)(2,1)S(1)}, u32[]{:S(2)}, u32[]{:S(2)}) collective-permute-start(bf16[384,256]{1,0:T(8,128)(2,1)S(1)} %get-tuple-element.53), channel_id=1, source_target_pairs={{0,4},{4,0},{8,12},{12,8},{1,5},{5,1},{9,13},{13,9},{2,6},{6,2},{1... | collective-permute-start | bytes 589832 | tf_op jit(solution)/shard_map/ppermute | solution.py:546
  49.9 6.9 %collective-permute-start.9 = (bf16[384,256]{1,0:T(8,128)(2,1)S(1)}, bf16[384,256]{1,0:T(8,128)(2,1)S(1)}, u32[]{:S(2)}, u32[]{:S(2)}) collective-permute-start(bf16[384,256]{1,0:T(8,128)(2,1)S(1)} %get-tuple-element.55), channel_id=1, source_target_pairs={{0,4},{4,0},{8,12},{12,8},{1,5},{5,1},{9,13},{13,9},{2,6},{6,2},{1... | collective-permute-start | bytes 589832 | tf_op jit(solution)/shard_map/ppermute | solution.py:546
  54.4 11.7 %collective-permute-start.6 = (bf16[384,512]{1,0:T(8,128)(2,1)S(1)}, bf16[384,512]{1,0:T(8,128)(2,1)S(1)}, u32[]{:S(2)}, u32[]{:S(2)}) collective-permute-start(bf16[384,512]{1,0:T(8,128)(2,1)S(1)} %get-tuple-element.51), channel_id=1, source_target_pairs={{0,4},{4,0},{8,12},{12,8},{1,5},{5,1},{9,13},{13,9},{2,6},{6,2},{1... | collective-permute-start | bytes 1179656 | tf_op jit(solution)/shard_map/ppermute | solution.py:567
  55.0 7.8 %collective-permute-start.8 = (bf16[384,256]{1,0:T(8,128)(2,1)S(1)}, bf16[384,256]{1,0:T(8,128)(2,1)S(1)}, u32[]{:S(2)}, u32[]{:S(2)}) collective-permute-start(bf16[384,256]{1,0:T(8,128)(2,1)S(1)} %add_convert_fusion.1), channel_id=1, source_target_pairs={{0,8},{4,12},{8,0},{12,4},{1,9},{5,13},{9,1},{13,5},{2,10},{6,14},... | collective-permute-start | bytes 589832 | tf_op jit(solution)/shard_map/ppermute | solution.py:548
  56.9 9.3 %collective-permute-start.10 = (bf16[384,256]{1,0:T(8,128)(2,1)S(1)}, bf16[384,256]{1,0:T(8,128)(2,1)S(1)}, u32[]{:S(2)}, u32[]{:S(2)}) collective-permute-start(bf16[384,256]{1,0:T(8,128)(2,1)S(1)} %add_convert_fusion), channel_id=1, source_target_pairs={{0,8},{4,12},{8,0},{12,4},{1,9},{5,13},{9,1},{13,5},{2,10},{6,14},... | collective-permute-start | bytes 589832 | tf_op jit(solution)/shard_map/ppermute | solution.py:548

commit v3 on v2

--- a/solution.py
+++ b/solution.py
@@ -221,92 +221,90 @@
     return jnp.concatenate([keys <= queries] * width, 1)
 
 
-def near_kernel(*refs, blocks, heads, groups, depth):
-    info, q_in, do_in = refs[:3]
-    own = refs[3 : 3 + heads]
-    near = refs[3 + heads : 3 + 2 * heads]
-    table, top, q_v, do_v, qt, dt, kbn, vtn, pn, dpn, on = refs[3 + 2 * heads : 14 + 2 * heads]
-    kv, vb, row_sem, kv_sem = refs[14 + 2 * heads :]
-
-    def row_copies(b):
-        rows = pl.ds(b * T, T)
-        return (
-            pltpu.make_async_copy(q_in.at[rows], q_v.at[rows], row_sem.at[0, b]),
-            pltpu.make_async_copy(do_in.at[rows], do_v.at[rows], row_sem.at[1, b]),
-        )
+def near_kernel(*refs, head, blocks, heads, groups, depth):
+    if head == 0:
+        info, q_in, do_in, own, near = refs[:5]
+        table, top, q_v, do_v, qt, dt, kbn, vtn, pn, dpn, on = refs[5:16]
+        kv, vb, kv_sem, row_sem = refs[16:]
+    else:
+        table, qt, dt, own, near = refs[:5]
+        top, kbn, vtn, pn, dpn, on = refs[5:11]
+        kv, vb, kv_sem = refs[11:]
 
     kv_copies = [
-        pltpu.make_async_copy(source, kv.at[i], kv_sem.at[i]) for i, source in enumerate(own + near)
+        pltpu.make_async_copy(source, kv.at[i], kv_sem.at[i]) for i, source in enumerate((own, near))
     ]
     for copy in kv_copies:
         copy.start()
-    for b in range(blocks):
-        for copy in row_copies(b):
-            copy.start()
-    relation_table(info, table, blocks, depth)
+    if head == 0:
+
+        def row_copies(b):
+            rows = pl.ds(b * T, T)
+            return (
+                pltpu.make_async_copy(q_in.at[rows], q_v.at[rows], row_sem.at[0, b]),
+                pltpu.make_async_copy(do_in.at[rows], do_v.at[rows], row_sem.at[1, b]),
+            )
+
+        for b in range(blocks):
+            for copy in row_copies(b):
+                copy.start()
+        relation_table(info, table, blocks, depth)
+        highest = jnp.zeros((1, heads * groups * T), F32)
+        for b in range(blocks):
+            for copy in row_copies(b):
+                copy.wait()
+            for g in range(heads * groups):
+                col = pl.ds(g * D, D)
+                qt[b, :, col] = q_v[pl.ds(b * T, T), col].T
+                dt[b, :, col] = do_v[pl.ds(b * T, T), col].T
+            wide = qt[b].astype(F32)
+            highest = jnp.maximum(highest, jnp.sum(wide * wide, axis=0, keepdims=True))
+        top[0] = jnp.max(highest)
     for copy in kv_copies:
         copy.wait()
-    for h in range(heads):
-        top[1 + h] = jnp.maximum(norm_top(kv[h, :, :D]), norm_top(kv[heads + h, :, :D]))
-    highest = jnp.zeros((1, heads * groups * T), F32)
-    for b in range(blocks):
-        for copy in row_copies(b):
-            copy.wait()
-        for g in range(heads * groups):
-            col = pl.ds(g * D, D)
-            qt[b, :, col] = q_v[pl.ds(b * T, T), col].T
-            dt[b, :, col] = do_v[pl.ds(b * T, T), col].T
-        wide = qt[b].astype(F32)
-        highest = jnp.maximum(highest, jnp.sum(wide * wide, axis=0, keepdims=True))
-    top[0] = jnp.max(highest)
+    top[1 if head == 0 else 0] = jnp.maximum(norm_top(kv[0, :, :D]), norm_top(kv[1, :, :D]))
+    for b in range(blocks):
+        for r in range(2):
+            index = table[b * LINKED + r]
+            here = pl.ds(r * T, T)
+            kbn[b, here, :] = kv[r, row_span(index), :D] * live_factor(index)
+            values = kv[r, row_span(index), D:] * live_factor(index)
+            vb[b, here, :] = values
+            vtn[b, :D, here] = values.T
+            vtn[b, D:, here] = jnp.full((ONES, T), live_factor(index), BF)
     tri = causal(WIDE)
-    for h in range(heads):
-        for b in range(blocks):
-            for r in range(2):
-                index = table[b * LINKED + r]
-                here = pl.ds(r * T, T)
-                source = kv.at[r * heads + h]
-                kbn[h, b, here, :] = source[row_span(index), :D] * live_factor(index)
-                values = source[row_span(index), D:] * live_factor(index)
-                vb[here, :] = values
-                vtn[h, b, :D, here] = values.T
-                vtn[h, b, D:, here] = jnp.full((ONES, T), live_factor(index), BF)
-            for j in range(0, groups, WIDE):
-                col = pl.ds(j * T, WIDE * T)
-                head_col = pl.ds((h * groups + j) * D, WIDE * D)
-                scores = jnp.dot(kbn[h, b], qt[b, :, head_col], preferred_element_type=F32)
-                exps = jnp.exp2(scores * (SCALE * LOG2E))
-                pn[h, b, :T, col] = jnp.where(tri, exps[:T], 0.0).astype(BF)
-                pn[h, b, T:, col] = exps[T:].astype(BF)
-                dpn[h, b, :, col] = jnp.dot(vb[...], dt[b, :, head_col], preferred_element_type=F32)
-                on[h, b, :, col] = jnp.dot(
-                    vtn[h, b], pn[h, b, :, col], preferred_element_type=F32
-                )[: D + 8]
+    pieces = [
+        (b, pl.ds(j * T, WIDE * T), pl.ds((head * groups + j) * D, WIDE * D))
+        for b in range(blocks)
+        for j in range(0, groups, WIDE)
+    ]
+    for b, col, head_col in pieces:
+        scores = jnp.dot(kbn[b], qt[b, :, head_col], preferred_element_type=F32)
+        exps = jnp.exp2(scores * (SCALE * LOG2E))
+        pn[b, :T, col] = jnp.where(tri, exps[:T], 0.0).astype(BF)
+        pn[b, T:, col] = exps[T:].astype(BF)
+    for b, col, head_col in pieces:
+        dpn[b, :, col] = jnp.dot(vb[b], dt[b, :, head_col], preferred_element_type=F32)
+    for b, col, head_col in pieces:
+        on[b, :, col] = jnp.dot(vtn[b], pn[b, :, col], preferred_element_type=F32)[: D + 8]
 
 
 def far_kernel(*refs, head, blocks, groups, chained):
-    table, top, q_v, do_v, qt, dt, kbn, vtn, pn, dpn, on = refs[:11]
-    sources = refs[11:13]
-    at = 14 if chained else 13
+    table, top, near_top, q_v, do_v, qt, dt, kbn, vtn, pn, dpn, on = refs[:12]
+    sources = refs[12:14]
+    at = 15 if chained else 14
     o_out, pt, dst, kb, far_ref, diagonal_ref = refs[at : at + 6]
-    kv, vb, vt, acc, o_buf, kv_sem, out_sem = refs[at + 6 :]
+    vb, vt, acc, o_buf, out_sem = refs[at + 6 :]
     tokens = blocks * T
-    kv_copies = [
-        pltpu.make_async_copy(source, kv.at[i], kv_sem.at[i]) for i, source in enumerate(sources)
-    ]
-    for copy in kv_copies:
-        copy.start()
     acc[...] = jnp.zeros_like(acc)
     for b in range(blocks):
-        kb[b, : 2 * T, :] = kbn[head, b]
-    for copy in kv_copies:
-        copy.wait()
+        kb[b, : 2 * T, :] = kbn[b]
     for b in range(blocks):
         for r in range(2):
             index = table[b * LINKED + 2 + r]
             here = pl.ds(r * T, T)
-            kb[b, pl.ds((2 + r) * T, T), :] = kv[r, row_span(index), :D] * live_factor(index)
-            values = kv[r, row_span(index), D:] * live_factor(index)
+            kb[b, pl.ds((2 + r) * T, T), :] = sources[r][row_span(index), :D] * live_factor(index)
+            values = sources[r][row_span(index), D:] * live_factor(index)
             vb[b, here, :] = values
             vt[b, :D, here] = values.T
             vt[b, D:, here] = jnp.full((ONES, T), live_factor(index), BF)
@@ -316,34 +314,40 @@
         columns = pl.ds(head * groups * D, groups * D)
         return pltpu.make_async_copy(o_buf.at[b], o_out.at[rows, columns], out_sem.at[b])
 
-    keys_top = jnp.maximum(norm_top(kv[0, :, :D]), norm_top(kv[1, :, :D]))
-    keys_top = jnp.maximum(keys_top, top[1 + head])
+    keys_top = jnp.maximum(norm_top(sources[0][:, :D]), norm_top(sources[1][:, :D]))
+    keys_top = jnp.maximum(keys_top, near_top[1 if head == 0 else 0])
     safe = top[0] * keys_top <= (SAFE_EXPONENT / (SCALE * LOG2E)) ** 2
 
     @pl.when(safe)
     def _():
-        for b in range(blocks):
-            for j in range(0, groups, WIDE):
-                col = pl.ds(j * T, WIDE * T)
-                head_col = pl.ds((head * groups + j) * D, WIDE * D)
-                scores = jnp.dot(kb[b, 2 * T :], qt[b, :, head_col], preferred_element_type=F32)
-                exps = jnp.exp2(scores * (SCALE * LOG2E)).astype(BF)
-                pt[b, 2 * T :, col] = exps
-                sums = jnp.dot(vt[b], pt[b, 2 * T :, col], preferred_element_type=F32)
-                sums = sums[: D + 8] + on[head, b, :, col]
-                inverse = 1.0 / sums[D : D + 1]
-                out_t = sums[:D] * inverse
-                inner = jnp.sum(out_t * dt[b, :, head_col].astype(F32), axis=0, keepdims=True)
-                for w in range(WIDE):
-                    o_buf[b, :, pl.ds((j + w) * D, D)] = out_t[:, w * T : (w + 1) * T].astype(BF).T
-                dprobs = jnp.dot(vb[b], dt[b, :, head_col], preferred_element_type=F32)
-                weights = pn[head, b, :, col].astype(F32) * inverse
-                pt[b, : 2 * T, col] = weights.astype(BF)
-                dst[b, : 2 * T, col] = (weights * (dpn[head, b, :, col] - inner)).astype(BF)
-                weights = pt[b, 2 * T :, col].astype(F32) * inverse
-                pt[b, 2 * T :, col] = weights.astype(BF)
-                dst[b, 2 * T :, col] = (weights * (dprobs - inner)).astype(BF)
-            out_copy(b).start()
+        pieces = [
+            (b, j, pl.ds(j * T, WIDE * T), pl.ds((head * groups + j) * D, WIDE * D))
+            for b in range(blocks)
+            for j in range(0, groups, WIDE)
+        ]
+        for b, j, col, head_col in pieces:
+            scores = jnp.dot(kb[b, 2 * T :], qt[b, :, head_col], preferred_element_type=F32)
+            pt[b, 2 * T :, col] = jnp.exp2(scores * (SCALE * LOG2E)).astype(BF)
+        rows_done = []
+        for b, j, col, head_col in pieces:
+            sums = jnp.dot(vt[b], pt[b, 2 * T :, col], preferred_element_type=F32)
+            sums = sums[: D + 8] + on[b, :, col]
+            inverse = 1.0 / sums[D : D + 1]
+            out_t = sums[:D] * inverse
+            inner = jnp.sum(out_t * dt[b, :, head_col].astype(F32), axis=0, keepdims=True)
+            rows_done.append((inverse, inner))
+            for w in range(WIDE):
+                o_buf[b, :, pl.ds((j + w) * D, D)] = out_t[:, w * T : (w + 1) * T].astype(BF).T
+            if j + WIDE == groups:
+                out_copy(b).start()
+        for (b, j, col, head_col), (inverse, inner) in zip(pieces, rows_done):
+            dprobs = jnp.dot(vb[b], dt[b, :, head_col], preferred_element_type=F32)
+            weights = pn[b, :, col].astype(F32) * inverse
+            pt[b, : 2 * T, col] = weights.astype(BF)
+            dst[b, : 2 * T, col] = (weights * (dpn[b, :, col] - inner)).astype(BF)
+            weights = pt[b, 2 * T :, col].astype(F32) * inverse
+            pt[b, 2 * T :, col] = weights.astype(BF)
+            dst[b, 2 * T :, col] = (weights * (dprobs - inner)).astype(BF)
 
     @pl.when(jnp.logical_not(safe))
     def _():
@@ -359,7 +363,7 @@
                 head_col = pl.ds((head * groups + g) * D, D)
                 scores = jnp.dot(kb[b], qt[b, :, head_col], preferred_element_type=F32)
                 dprobs = jnp.dot(vb[b], dt[b, :, head_col], preferred_element_type=F32)
-                dparts = [dpn[head, b, pl.ds(r * T, T), col] for r in range(2)]
+                dparts = [dpn[b, pl.ds(r * T, T), col] for r in range(2)]
                 dparts += [dprobs[:T], dprobs[T:]]
                 parts = [scores[r * T : (r + 1) * T] * (SCALE * LOG2E) for r in range(LINKED)]
                 parts[0] = jnp.where(tri, parts[0], -jnp.inf)
@@ -380,7 +384,7 @@
                     pt[b, here, col] = weights.astype(BF)
                     dst[b, here, col] = (weights * (dparts[r] - inner)).astype(BF)
                 out_t = jnp.dot(
-                    vtn[head, b], pt[b, : 2 * T, col], preferred_element_type=F32
+                    vtn[b], pt[b, : 2 * T, col], preferred_element_type=F32
                 ) + jnp.dot(vt[b], pt[b, 2 * T :, col], preferred_element_type=F32)
                 o_buf[b, :, pl.ds(g * D, D)] = out_t[:D].astype(BF).T
             out_copy(b).start()
@@ -409,54 +413,49 @@
         out_copy(b).wait()
 
 
-def tail_kernel(*refs, blocks, heads, groups):
-    table, q_v, do_v = refs[:3]
-    probs = refs[3 : 3 + 3 * heads]
-    dq_out, own_ref, core_ref = refs[3 + 3 * heads : 6 + 3 * heads]
-    acc, dq_buf, out_sem = refs[6 + 3 * heads :]
+def tail_kernel(*refs, head, blocks, groups, chained):
+    table, q_v, do_v, pt, dst, kb = refs[:6]
+    dq_out, own_ref, core_ref = refs[7:10] if chained else refs[6:9]
+    acc, dq_buf, out_sem = refs[10:] if chained else refs[9:]
     tokens = blocks * T
 
-    def out_copy(h, b):
+    def out_copy(b):
         rows = pl.ds(b * T, T)
-        columns = pl.ds(h * groups * D, groups * D)
-        return pltpu.make_async_copy(dq_buf.at[h, b], dq_out.at[rows, columns], out_sem.at[h, b])
+        columns = pl.ds(head * groups * D, groups * D)
+        return pltpu.make_async_copy(dq_buf.at[b], dq_out.at[rows, columns], out_sem.at[b])
 
     acc[...] = jnp.zeros_like(acc)
-    for h in range(heads):
-        pt, dst, kb = probs[3 * h : 3 * h + 3]
-        key_col = pl.ds(h * D, D)
-        value_col = pl.ds((heads + h) * D, D)
-        for b in range(blocks):
-            rows = pl.ds(b * T, T)
-            q_rows, do_rows = (
-                jnp.concatenate(
-                    [ref[rows, pl.ds((h * groups + g) * D, D)] for g in range(groups)], 0
-                )
-                for ref in (q_v, do_v)
+    for b in range(blocks):
+        for j in range(0, groups, WIDE):
+            dq_t = SCALE * lax.dot_general(
+                kb[b], dst[b, :, pl.ds(j * T, WIDE * T)], TN, preferred_element_type=F32
             )
-            dv = jnp.dot(pt[b, : 2 * T], do_rows, preferred_element_type=F32)
-            dk = jnp.dot(dst[b, : 2 * T], q_rows, preferred_element_type=F32) * SCALE
-            own_ref[rows, key_col] = dk[:T]
-            own_ref[rows, value_col] = dv[:T]
-            index = table[b * LINKED + 1]
-            here = row_span(jnp.where(index >= 0, index, blocks))
-            acc[here, key_col] += dk[T:]
-            acc[here, value_col] += dv[T:]
-        core_ref[:, key_col] = acc[:tokens, key_col].astype(BF)
-        core_ref[:, value_col] = acc[:tokens, value_col].astype(BF)
-        for b in range(blocks):
-            for j in range(0, groups, WIDE):
-                dq_t = SCALE * lax.dot_general(
-                    kb[b], dst[b, :, pl.ds(j * T, WIDE * T)], TN, preferred_element_type=F32
-                )
-                for w in range(WIDE):
-                    dq_buf[h, b, :, pl.ds((j + w) * D, D)] = (
-                        dq_t[:, w * T : (w + 1) * T].astype(BF).T
-                    )
-            out_copy(h, b).start()
-    for h in range(heads):
-        for b in range(blocks):
-            out_copy(h, b).wait()
+            for w in range(WIDE):
+                dq_buf[b, :, pl.ds((j + w) * D, D)] = dq_t[:, w * T : (w + 1) * T].astype(BF).T
+        out_copy(b).start()
+    for b in range(blocks):
+        rows = pl.ds(b * T, T)
+        q_rows, do_rows = (
+            jnp.concatenate(
+                [ref[rows, pl.ds((head * groups + g) * D, D)] for g in range(groups)], 0
+            )
+            for ref in (q_v, do_v)
+        )
+        dv = jnp.dot(pt[b, : 2 * T], do_rows, preferred_element_type=F32)
+        dk = jnp.dot(dst[b, : 2 * T], q_rows, preferred_element_type=F32) * SCALE
+        own_ref[rows, :D] = dk[:T]
+        own_ref[rows, D:] = dv[:T]
+        index = table[b * LINKED + 1]
+        here = row_span(jnp.where(index >= 0, index, blocks))
+        acc[here, :D] += dk[T:]
+        acc[here, D:] += dv[T:]
+    core_ref[...] = acc[:tokens].astype(BF)
+    for b in range(blocks):
+        out_copy(b).wait()
+
+
+def work(microseconds):
+    return pl.CostEstimate(flops=microseconds * 10**9, bytes_accessed=0, transcendentals=0)
 
 
 def linked_body(info, queries, output_gradient, packed):
@@ -468,9 +467,8 @@
     depth = min(PATH_DEPTH_MAX, LINKED)
     core = [(i, i ^ 1) for i in range(LINKED)]
     across = [(i, i ^ 2) for i in range(LINKED)]
+    near = [lax.ppermute(own, "ctx", core) for own in packed]
     far = [lax.ppermute(own, "ctx", across) for own in packed]
-    near = [lax.ppermute(own, "ctx", core) for own in packed]
-    diagonal = [lax.ppermute(x, "ctx", core) for x in far]
 
     vmem = pl.BlockSpec(memory_space=pltpu.VMEM)
     smem = pl.BlockSpec(memory_space=pltpu.SMEM)
@@ -480,44 +478,76 @@
     def keep(x):
         return pltpu.with_memory_space_constraint(x, pltpu.VMEM)
 
-    shared = pl.pallas_call(
-        functools.partial(near_kernel, blocks=blocks, heads=heads, groups=groups, depth=depth),
-        in_specs=[smem] + [hbm] * (2 + 2 * heads),
-        out_specs=[smem, smem] + [vmem] * 9,
-        out_shape=[
-            jax.ShapeDtypeStruct((blocks * LINKED,), jnp.int32),
-            jax.ShapeDtypeStruct((1 + heads,), F32),
+    def near_work(h, local):
+        first = local is None
+        parts = [
+            kept((blocks, 2 * T, D), BF),
+            kept((blocks, D + ONES, 2 * T), BF),
+            kept((blocks, 2 * T, width), BF),
+            kept((blocks, 2 * T, width), F32),
+            kept((blocks, D + 8, width), F32),
+        ]
+        whole = [
             kept(queries.shape, BF),
             kept(queries.shape, BF),
             kept((blocks, D, heads * width), BF),
             kept((blocks, D, heads * width), BF),
-            kept((heads, blocks, 2 * T, D), BF),
-            kept((heads, blocks, D + ONES, 2 * T), BF),
-            kept((heads, blocks, 2 * T, width), BF),
-            kept((heads, blocks, 2 * T, width), F32),
-            kept((heads, blocks, D + 8, width), F32),
-        ],
-        scratch_shapes=[
-            pltpu.VMEM((2 * heads, tokens, 2 * D), BF),
-            pltpu.VMEM((2 * T, D), BF),
-            pltpu.SemaphoreType.DMA((2, blocks)),
-            pltpu.SemaphoreType.DMA((2 * heads,)),
-        ],
-        compiler_params=pltpu.CompilerParams(vmem_limit_bytes=12 * 2**20),
-        name="near",
-    )(info, queries, output_gradient, *packed, *near)
+        ]
+        table_shape = jax.ShapeDtypeStruct((blocks * LINKED,), jnp.int32)
+        if first:
+            wide = pl.BlockSpec(memory_space=pltpu.HBM)
+            operands = [
+                info,
+                pltpu.with_memory_space_constraint(queries, pltpu.HBM),
+                pltpu.with_memory_space_constraint(output_gradient, pltpu.HBM),
+            ]
+            in_specs = [smem, wide, wide]
+            out_specs = [smem, smem] + [vmem] * 9
+            out_shape = [table_shape, jax.ShapeDtypeStruct((2,), F32)] + whole + parts
+        else:
+            operands = [local[0], local[4], local[5]]
+            in_specs = [smem, vmem, vmem]
+            out_specs = [smem] + [vmem] * 5
+            out_shape = [jax.ShapeDtypeStruct((1,), F32)] + parts
+        done = pl.pallas_call(
+            functools.partial(
+                near_kernel, head=h, blocks=blocks, heads=heads, groups=groups, depth=depth
+            ),
+            in_specs=in_specs + [hbm, hbm],
+            out_specs=out_specs,
+            out_shape=out_shape,
+            scratch_shapes=[
+                pltpu.VMEM((2, tokens, 2 * D), BF),
+                pltpu.VMEM((blocks, 2 * T, D), BF),
+                pltpu.SemaphoreType.DMA((2,)),
+            ]
+            + ([pltpu.SemaphoreType.DMA((2, blocks))] if first else []),
+            compiler_params=pltpu.CompilerParams(vmem_limit_bytes=12 * 2**20),
+            cost_estimate=work(4),
+            name="near",
+        )(*operands, packed[h], near[h])
+        return [x if x.ndim == 1 else keep(x) for x in done]
+
+    shared = near_work(0, None)
     table, top = shared[:2]
-    local = [keep(x) for x in shared[2:]]
+    local = shared[2:6]
+    far[0], table = lax.optimization_barrier((far[0], table))
+    diagonal = [lax.ppermute(far[0], "ctx", core)]
+    near_parts = [[top] + shared[6:]]
+    for h in range(1, heads):
+        near_parts.append(near_work(h, [table, None] + local))
+        far[h], near_parts[h][0] = lax.optimization_barrier((far[h], near_parts[h][0]))
+        diagonal.append(lax.ppermute(far[h], "ctx", core))
 
     attended = None
     probs = []
-    far_sums = []
+    far_parts = []
     for h in range(heads):
         chained = attended is not None
-        operands = [table, top, *local, far[h], diagonal[h]]
+        operands = [table, top, near_parts[h][0], *local, *near_parts[h][1:], keep(far[h]), keep(diagonal[h])]
         done = pl.pallas_call(
             functools.partial(far_kernel, head=h, blocks=blocks, groups=groups, chained=chained),
-            in_specs=[smem, smem] + [vmem] * 9 + [hbm] * (3 if chained else 2),
+            in_specs=[smem] * 3 + [vmem] * 11 + [hbm] * (1 if chained else 0),
             out_specs=[hbm] + [vmem] * 5,
             out_shape=[
                 jax.ShapeDtypeStruct(queries.shape, BF),
@@ -529,49 +559,61 @@
             ],
             input_output_aliases={len(operands): 0} if chained else {},
             scratch_shapes=[
-                pltpu.VMEM((2, tokens, 2 * D), BF),
                 pltpu.VMEM((blocks, 2 * T, D), BF),
                 pltpu.VMEM((blocks, D + ONES, 2 * T), BF),
                 pltpu.VMEM((2 * tokens + T, 2 * D), F32),
                 pltpu.VMEM((blocks, T, groups * D), BF),
-                pltpu.SemaphoreType.DMA((2,)),
                 pltpu.SemaphoreType.DMA((blocks,)),
             ],
             compiler_params=pltpu.CompilerParams(vmem_limit_bytes=12 * 2**20),
+            cost_estimate=work(5),
             name="far",
         )(*operands, *([attended] if chained else []))
         attended = done[0]
-        probs += [keep(x) for x in done[1:4]]
-        to_far, to_diagonal = done[4:]
-        onward = lax.ppermute(to_diagonal, "ctx", core)
-        onward = (to_far.astype(F32) + onward.astype(F32)).astype(BF)
-        far_sums.append(lax.ppermute(onward, "ctx", across))
-
-    d_queries, own_sums, to_core = pl.pallas_call(
-        functools.partial(tail_kernel, blocks=blocks, heads=heads, groups=groups),
-        in_specs=[smem] + [vmem] * (2 + 3 * heads),
-        out_specs=[hbm, vmem, vmem],
-        out_shape=[
-            jax.ShapeDtypeStruct(queries.shape, BF),
-            jax.ShapeDtypeStruct((tokens, 2 * heads * D), F32),
-            jax.ShapeDtypeStruct((tokens, 2 * heads * D), BF),
-        ],
-        scratch_shapes=[
-            pltpu.VMEM((tokens + T, 2 * heads * D), F32),
-            pltpu.VMEM((heads, blocks, T, groups * D), BF),
-            pltpu.SemaphoreType.DMA((heads, blocks)),
-        ],
-        compiler_params=pltpu.CompilerParams(vmem_limit_bytes=12 * 2**20),
-        name="tail",
-    )(table, local[0], local[1], *probs)
-    near_sums = own_sums + lax.ppermute(to_core, "ctx", core).astype(F32)
-    d_keys = near_sums[:, : heads * D] + jnp.concatenate(
-        [x[:, :D].astype(F32) for x in far_sums], 1
-    )
-    d_values = near_sums[:, heads * D :] + jnp.concatenate(
-        [x[:, D:].astype(F32) for x in far_sums], 1
-    )
-    return attended, d_queries, d_keys.astype(BF), d_values.astype(BF)
+        probs.append([keep(x) for x in done[1:4]])
+        far_parts.append(done[4:])
+
+    onward = []
+    d_queries = None
+    summed = []
+    for h in range(heads):
+        to_far, to_diagonal = far_parts[h]
+        received = lax.ppermute(to_diagonal, "ctx", core)
+        sums = (to_far.astype(F32) + received.astype(F32)).astype(BF)
+        onward.append(lax.ppermute(sums, "ctx", across))
+        chained = d_queries is not None
+        operands = [table, local[0], local[1], *probs[h]]
+        operands[0], _ = lax.optimization_barrier((table, sums))
+        done = pl.pallas_call(
+            functools.partial(
+                tail_kernel, head=h, blocks=blocks, groups=groups, chained=chained
+            ),
+            in_specs=[smem] + [vmem] * 5 + ([hbm] if chained else []),
+            out_specs=[hbm, vmem, vmem],
+            out_shape=[
+                jax.ShapeDtypeStruct(queries.shape, BF),
+                jax.ShapeDtypeStruct((tokens, 2 * D), F32),
+                jax.ShapeDtypeStruct((tokens, 2 * D), BF),
+            ],
+            input_output_aliases={len(operands): 0} if chained else {},
+            scratch_shapes=[
+                pltpu.VMEM((tokens + T, 2 * D), F32),
+                pltpu.VMEM((blocks, T, groups * D), BF),
+                pltpu.SemaphoreType.DMA((blocks,)),
+            ],
+            compiler_params=pltpu.CompilerParams(vmem_limit_bytes=12 * 2**20),
+            cost_estimate=work(3),
+            name="tail",
+        )(*operands, *([d_queries] if chained else []))
+        d_queries = done[0]
+        summed.append(done[1] + lax.ppermute(done[2], "ctx", core).astype(F32))
+    d_keys = jnp.concatenate(
+        [(x + y.astype(F32))[:, :D] for x, y in zip(summed, onward)], 1
+    ).astype(BF)
+    d_values = jnp.concatenate(
+        [(x + y.astype(F32))[:, D:] for x, y in zip(summed, onward)], 1
+    ).astype(BF)
+    return attended, d_queries, d_keys, d_values
 
 
 def body(queries, key_states, value_tensor, output_gradient, parent, block_owner, shards):

time: 67.3 us -> 54.5 us (0.81)
  waiting for transfers between devices: 17.3 us -> 2.87 us
  local copies, waits for them, and re-layouts: 2.63 us -> 1.11 us
  Pallas kernels: 38.3 us -> 39.6 us
  starting transfers between devices: 7.04 us -> 8.22 us
    ppermute x2, waiting for transfers between devices: 8.34 us -> 0.89 us  [linked_body(): far = [lax.ppermute(own, 'ctx', across) for own in packed]]
    ppermute x7 -> x8, waiting for transfers between devices: 8.9 us -> 1.97 us  [the longest x2 0.99 us: linked_body(): onward.append(lax.ppermute(sums, 'ctx', across))]
    pallas_call x2 -> x4, Pallas kernels: 11.9 us -> 13.7 us  [the longest x2 8.03 us: near_work(): pl.pallas_call(functools.partial(near_kernel, head=h, blocks=blocks, head...]
    unnamed x8 -> x4, local copies, waits for them, and re-layouts: 1.42 us -> 0.01 us
    concatenate x0 -> x2, other arithmetic: none -> 1.4 us  [the longest x1 0.7 us: linked_body(): jnp.concatenate([(x + y.astype(F32))[:, D:] for x, y in zip(summed, onwar...]
    ppermute x7 -> x8, starting transfers between devices: 3.37 us -> 4.61 us  [the longest x2 3.18 us: linked_body(): onward.append(lax.ppermute(sums, 'ctx', across))]
    convert_element_type x3 -> x2, other arithmetic: 0.93 us -> 0.1 us  [linked_body(): sums = (to_far.astype(F32) + received.astype(F32)).astype(BF)]
  transfers between devices with their start and end apart: 11 -> 12, of which waited for: 4 -> 3; matrix products, arithmetic and copies ran while one was open for 0% -> 1% of each run, Pallas kernels for 57% -> 73%
where the time goes in v3:
time: 54.5 us; the launch traced here: 54.4 us
  Pallas kernels  39.6 us (73%)
  starting transfers between devices  8.22 us (15%)
  waiting for transfers between devices  2.87 us (5%)
  other arithmetic  1.75 us (3%)
  local copies, waits for them, and re-layouts  1.11 us (2%)
  between operations  0.77 us (1%)
    pallas_call x2, Pallas kernels, linked_body(): pl.pallas_call(functools.partial(far_kernel, head=h, blocks=blocks, group...  26 us
    pallas_call x2, Pallas kernels, near_work(): pl.pallas_call(functools.partial(near_kernel, head=h, blocks=blocks, head...  8.03 us
    pallas_call x2, Pallas kernels, linked_body(): pl.pallas_call(functools.partial(tail_kernel, head=h, blocks=blocks, grou...  5.65 us
    ppermute x2, starting transfers between devices, linked_body(): onward.append(lax.ppermute(sums, 'ctx', across))  3.18 us
    ppermute x2, starting transfers between devices, linked_body(): far = [lax.ppermute(own, 'ctx', across) for own in packed]  2.86 us
  transfers between devices with their start and end apart: 12, of which 3 were waited for; matrix products, arithmetic and copies ran while one was open for 1% of the time, Pallas kernels for 73%

profile of v3, /device:TPU:0, one launch (start us, length us, event | category | flops | bytes accessed | tf_op | source)
XLA Modules:
  0.0 54.4 jit_solution(11032051100865472306)
XLA Ops:
  0.6 0.0 copy-start
  0.6 0.0 copy-start.1
  0.7 1.1 %fusion.2 = (bf16[384,128]{1,0:T(8,128)(2,1)S(1)}, bf16[384,128]{1,0:T(8,128)(2,1)S(1)}, bf16[384,128]{1,0:T(8,128)(2,1)S(1)}, bf16[384,128]{1,0:T(8,128)(2,1)S(1)}) fusion(bf16[384,256]{1,0:T(8,128)(2,1)} %param.7, bf16[384,256]{1,0:T(8,128)(2,1)} %param.8), kind=kLoop, calls=%fused_computation.11 | loop fusion | bytes 786432 | tf_op jit(solution)/shard_map/slice | solution.py:624
  1.8 0.5 collective-permute-start.1
  2.3 2.6 %collective-permute-start = (bf16[384,256]{1,0:T(8,128)(2,1)S(1)}, bf16[384,256]{1,0:T(8,128)(2,1)S(1)}, u32[]{:S(2)}, u32[]{:S(2)}) collective-permute-start(bf16[384,256]{1,0:T(8,128)(2,1)S(1)} %pad_maximum_fusion.refs_3_), channel_id=1, source_target_pairs={{0,8},{4,12},{8,0},{12,4},{1,9},{5,13},{9,1},{13,5},{2,10},{6,14},... | collective-permute-start | bytes 589832 | tf_op jit(solution)/shard_map/ppermute | solution.py:471
  4.9 0.2 collective-permute-start.3
  5.1 0.3 collective-permute-start.2
  5.4 0.0 copy-done
  5.4 0.0 copy-done.1
  5.4 0.1 pad_add_fusion.refs_0_
  5.5 0.0 collective-permute-done.1.refs_4_
  5.5 5.3 %near.2 = (s32[12]{0:T(128)S(1)}, f32[2]{0:T(128)S(1)}, bf16[384,2048]{1,0:T(8,128)(2,1)S(1)}, bf16[384,2048]{1,0:T(8,128)(2,1)S(1)}, bf16[3,128,2048]{2,1,0:T(8...) custom-call(s32[25]{0:T(128)S(1)} %pad_add_fusion.refs_0_, ...), custom_call_target="tpu_custom_call" | custom-call | flops 4000000000 | tf_op jit(solution)/shard_map/near/pallas_call | solution.py:512
  10.8 0.0 collective-permute-done.refs_12_
  10.8 0.1 collective-permute-start.5
  11.0 0.0 collective-permute-done.3.refs_4_
  11.0 2.7 %near.3 = (f32[1]{0:T(128)}, bf16[3,256,128]{2,1,0:T(8,128)(2,1)S(1)}, bf16[3,144,256]{2,1,0:T(8,128)(2,1)S(1)}, bf16[3,256,1024]{2,1,0:T(8,128)(2,1)S(1)}, f32[...) custom-call(s32[12]{0:T(128)S(1)} %get-tuple-element.76.refs_0_, ...), custom_call_target="tpu_custom_call" | custom-call | flops 4000000000 | tf_op jit(solution)/shard_map/near/pallas_call | solution.py:512
  13.7 0.9 %collective-permute-done.2.refs_12_ = bf16[384,256]{1,0:T(8,128)(2,1)S(1)} collective-permute-done((bf16[384,256]{1,0:T(8,128)(2,1)S(1)}, bf16[384,256]{1,0:T(8,128)(2,1)S(1)}, u32[]{:S(2)}, u32[]{:S(2)}) %collective-permute-start.2) | collective-permute-done | bytes 196640 | tf_op jit(solution)/shard_map/ppermute | solution.py:471
  14.6 0.0 collective-permute-start.4
  14.6 0.0 collective-permute-done.5.refs_13_
  14.6 12.6 %far.2 = (bf16[384,2048]{1,0:T(8,128)(2,1)}, bf16[3,512,1024]{2,1,0:T(8,128)(2,1)S(1)}, bf16[3,512,1024]{2,1,0:T(8,128)(2,1)S(1)}, bf16[3,512,128]{2,1,0:T(8,128...) custom-call(s32[12]{0:T(128)S(1)} %get-tuple-element.76.refs_0_, ...), custom_call_target="tpu_custom_call" | custom-call | flops 5000000000 | tf_op jit(solution)/shard_map/far/pallas_call | solution.py:548
  27.2 0.6 %collective-permute-start.7 = (bf16[384,256]{1,0:T(8,128)(2,1)S(1)}, bf16[384,256]{1,0:T(8,128)(2,1)S(1)}, u32[]{:S(2)}, u32[]{:S(2)}) collective-permute-start(bf16[384,256]{1,0:T(8,128)(2,1)S(1)} %get-tuple-element.75), channel_id=1, source_target_pairs={{0,4},{4,0},{8,12},{12,8},{1,5},{5,1},{9,13},{13,9},{2,6},{6,2},{1... | collective-permute-start | bytes 589832 | tf_op jit(solution)/shard_map/ppermute | solution.py:581
  27.7 0.0 collective-permute-done.4.refs_13_
  27.7 13.4 %far.3 = (bf16[384,2048]{1,0:T(8,128)(2,1)}, bf16[3,512,1024]{2,1,0:T(8,128)(2,1)S(1)}, bf16[3,512,1024]{2,1,0:T(8,128)(2,1)S(1)}, bf16[3,512,128]{2,1,0:T(8,128...) custom-call(s32[12]{0:T(128)S(1)} %get-tuple-element.76.refs_0_, ...), custom_call_target="tpu_custom_call", output_to_operand_aliasing={{0}: (14, {})} | custom-call | flops 5000000000 | tf_op jit(solution)/shard_map/far/pallas_call | solution.py:548
  41.1 0.1 collective-permute-start.6
  41.2 0.0 collective-permute-done.7
  41.2 0.1 add_convert_fusion.2
  41.3 1.8 %collective-permute-start.9 = (bf16[384,256]{1,0:T(8,128)(2,1)S(1)}, bf16[384,256]{1,0:T(8,128)(2,1)S(1)}, u32[]{:S(2)}, u32[]{:S(2)}) collective-permute-start(bf16[384,256]{1,0:T(8,128)(2,1)S(1)} %add_convert_fusion.2), channel_id=1, source_target_pairs={{0,8},{4,12},{8,0},{12,4},{1,9},{5,13},{9,1},{13,5},{2,10},{6,14},... | collective-permute-start | bytes 589832 | tf_op jit(solution)/shard_map/ppermute | solution.py:583
  43.1 0.0 collective-permute-done.6
  43.2 1.4 %collective-permute-start.11 = (bf16[384,256]{1,0:T(8,128)(2,1)S(1)}, bf16[384,256]{1,0:T(8,128)(2,1)S(1)}, u32[]{:S(2)}, u32[]{:S(2)}) collective-permute-start(bf16[384,256]{1,0:T(8,128)(2,1)S(1)} %add_convert_fusion.3), channel_id=1, source_target_pairs={{0,8},{4,12},{8,0},{12,4},{1,9},{5,13},{9,1},{13,5},{2,10},{6,14},... | collective-permute-start | bytes 589832 | tf_op jit(solution)/shard_map/ppermute | solution.py:583
  44.5 2.8 %tail.2 = (bf16[384,2048]{1,0:T(8,128)(2,1)}, f32[384,256]{1,0:T(8,128)S(1)}, bf16[384,256]{1,0:T(8,128)(2,1)S(1)}) custom-call(s32[12]{0:T(128)S(1)} %get-tuple-element.76.refs_0_, bf16[384,2048]{1,0:T(8,128)(2,1)S(1)} %get-tuple-element.52.refs_3_.refs_1_, bf16[384,2048]{1,0:T(8,128)(2,1)S(1)} %get-tuple-element.53.refs_4_.refs_2_, ...), custom_call_target="tpu_custom_call" | custom-call | flops 3000000000 | tf_op jit(solution)/shard_map/tail/pallas_call | solution.py:587
  47.4 0.1 collective-permute-start.8
  47.4 2.8 %tail.3 = (bf16[384,2048]{1,0:T(8,128)(2,1)}, f32[384,256]{1,0:T(8,128)S(1)}, bf16[384,256]{1,0:T(8,128)(2,1)S(1)}) custom-call(s32[12]{0:T(128)S(1)} %get-tuple-element.76.refs_0_, bf16[384,2048]{1,0:T(8,128)(2,1)S(1)} %get-tuple-element.52.refs_3_.refs_1_, ...), custom_call_target="tpu_custom_call", output_to_operand_aliasing={{0}: (6, {})} | custom-call | flops 3000000000 | tf_op jit(solution)/shard_map/tail/pallas_call | solution.py:587
  50.3 0.6 %collective-permute-start.10 = (bf16[384,256]{1,0:T(8,128)(2,1)S(1)}, bf16[384,256]{1,0:T(8,128)(2,1)S(1)}, u32[]{:S(2)}, u32[]{:S(2)}) collective-permute-start(bf16[384,256]{1,0:T(8,128)(2,1)S(1)} %get-tuple-element.85), channel_id=1, source_target_pairs={{0,4},{4,0},{8,12},{12,8},{1,5},{5,1},{9,13},{13,9},{2,6},{6,2},{1... | collective-permute-start | bytes 589832 | tf_op jit(solution)/shard_map/ppermute | solution.py:609
  50.8 0.0 collective-permute-done.8
  50.8 0.0 collective-permute-done.9
  50.8 0.1 add_convert_fusion.1
  50.9 1.0 %collective-permute-done.10 = bf16[384,256]{1,0:T(8,128)(2,1)S(1)} collective-permute-done((bf16[384,256]{1,0:T(8,128)(2,1)S(1)}, bf16[384,256]{1,0:T(8,128)(2,1)S(1)}, u32[]{:S(2)}, u32[]{:S(2)}) %collective-permute-start.10) | collective-permute-done | bytes 196640 | tf_op jit(solution)/shard_map/ppermute | solution.py:609
  51.9 1.0 %collective-permute-done.11 = bf16[384,256]{1,0:T(8,128)(2,1)S(1)} collective-permute-done((bf16[384,256]{1,0:T(8,128)(2,1)S(1)}, bf16[384,256]{1,0:T(8,128)(2,1)S(1)}, u32[]{:S(2)}, u32[]{:S(2)}) %collective-permute-start.11) | collective-permute-done | bytes 196640 | tf_op jit(solution)/shard_map/ppermute | solution.py:583
  52.9 0.1 add_convert_fusion
  53.0 0.7 %pad_maximum_fusion.3 = bf16[384,256]{1,0:T(8,128)(2,1)} fusion(bf16[384,128]{1,0:T(8,128)(2,1)S(1)} %get-tuple-element.88, bf16[384,128]{1,0:T(8,128)(2,1)S(1)} %get-tuple-element.86), kind=kLoop, calls=%fused_computation.7 | loop fusion | flops 393216 | bytes 393216 | tf_op jit(solution)/shard_map/concatenate | solution.py:613
  53.7 0.7 %pad_maximum_fusion.2 = bf16[384,256]{1,0:T(8,128)(2,1)} fusion(bf16[384,128]{1,0:T(8,128)(2,1)S(1)} %get-tuple-element.89, bf16[384,128]{1,0:T(8,128)(2,1)S(1)} %get-tuple-element.87), kind=kLoop, calls=%fused_computation.6 | loop fusion | flops 393216 | bytes 393216 | tf_op jit(solution)/shard_map/concatenate | solution.py:610
  (5 shorter events, 0.1 us)
Async XLA Ops:
  0.6 4.8 %copy-start = (s32[12]{0:T(128)S(1)}, s32[12]{0:T(128)}, u32[]{:S(2)}) copy-start(s32[12]{0:T(128)} %param.11) | copy-start | bytes 148
  0.6 4.8 %copy-start.1 = (s32[12]{0:T(128)S(1)}, s32[12]{0:T(128)}, u32[]{:S(2)}) copy-start(s32[12]{0:T(128)} %param.10) | copy-start | bytes 148
  1.8 3.7 %collective-permute-start.1 = (bf16[384,256]{1,0:T(8,128)(2,1)S(1)}, bf16[384,256]{1,0:T(8,128)(2,1)S(1)}, u32[]{:S(2)}, u32[]{:S(2)}) collective-permute-start(bf16[384,256]{1,0:T(8,128)(2,1)S(1)} %pad_maximum_fusion.refs_3_), channel_id=1, source_target_pairs={{0,4},{4,0},{8,12},{12,8},{1,5},{5,1},{9,13},{13,9},{2,6},{6,2},{1... | collective-permute-start | bytes 589832 | tf_op jit(solution)/shard_map/ppermute | solution.py:470
  2.3 8.5 %collective-permute-start = (bf16[384,256]{1,0:T(8,128)(2,1)S(1)}, bf16[384,256]{1,0:T(8,128)(2,1)S(1)}, u32[]{:S(2)}, u32[]{:S(2)}) collective-permute-start(bf16[384,256]{1,0:T(8,128)(2,1)S(1)} %pad_maximum_fusion.refs_3_), channel_id=1, source_target_pairs={{0,8},{4,12},{8,0},{12,4},{1,9},{5,13},{9,1},{13,5},{2,10},{6,14},... | collective-permute-start | bytes 589832 | tf_op jit(solution)/shard_map/ppermute | solution.py:471
  4.9 6.1 %collective-permute-start.3 = (bf16[384,256]{1,0:T(8,128)(2,1)S(1)}, bf16[384,256]{1,0:T(8,128)(2,1)S(1)}, u32[]{:S(2)}, u32[]{:S(2)}) collective-permute-start(bf16[384,256]{1,0:T(8,128)(2,1)S(1)} %pad_maximum_fusion.1.refs_3_), channel_id=1, source_target_pairs={{0,4},{4,0},{8,12},{12,8},{1,5},{5,1},{9,13},{13,9},{2,6},{6,2},{1... | collective-permute-start | bytes 589832 | tf_op jit(solution)/shard_map/ppermute | solution.py:470
  5.1 9.4 %collective-permute-start.2 = (bf16[384,256]{1,0:T(8,128)(2,1)S(1)}, bf16[384,256]{1,0:T(8,128)(2,1)S(1)}, u32[]{:S(2)}, u32[]{:S(2)}) collective-permute-start(bf16[384,256]{1,0:T(8,128)(2,1)S(1)} %pad_maximum_fusion.1.refs_3_), channel_id=1, source_target_pairs={{0,8},{4,12},{8,0},{12,4},{1,9},{5,13},{9,1},{13,5},{2,10},{6,14},... | collective-permute-start | bytes 589832 | tf_op jit(solution)/shard_map/ppermute | solution.py:471
  10.8 3.8 %collective-permute-start.5 = (bf16[384,256]{1,0:T(8,128)(2,1)S(1)}, bf16[384,256]{1,0:T(8,128)(2,1)S(1)}, u32[]{:S(2)}, u32[]{:S(2)}) collective-permute-start(bf16[384,256]{1,0:T(8,128)(2,1)S(1)} %collective-permute-done.refs_12_), channel_id=1, source_target_pairs={{0,4},{4,0},{8,12},{12,8},{1,5},{5,1},{9,13},{13,9},{2,6},{6,2},{1... | collective-permute-start | bytes 589832 | tf_op jit(solution)/shard_map/ppermute | solution.py:535
  14.6 13.1 %collective-permute-start.4 = (bf16[384,256]{1,0:T(8,128)(2,1)S(1)}, bf16[384,256]{1,0:T(8,128)(2,1)S(1)}, u32[]{:S(2)}, u32[]{:S(2)}) collective-permute-start(bf16[384,256]{1,0:T(8,128)(2,1)S(1)} %collective-permute-done.2.refs_12_), channel_id=1, source_target_pairs={{0,4},{4,0},{8,12},{12,8},{1,5},{5,1},{9,13},{13,9},{2,6},{6,2},{1... | collective-permute-start | bytes 589832 | tf_op jit(solution)/shard_map/ppermute | solution.py:540
  27.2 14.1 %collective-permute-start.7 = (bf16[384,256]{1,0:T(8,128)(2,1)S(1)}, bf16[384,256]{1,0:T(8,128)(2,1)S(1)}, u32[]{:S(2)}, u32[]{:S(2)}) collective-permute-start(bf16[384,256]{1,0:T(8,128)(2,1)S(1)} %get-tuple-element.75), channel_id=1, source_target_pairs={{0,4},{4,0},{8,12},{12,8},{1,5},{5,1},{9,13},{13,9},{2,6},{6,2},{1... | collective-permute-start | bytes 589832 | tf_op jit(solution)/shard_map/ppermute | solution.py:581
  41.1 2.0 %collective-permute-start.6 = (bf16[384,256]{1,0:T(8,128)(2,1)S(1)}, bf16[384,256]{1,0:T(8,128)(2,1)S(1)}, u32[]{:S(2)}, u32[]{:S(2)}) collective-permute-start(bf16[384,256]{1,0:T(8,128)(2,1)S(1)} %get-tuple-element.69), channel_id=1, source_target_pairs={{0,4},{4,0},{8,12},{12,8},{1,5},{5,1},{9,13},{13,9},{2,6},{6,2},{1... | collective-permute-start | bytes 589832 | tf_op jit(solution)/shard_map/ppermute | solution.py:581
  41.3 9.5 %collective-permute-start.9 = (bf16[384,256]{1,0:T(8,128)(2,1)S(1)}, bf16[384,256]{1,0:T(8,128)(2,1)S(1)}, u32[]{:S(2)}, u32[]{:S(2)}) collective-permute-start(bf16[384,256]{1,0:T(8,128)(2,1)S(1)} %add_convert_fusion.2), channel_id=1, source_target_pairs={{0,8},{4,12},{8,0},{12,4},{1,9},{5,13},{9,1},{13,5},{2,10},{6,14},... | collective-permute-start | bytes 589832 | tf_op jit(solution)/shard_map/ppermute | solution.py:583
  43.2 9.7 %collective-permute-start.11 = (bf16[384,256]{1,0:T(8,128)(2,1)S(1)}, bf16[384,256]{1,0:T(8,128)(2,1)S(1)}, u32[]{:S(2)}, u32[]{:S(2)}) collective-permute-start(bf16[384,256]{1,0:T(8,128)(2,1)S(1)} %add_convert_fusion.3), channel_id=1, source_target_pairs={{0,8},{4,12},{8,0},{12,4},{1,9},{5,13},{9,1},{13,5},{2,10},{6,14},... | collective-permute-start | bytes 589832 | tf_op jit(solution)/shard_map/ppermute | solution.py:583
  47.4 3.5 %collective-permute-start.8 = (bf16[384,256]{1,0:T(8,128)(2,1)S(1)}, bf16[384,256]{1,0:T(8,128)(2,1)S(1)}, u32[]{:S(2)}, u32[]{:S(2)}) collective-permute-start(bf16[384,256]{1,0:T(8,128)(2,1)S(1)} %get-tuple-element.83), channel_id=1, source_target_pairs={{0,4},{4,0},{8,12},{12,8},{1,5},{5,1},{9,13},{13,9},{2,6},{6,2},{1... | collective-permute-start | bytes 589832 | tf_op jit(solution)/shard_map/ppermute | solution.py:609
  50.3 1.6 %collective-permute-start.10 = (bf16[384,256]{1,0:T(8,128)(2,1)S(1)}, bf16[384,256]{1,0:T(8,128)(2,1)S(1)}, u32[]{:S(2)}, u32[]{:S(2)}) collective-permute-start(bf16[384,256]{1,0:T(8,128)(2,1)S(1)} %get-tuple-element.85), channel_id=1, source_target_pairs={{0,4},{4,0},{8,12},{12,8},{1,5},{5,1},{9,13},{13,9},{2,6},{6,2},{1... | collective-permute-start | bytes 589832 | tf_op jit(solution)/shard_map/ppermute | solution.py:609

commit v4 on v3

--- a/solution.py
+++ b/solution.py
@@ -187,19 +187,39 @@
 def relation_table(info, table, blocks, depth):
     me = info[0]
     group_blocks = blocks * LINKED
-    for b in range(blocks):
-        for r in range(LINKED):
-            table[b * LINKED + r] = -1
+
+    def walk(block, visit):
         current = jnp.int32(0)
         for t in range(group_blocks):
-            current = jnp.where(info[1 + group_blocks + t] == me * blocks + b, t, current)
+            current = jnp.where(info[1 + group_blocks + t] == block, t, current)
         for d in range(depth):
             if d:
                 current = jnp.where(current >= 0, info[1 + jnp.maximum(current, 0)], -1)
             owner = info[1 + group_blocks + jnp.maximum(current, 0)]
             shard = lax.div(owner, jnp.int32(blocks))
+            visit(current >= 0, shard, owner - shard * blocks)
+
+    for b in range(blocks):
+        for r in range(LINKED):
+            table[b * LINKED + r] = -1
+
+        def visit(live, shard, index):
             slot = b * LINKED + (shard ^ me)
-            table[slot] = jnp.where(current >= 0, owner - shard * blocks, table[slot])
+            table[slot] = jnp.where(live, index, table[slot])
+
+        walk(me * blocks + b, visit)
+    for r in range(2):
+        ends = [jnp.int32(blocks), jnp.int32(-1)]
+
+        def visit(live, shard, index):
+            mine = jnp.logical_and(live, shard == me)
+            ends[0] = jnp.where(mine, jnp.minimum(ends[0], index), ends[0])
+            ends[1] = jnp.where(mine, jnp.maximum(ends[1], index), ends[1])
+
+        for b in range(blocks):
+            walk((me ^ (2 + r)) * blocks + b, visit)
+        for side in range(2):
+            table[blocks * LINKED + 2 * r + side] = ends[side]
 
 
 def row_span(index):
@@ -289,21 +309,20 @@
         on[b, :, col] = jnp.dot(vtn[b], pn[b, :, col], preferred_element_type=F32)[: D + 8]
 
 
-def far_kernel(*refs, head, blocks, groups, chained):
+def far_kernel(*refs, head, blocks, groups, chained, direct):
     table, top, near_top, q_v, do_v, qt, dt, kbn, vtn, pn, dpn, on = refs[:12]
     sources = refs[12:14]
     at = 15 if chained else 14
-    o_out, pt, dst, kb, far_ref, diagonal_ref = refs[at : at + 6]
-    vb, vt, acc, o_buf, out_sem = refs[at + 6 :]
-    tokens = blocks * T
+    o_out, pn_out, dst, kb, stats = refs[at : at + 5]
+    sent = refs[at + 5 : at + (8 if direct else 7)]
+    pt, vb, vt, acc, o_buf, out_sem = refs[at + (8 if direct else 7) :]
     acc[...] = jnp.zeros_like(acc)
     for b in range(blocks):
-        kb[b, : 2 * T, :] = kbn[b]
-    for b in range(blocks):
+        kb[b, :T, :] = kbn[b, T:]
         for r in range(2):
             index = table[b * LINKED + 2 + r]
             here = pl.ds(r * T, T)
-            kb[b, pl.ds((2 + r) * T, T), :] = sources[r][row_span(index), :D] * live_factor(index)
+            kb[b, pl.ds((1 + r) * T, T), :] = sources[r][row_span(index), :D] * live_factor(index)
             values = sources[r][row_span(index), D:] * live_factor(index)
             vb[b, here, :] = values
             vt[b, :D, here] = values.T
@@ -326,28 +345,29 @@
             for j in range(0, groups, WIDE)
         ]
         for b, j, col, head_col in pieces:
-            scores = jnp.dot(kb[b, 2 * T :], qt[b, :, head_col], preferred_element_type=F32)
-            pt[b, 2 * T :, col] = jnp.exp2(scores * (SCALE * LOG2E)).astype(BF)
-        rows_done = []
+            scores = jnp.dot(kb[b, T:], qt[b, :, head_col], preferred_element_type=F32)
+            pt[b, T:, col] = jnp.exp2(scores * (SCALE * LOG2E)).astype(BF)
         for b, j, col, head_col in pieces:
-            sums = jnp.dot(vt[b], pt[b, 2 * T :, col], preferred_element_type=F32)
+            sums = jnp.dot(vt[b], pt[b, T:, col], preferred_element_type=F32)
             sums = sums[: D + 8] + on[b, :, col]
             inverse = 1.0 / sums[D : D + 1]
             out_t = sums[:D] * inverse
             inner = jnp.sum(out_t * dt[b, :, head_col].astype(F32), axis=0, keepdims=True)
-            rows_done.append((inverse, inner))
+            stats[b, :8, col] = jnp.broadcast_to(inverse, (8, WIDE * T))
+            stats[b, 8:, col] = jnp.broadcast_to(inner, (8, WIDE * T))
             for w in range(WIDE):
                 o_buf[b, :, pl.ds((j + w) * D, D)] = out_t[:, w * T : (w + 1) * T].astype(BF).T
             if j + WIDE == groups:
                 out_copy(b).start()
-        for (b, j, col, head_col), (inverse, inner) in zip(pieces, rows_done):
+        for b, j, col, head_col in pieces:
             dprobs = jnp.dot(vb[b], dt[b, :, head_col], preferred_element_type=F32)
-            weights = pn[b, :, col].astype(F32) * inverse
-            pt[b, : 2 * T, col] = weights.astype(BF)
-            dst[b, : 2 * T, col] = (weights * (dpn[b, :, col] - inner)).astype(BF)
-            weights = pt[b, 2 * T :, col].astype(F32) * inverse
-            pt[b, 2 * T :, col] = weights.astype(BF)
-            dst[b, 2 * T :, col] = (weights * (dprobs - inner)).astype(BF)
+            weights = pt[b, T:, col].astype(F32) * stats[b, :1, col]
+            pt[b, T:, col] = weights.astype(BF)
+            dst[b, T:, col] = (weights * (dprobs - stats[b, 8:9, col])).astype(BF)
+        for b, j, col, head_col in pieces:
+            weights = pn[b, T:, col].astype(F32) * stats[b, :1, col]
+            pt[b, :T, col] = weights.astype(BF)
+            dst[b, :T, col] = (weights * (dpn[b, T:, col] - stats[b, 8:9, col])).astype(BF)
 
     @pl.when(jnp.logical_not(safe))
     def _():
@@ -361,11 +381,12 @@
             for g in range(groups):
                 col = pl.ds(g * T, T)
                 head_col = pl.ds((head * groups + g) * D, D)
-                scores = jnp.dot(kb[b], qt[b, :, head_col], preferred_element_type=F32)
+                near_scores = jnp.dot(kbn[b], qt[b, :, head_col], preferred_element_type=F32)
+                scores = jnp.dot(kb[b, T:], qt[b, :, head_col], preferred_element_type=F32)
                 dprobs = jnp.dot(vb[b], dt[b, :, head_col], preferred_element_type=F32)
-                dparts = [dpn[b, pl.ds(r * T, T), col] for r in range(2)]
-                dparts += [dprobs[:T], dprobs[T:]]
-                parts = [scores[r * T : (r + 1) * T] * (SCALE * LOG2E) for r in range(LINKED)]
+                dparts = [dpn[b, :T, col], dpn[b, T:, col], dprobs[:T], dprobs[T:]]
+                parts = [near_scores[:T], near_scores[T:], scores[:T], scores[T:]]
+                parts = [x * (SCALE * LOG2E) for x in parts]
                 parts[0] = jnp.where(tri, parts[0], -jnp.inf)
                 highs = [jnp.max(x, axis=0, keepdims=True) + bias[r] for r, x in enumerate(parts)]
                 high = functools.reduce(jnp.maximum, highs)
@@ -378,84 +399,125 @@
                     jnp.add,
                     [jnp.sum(x * y, axis=0, keepdims=True) for x, y in zip(exps, dparts)],
                 )
-                for r in range(LINKED):
-                    weights = exps[r] * inverse
+                stats[b, :8, col] = jnp.ones((8, T), F32)
+                stats[b, 8:, col] = jnp.broadcast_to(inner, (8, T))
+                pn_out[b, :T, col] = (exps[0] * inverse).astype(BF)
+                pn_out[b, T:, col] = (exps[1] * inverse).astype(BF)
+                for r in range(3):
                     here = pl.ds(r * T, T)
+                    weights = exps[1 + r] * inverse
                     pt[b, here, col] = weights.astype(BF)
-                    dst[b, here, col] = (weights * (dparts[r] - inner)).astype(BF)
+                    dst[b, here, col] = (weights * (dparts[1 + r] - inner)).astype(BF)
                 out_t = jnp.dot(
-                    vtn[b], pt[b, : 2 * T, col], preferred_element_type=F32
-                ) + jnp.dot(vt[b], pt[b, 2 * T :, col], preferred_element_type=F32)
+                    vtn[b], pn_out[b, :, col], preferred_element_type=F32
+                ) + jnp.dot(vt[b], pt[b, T:, col], preferred_element_type=F32)
                 o_buf[b, :, pl.ds(g * D, D)] = out_t[:D].astype(BF).T
             out_copy(b).start()
             return carry
 
         lax.fori_loop(0, blocks, block, 0)
 
-    for b in range(blocks):
-        rows = pl.ds(b * T, T)
-        q_rows, do_rows = (
-            jnp.concatenate(
-                [ref[rows, pl.ds((head * groups + g) * D, D)] for g in range(groups)], 0
-            )
-            for ref in (q_v, do_v)
+    lows = [
+        functools.reduce(
+            jnp.minimum,
+            [
+                jnp.where(table[b * LINKED + r] >= 0, table[b * LINKED + r], blocks)
+                for b in range(blocks)
+            ],
         )
-        dv = jnp.dot(pt[b, 2 * T :], do_rows, preferred_element_type=F32)
-        dk = jnp.dot(dst[b, 2 * T :], q_rows, preferred_element_type=F32) * SCALE
-        for r in range(2):
-            index = table[b * LINKED + 2 + r]
-            here = row_span(jnp.where(index >= 0, index + r * blocks, 2 * blocks))
+        for r in (2, 3)
+    ]
+    slots = 2 if direct else blocks
+    for b in range(blocks):
+        q_rows, do_rows = (stacked(ref, head, b, groups) for ref in (q_v, do_v))
+        dv = jnp.dot(pt[b], do_rows, preferred_element_type=F32)
+        dk = jnp.dot(dst[b], q_rows, preferred_element_type=F32) * SCALE
+        places = [table[b * LINKED + 1 + r] for r in range(3)]
+        for r, index in enumerate(places):
+            slot = index
+            if r:
+                if direct:
+                    slot = jnp.where(index == lows[r - 1], 0, 1)
+                slot = blocks + slot + (r - 1) * slots
+            here = row_span(jnp.where(index >= 0, slot, 3 * blocks))
             acc[here, :D] += dk[r * T : (r + 1) * T]
             acc[here, D:] += dv[r * T : (r + 1) * T]
-    far_ref[...] = acc[:tokens].astype(BF)
-    diagonal_ref[...] = acc[tokens : 2 * tokens].astype(BF)
+    tokens = blocks * T
+    ends = [0, tokens, tokens + slots * T, tokens + 2 * slots * T]
+    if direct:
+        for r in range(3):
+            sent[r][...] = acc[ends[r] : ends[r + 1]].astype(BF)
+    else:
+        sent[0][:tokens] = acc[:tokens].astype(BF)
+        sent[0][tokens:] = acc[ends[2] : ends[3]].astype(BF)
+        sent[1][...] = acc[ends[1] : ends[2]].astype(BF)
     for b in range(blocks):
         out_copy(b).wait()
 
 
+def stacked(ref, head, b, groups):
+    return jnp.concatenate(
+        [ref[pl.ds(b * T, T), pl.ds((head * groups + g) * D, D)] for g in range(groups)], 0
+    )
+
+
 def tail_kernel(*refs, head, blocks, groups, chained):
-    table, q_v, do_v, pt, dst, kb = refs[:6]
-    dq_out, own_ref, core_ref = refs[7:10] if chained else refs[6:9]
-    acc, dq_buf, out_sem = refs[10:] if chained else refs[9:]
-    tokens = blocks * T
+    q_v, do_v, kbn, pn, dpn, dst, kb, stats = refs[:8]
+    at = 9 if chained else 8
+    dq_out, own_ref = refs[at : at + 2]
+    ptn, dsn, dq_buf, out_sem = refs[at + 2 :]
 
     def out_copy(b):
         rows = pl.ds(b * T, T)
         columns = pl.ds(head * groups * D, groups * D)
         return pltpu.make_async_copy(dq_buf.at[b], dq_out.at[rows, columns], out_sem.at[b])
 
-    acc[...] = jnp.zeros_like(acc)
-    for b in range(blocks):
-        for j in range(0, groups, WIDE):
-            dq_t = SCALE * lax.dot_general(
-                kb[b], dst[b, :, pl.ds(j * T, WIDE * T)], TN, preferred_element_type=F32
-            )
-            for w in range(WIDE):
-                dq_buf[b, :, pl.ds((j + w) * D, D)] = dq_t[:, w * T : (w + 1) * T].astype(BF).T
-        out_copy(b).start()
+    pieces = [(b, j, pl.ds(j * T, WIDE * T)) for b in range(blocks) for j in range(0, groups, WIDE)]
+    for b, j, col in pieces:
+        weights = pn[b, :T, col].astype(F32) * stats[b, :1, col]
+        ptn[b, :, col] = weights.astype(BF)
+        dsn[b, :, col] = (weights * (dpn[b, :T, col] - stats[b, 8:9, col])).astype(BF)
+    for b, j, col in pieces:
+        dq_t = lax.dot_general(kbn[b, :T], dsn[b, :, col], TN, preferred_element_type=F32)
+        dq_t += lax.dot_general(kb[b], dst[b, :, col], TN, preferred_element_type=F32)
+        dq_t = dq_t * SCALE
+        for w in range(WIDE):
+            dq_buf[b, :, pl.ds((j + w) * D, D)] = dq_t[:, w * T : (w + 1) * T].astype(BF).T
+        if j + WIDE == groups:
+            out_copy(b).start()
     for b in range(blocks):
         rows = pl.ds(b * T, T)
-        q_rows, do_rows = (
-            jnp.concatenate(
-                [ref[rows, pl.ds((head * groups + g) * D, D)] for g in range(groups)], 0
-            )
-            for ref in (q_v, do_v)
-        )
-        dv = jnp.dot(pt[b, : 2 * T], do_rows, preferred_element_type=F32)
-        dk = jnp.dot(dst[b, : 2 * T], q_rows, preferred_element_type=F32) * SCALE
-        own_ref[rows, :D] = dk[:T]
-        own_ref[rows, D:] = dv[:T]
-        index = table[b * LINKED + 1]
-        here = row_span(jnp.where(index >= 0, index, blocks))
-        acc[here, :D] += dk[T:]
-        acc[here, D:] += dv[T:]
-    core_ref[...] = acc[:tokens].astype(BF)
+        q_rows, do_rows = (stacked(ref, head, b, groups) for ref in (q_v, do_v))
+        own_ref[rows, :D] = jnp.dot(dsn[b], q_rows, preferred_element_type=F32) * SCALE
+        own_ref[rows, D:] = jnp.dot(ptn[b], do_rows, preferred_element_type=F32)
     for b in range(blocks):
         out_copy(b).wait()
 
 
+def finish_kernel(*refs, heads, blocks):
+    table = refs[0]
+    dk_ref, dv_ref, acc = refs[-3:]
+    at = 1
+    tokens = blocks * T
+    for h in range(heads):
+        own, core = refs[at : at + 2]
+        at += 2
+        acc[...] = own[...] + core[:tokens].astype(F32)
+        if h + 1 == heads:
+            acc[...] += refs[at][...].astype(F32)
+            at += 1
+        else:
+            for r in range(2):
+                for side in range(2):
+                    index = jnp.minimum(table[blocks * LINKED + 2 * r + side], blocks - 1)
+                    acc[row_span(index)] += refs[at + r][pl.ds(side * T, T)].astype(F32)
+            at += 2
+        dk_ref[:, pl.ds(h * D, D)] = acc[:, :D].astype(BF)
+        dv_ref[:, pl.ds(h * D, D)] = acc[:, D:].astype(BF)
+
+
 def work(microseconds):
-    return pl.CostEstimate(flops=microseconds * 10**9, bytes_accessed=0, transcendentals=0)
+    return pl.CostEstimate(flops=int(microseconds * 10**9), bytes_accessed=0, transcendentals=0)
 
 
 def linked_body(info, queries, output_gradient, packed):
@@ -467,6 +529,7 @@
     depth = min(PATH_DEPTH_MAX, LINKED)
     core = [(i, i ^ 1) for i in range(LINKED)]
     across = [(i, i ^ 2) for i in range(LINKED)]
+    corner = [(i, i ^ 3) for i in range(LINKED)]
     near = [lax.ppermute(own, "ctx", core) for own in packed]
     far = [lax.ppermute(own, "ctx", across) for own in packed]
 
@@ -477,6 +540,9 @@
 
     def keep(x):
         return pltpu.with_memory_space_constraint(x, pltpu.VMEM)
+
+    def scalars(x):
+        return pltpu.with_memory_space_constraint(x, pltpu.SMEM)
 
     def near_work(h, local):
         first = local is None
@@ -493,7 +559,7 @@
             kept((blocks, D, heads * width), BF),
             kept((blocks, D, heads * width), BF),
         ]
-        table_shape = jax.ShapeDtypeStruct((blocks * LINKED,), jnp.int32)
+        table_shape = pltpu.SMEM((blocks * LINKED + 4,), jnp.int32)
         if first:
             wide = pl.BlockSpec(memory_space=pltpu.HBM)
             operands = [
@@ -503,12 +569,12 @@
             ]
             in_specs = [smem, wide, wide]
             out_specs = [smem, smem] + [vmem] * 9
-            out_shape = [table_shape, jax.ShapeDtypeStruct((2,), F32)] + whole + parts
+            out_shape = [table_shape, pltpu.SMEM((2,), F32)] + whole + parts
         else:
             operands = [local[0], local[4], local[5]]
             in_specs = [smem, vmem, vmem]
             out_specs = [smem] + [vmem] * 5
-            out_shape = [jax.ShapeDtypeStruct((1,), F32)] + parts
+            out_shape = [pltpu.SMEM((1,), F32)] + parts
         done = pl.pallas_call(
             functools.partial(
                 near_kernel, head=h, blocks=blocks, heads=heads, groups=groups, depth=depth
@@ -526,42 +592,51 @@
             cost_estimate=work(4),
             name="near",
         )(*operands, packed[h], near[h])
-        return [x if x.ndim == 1 else keep(x) for x in done]
+        return [scalars(x) if x.ndim == 1 else keep(x) for x in done]
 
     shared = near_work(0, None)
     table, top = shared[:2]
     local = shared[2:6]
-    far[0], table = lax.optimization_barrier((far[0], table))
+    far[0], _ = lax.optimization_barrier((far[0], shared[10]))
     diagonal = [lax.ppermute(far[0], "ctx", core)]
     near_parts = [[top] + shared[6:]]
     for h in range(1, heads):
         near_parts.append(near_work(h, [table, None] + local))
-        far[h], near_parts[h][0] = lax.optimization_barrier((far[h], near_parts[h][0]))
+        far[h], _ = lax.optimization_barrier((far[h], near_parts[h][5]))
         diagonal.append(lax.ppermute(far[h], "ctx", core))
 
     attended = None
     probs = []
-    far_parts = []
+    arrivals = []
     for h in range(heads):
         chained = attended is not None
-        operands = [table, top, near_parts[h][0], *local, *near_parts[h][1:], keep(far[h]), keep(diagonal[h])]
+        direct = h + 1 < heads
+        if direct:
+            sent = [tokens, 2 * T, 2 * T]
+        else:
+            sent = [2 * tokens, tokens]
+        operands = [table, top, near_parts[h][0], *local, *near_parts[h][1:]]
+        operands += [keep(far[h]), keep(diagonal[h])]
         done = pl.pallas_call(
-            functools.partial(far_kernel, head=h, blocks=blocks, groups=groups, chained=chained),
+            functools.partial(
+                far_kernel, head=h, blocks=blocks, groups=groups, chained=chained, direct=direct
+            ),
             in_specs=[smem] * 3 + [vmem] * 11 + [hbm] * (1 if chained else 0),
-            out_specs=[hbm] + [vmem] * 5,
+            out_specs=[hbm] + [vmem] * (4 + len(sent)),
             out_shape=[
                 jax.ShapeDtypeStruct(queries.shape, BF),
-                kept((blocks, LINKED * T, width), BF),
-                kept((blocks, LINKED * T, width), BF),
-                kept((blocks, LINKED * T, D), BF),
-                jax.ShapeDtypeStruct((tokens, 2 * D), BF),
-                jax.ShapeDtypeStruct((tokens, 2 * D), BF),
-            ],
-            input_output_aliases={len(operands): 0} if chained else {},
+                kept((blocks, 2 * T, width), BF),
+                kept((blocks, 3 * T, width), BF),
+                kept((blocks, 3 * T, D), BF),
+                kept((blocks, 16, width), F32),
+            ]
+            + [kept((rows, 2 * D), BF) for rows in sent],
+            input_output_aliases={9: 1} | ({len(operands): 0} if chained else {}),
             scratch_shapes=[
+                pltpu.VMEM((blocks, 3 * T, width), BF),
                 pltpu.VMEM((blocks, 2 * T, D), BF),
                 pltpu.VMEM((blocks, D + ONES, 2 * T), BF),
-                pltpu.VMEM((2 * tokens + T, 2 * D), F32),
+                pltpu.VMEM((3 * tokens + T, 2 * D), F32),
                 pltpu.VMEM((blocks, T, groups * D), BF),
                 pltpu.SemaphoreType.DMA((blocks,)),
             ],
@@ -570,49 +645,60 @@
             name="far",
         )(*operands, *([attended] if chained else []))
         attended = done[0]
-        probs.append([keep(x) for x in done[1:4]])
-        far_parts.append(done[4:])
-
-    onward = []
+        near_probs, *rest = [keep(x) for x in done[1:5]]
+        _, kbn, _, _, dpn, _ = near_parts[h]
+        probs.append([kbn, near_probs, dpn, *rest])
+        if direct:
+            to_core, to_far, to_corner = done[5:]
+            arrivals.append(
+                [
+                    lax.ppermute(to_core, "ctx", core),
+                    lax.ppermute(to_far, "ctx", across),
+                    lax.ppermute(to_corner, "ctx", corner),
+                ]
+            )
+        else:
+            to_core, to_far = done[5:]
+            if arrivals:
+                to_core, arrivals[-1] = lax.optimization_barrier((to_core, arrivals[-1]))
+            received = lax.ppermute(to_core, "ctx", core)
+            sums = (to_far.astype(F32) + received[tokens:].astype(F32)).astype(BF)
+            arrivals.append([received, lax.ppermute(sums, "ctx", across)])
+
     d_queries = None
-    summed = []
+    finishing = [table]
     for h in range(heads):
-        to_far, to_diagonal = far_parts[h]
-        received = lax.ppermute(to_diagonal, "ctx", core)
-        sums = (to_far.astype(F32) + received.astype(F32)).astype(BF)
-        onward.append(lax.ppermute(sums, "ctx", across))
         chained = d_queries is not None
-        operands = [table, local[0], local[1], *probs[h]]
-        operands[0], _ = lax.optimization_barrier((table, sums))
+        operands = [local[0], local[1], *probs[h]]
+        if not chained:
+            operands[-1], _ = lax.optimization_barrier((operands[-1], sums))
+            operands[-1] = keep(operands[-1])
         done = pl.pallas_call(
-            functools.partial(
-                tail_kernel, head=h, blocks=blocks, groups=groups, chained=chained
-            ),
-            in_specs=[smem] + [vmem] * 5 + ([hbm] if chained else []),
-            out_specs=[hbm, vmem, vmem],
-            out_shape=[
-                jax.ShapeDtypeStruct(queries.shape, BF),
-                jax.ShapeDtypeStruct((tokens, 2 * D), F32),
-                jax.ShapeDtypeStruct((tokens, 2 * D), BF),
-            ],
+            functools.partial(tail_kernel, head=h, blocks=blocks, groups=groups, chained=chained),
+            in_specs=[vmem] * 8 + ([hbm] if chained else []),
+            out_specs=[hbm, vmem],
+            out_shape=[jax.ShapeDtypeStruct(queries.shape, BF), kept((tokens, 2 * D), F32)],
             input_output_aliases={len(operands): 0} if chained else {},
             scratch_shapes=[
-                pltpu.VMEM((tokens + T, 2 * D), F32),
+                pltpu.VMEM((blocks, T, width), BF),
+                pltpu.VMEM((blocks, T, width), BF),
                 pltpu.VMEM((blocks, T, groups * D), BF),
                 pltpu.SemaphoreType.DMA((blocks,)),
             ],
             compiler_params=pltpu.CompilerParams(vmem_limit_bytes=12 * 2**20),
-            cost_estimate=work(3),
+            cost_estimate=work(0.3),
             name="tail",
         )(*operands, *([d_queries] if chained else []))
         d_queries = done[0]
-        summed.append(done[1] + lax.ppermute(done[2], "ctx", core).astype(F32))
-    d_keys = jnp.concatenate(
-        [(x + y.astype(F32))[:, :D] for x, y in zip(summed, onward)], 1
-    ).astype(BF)
-    d_values = jnp.concatenate(
-        [(x + y.astype(F32))[:, D:] for x, y in zip(summed, onward)], 1
-    ).astype(BF)
+        finishing += [keep(done[1])] + [keep(x) for x in arrivals[h]]
+    d_keys, d_values = pl.pallas_call(
+        functools.partial(finish_kernel, heads=heads, blocks=blocks),
+        in_specs=[smem] + [vmem] * (len(finishing) - 1),
+        out_specs=[vmem, vmem],
+        out_shape=[jax.ShapeDtypeStruct((tokens, heads * D), BF)] * 2,
+        scratch_shapes=[pltpu.VMEM((tokens, 2 * D), F32)],
+        name="finish",
+    )(*finishing)
     return attended, d_queries, d_keys, d_values
 
 

time: 54.5 us -> 49.2 us (0.903)
  Pallas kernels: 39.6 us -> 34.6 us
  other arithmetic: 1.75 us -> 0.18 us
  waiting for transfers between devices: 2.87 us -> 4.09 us
    pallas_call x2, Pallas kernels: 26 us -> 22.9 us  [linked_body(): pl.pallas_call(functools.partial(far_kernel, head=h, blocks=blocks, group...]
    pallas_call x2, Pallas kernels: 8.03 us -> 6.6 us  [near_work(): pl.pallas_call(functools.partial(near_kernel, head=h, blocks=blocks, head...]
    pallas_call x2, Pallas kernels: 5.65 us -> 4.22 us  [linked_body(): pl.pallas_call(functools.partial(tail_kernel, head=h, blocks=blocks, grou...]
    concatenate x2 -> x0, other arithmetic: 1.4 us -> none  [the longest x1 0.7 us: linked_body(): jnp.concatenate([(x + y.astype(F32))[:, D:] for x, y in zip(summed, onwar...]
    pallas_call x0 -> x1, Pallas kernels: none -> 0.95 us  [linked_body(): pl.pallas_call(functools.partial(finish_kernel, heads=heads, blocks=block...]
    ppermute x2, waiting for transfers between devices: 0.01 us -> 0.68 us  [linked_body(): near = [lax.ppermute(own, 'ctx', core) for own in packed]]
    ppermute x6 -> x5, waiting for transfers between devices: 1.97 us -> 2.56 us  [the longest x1 1.43 us: linked_body(): received = lax.ppermute(to_core, 'ctx', core)]
    ppermute x6 -> x5, starting transfers between devices: 4.47 us -> 4.37 us  [the longest x1 1.82 us: linked_body(): lax.ppermute(to_far, 'ctx', across)]
  transfers between devices with their start and end apart: 12 -> 11, of which waited for: 3 -> 4; matrix products, arithmetic and copies ran while one was open for 1% -> 0% of each run, Pallas kernels for 73% -> 69%
where the time goes in v4:
time: 49.2 us; the launch traced here: 49 us
  Pallas kernels  34.6 us (70%)
  starting transfers between devices  8.27 us (17%)
  waiting for transfers between devices  4.09 us (8%)
  local copies, waits for them, and re-layouts  1.08 us (2%)
  between operations  0.76 us (2%)
    pallas_call x2, Pallas kernels, linked_body(): pl.pallas_call(functools.partial(far_kernel, head=h, blocks=blocks, group...  22.9 us
    pallas_call x2, Pallas kernels, near_work(): pl.pallas_call(functools.partial(near_kernel, head=h, blocks=blocks, head...  6.6 us
    pallas_call x2, Pallas kernels, linked_body(): pl.pallas_call(functools.partial(tail_kernel, head=h, blocks=blocks, grou...  4.22 us
    ppermute x2, starting transfers between devices, linked_body(): far = [lax.ppermute(own, 'ctx', across) for own in packed]  3.19 us
    ppermute x1, starting transfers between devices, linked_body(): lax.ppermute(to_far, 'ctx', across)  1.82 us
    ppermute x1, starting transfers between devices, linked_body(): arrivals.append([received, lax.ppermute(sums, 'ctx', across)])  1.81 us
    ppermute x1, waiting for transfers between devices, linked_body(): received = lax.ppermute(to_core, 'ctx', core)  1.43 us
    ppermute x1, waiting for transfers between devices, linked_body(): arrivals.append([received, lax.ppermute(sums, 'ctx', across)])  1.12 us
  transfers between devices with their start and end apart: 11, of which 4 were waited for; matrix products, arithmetic and copies ran while one was open for 0% of the time, Pallas kernels for 69%

profile of v4, /device:TPU:0, one launch (start us, length us, event | category | flops | bytes accessed | tf_op | source)
XLA Modules:
  0.0 49.0 jit_solution(13172584057969075748)
XLA Ops:
  0.6 0.0 copy-start
  0.6 0.0 copy-start.1
  0.7 1.1 %fusion = (bf16[384,128]{1,0:T(8,128)(2,1)S(1)}, bf16[384,128]{1,0:T(8,128)(2,1)S(1)}, bf16[384,128]{1,0:T(8,128)(2,1)S(1)}, bf16[384,128]{1,0:T(8,128)(2,1)S(1)}) fusion(bf16[384,256]{1,0:T(8,128)(2,1)} %param.7, bf16[384,256]{1,0:T(8,128)(2,1)} %param.8), kind=kLoop, calls=%fused_computation.4 | loop fusion | bytes 786432 | tf_op jit(solution)/shard_map/slice | solution.py:710
  1.8 3.0 %collective-permute-start.4 = (bf16[384,256]{1,0:T(8,128)(2,1)S(1)}, bf16[384,256]{1,0:T(8,128)(2,1)S(1)}, u32[]{:S(2)}, u32[]{:S(2)}) collective-permute-start(bf16[384,256]{1,0:T(8,128)(2,1)S(1)} %pad_maximum_fusion.refs_3_), channel_id=1, source_target_pairs={{0,8},{4,12},{8,0},{12,4},{1,9},{5,13},{9,1},{13,5},{2,10},{6,14},... | collective-permute-start | bytes 589832 | tf_op jit(solution)/shard_map/ppermute | solution.py:534
  4.8 0.0 collective-permute-start
  4.8 0.2 collective-permute-start.2
  5.0 0.5 %collective-permute-start.1 = (bf16[384,256]{1,0:T(8,128)(2,1)S(1)}, bf16[384,256]{1,0:T(8,128)(2,1)S(1)}, u32[]{:S(2)}, u32[]{:S(2)}) collective-permute-start(bf16[384,256]{1,0:T(8,128)(2,1)S(1)} %pad_maximum_fusion.1.refs_3_), channel_id=1, source_target_pairs={{0,4},{4,0},{8,12},{12,8},{1,5},{5,1},{9,13},{13,9},{2,6},{6,2},{1... | collective-permute-start | bytes 589832 | tf_op jit(solution)/shard_map/ppermute | solution.py:533
  5.5 0.0 copy-done
  5.5 0.0 copy-done.1
  5.5 0.1 pad_add_fusion.refs_0_
  5.6 0.7 %collective-permute-done.refs_4_ = bf16[384,256]{1,0:T(8,128)(2,1)S(1)} collective-permute-done((bf16[384,256]{1,0:T(8,128)(2,1)S(1)}, bf16[384,256]{1,0:T(8,128)(2,1)S(1)}, u32[]{:S(2)}, u32[]{:S(2)}) %collective-permute-start) | collective-permute-done | bytes 196640 | tf_op jit(solution)/shard_map/ppermute | solution.py:533
  6.2 4.9 %near.2 = (s32[16]{0:T(128)S(4)}, f32[2]{0:T(128)S(4)}, bf16[384,2048]{1,0:T(8,128)(2,1)S(1)}, bf16[384,2048]{1,0:T(8,128)(2,1)S(1)}, bf16[3,128,2048]{2,1,0:T(8...) custom-call(s32[25]{0:T(128)S(1)} %pad_add_fusion.refs_0_, ...), custom_call_target="tpu_custom_call" | custom-call | flops 4000000000 | tf_op jit(solution)/shard_map/near/pallas_call | solution.py:578
  11.1 0.0 collective-permute-done.4.refs_12_
  11.1 0.2 collective-permute-start.5
  11.3 0.0 collective-permute-done.1.refs_4_
  11.3 1.7 %near.3 = (f32[1]{0:T(128)S(4)}, bf16[3,256,128]{2,1,0:T(8,128)(2,1)S(1)}, bf16[3,144,256]{2,1,0:T(8,128)(2,1)S(1)}, bf16[3,256,1024]{2,1,0:T(8,128)(2,1)S(1)}, ...) custom-call(s32[16]{0:T(128)S(4)} %get-tuple-element.49.refs_0_, ...), custom_call_target="tpu_custom_call" | custom-call | flops 4000000000 | tf_op jit(solution)/shard_map/near/pallas_call | solution.py:578
  13.1 0.8 %collective-permute-done.2.refs_12_ = bf16[384,256]{1,0:T(8,128)(2,1)S(1)} collective-permute-done((bf16[384,256]{1,0:T(8,128)(2,1)S(1)}, bf16[384,256]{1,0:T(8,128)(2,1)S(1)}, u32[]{:S(2)}, u32[]{:S(2)}) %collective-permute-start.2) | collective-permute-done | bytes 196640 | tf_op jit(solution)/shard_map/ppermute | solution.py:534
  13.9 0.0 collective-permute-start.3
  13.9 0.0 collective-permute-done.5.refs_13_
  13.9 11.4 %far.2 = (bf16[384,2048]{1,0:T(8,128)(2,1)}, bf16[3,256,1024]{2,1,0:T(8,128)(2,1)S(1)}, bf16[3,384,1024]{2,1,0:T(8,128)(2,1)S(1)}, bf16[3,384,128]{2,1,0:T(8,128...) custom-call(s32[16]{0:T(128)S(4)} %get-tuple-element.49.refs_0_, ...), custom_call_target="tpu_custom_call", output_to_operand_aliasing={{1}: (9, {})} | custom-call | flops 5000000000 | tf_op jit(solution)/shard_map/far/pallas_call | solution.py:620
  25.3 1.8 %collective-permute-start.7 = (bf16[256,256]{1,0:T(8,128)(2,1)S(1)}, bf16[256,256]{1,0:T(8,128)(2,1)S(1)}, u32[]{:S(2)}, u32[]{:S(2)}) collective-permute-start(bf16[256,256]{1,0:T(8,128)(2,1)S(1)} %get-tuple-element.81), channel_id=1, source_target_pairs={{0,8},{4,12},{8,0},{12,4},{1,9},{5,13},{9,1},{13,5},{2,10},{6,14},... | collective-permute-start | bytes 393224 | tf_op jit(solution)/shard_map/ppermute | solution.py:656
  27.1 0.2 collective-permute-start.8
  27.3 0.2 collective-permute-start.6
  27.5 0.0 collective-permute-done.3.refs_13_
  27.5 11.5 %far.3 = (bf16[384,2048]{1,0:T(8,128)(2,1)}, bf16[3,256,1024]{2,1,0:T(8,128)(2,1)S(1)}, bf16[3,384,1024]{2,1,0:T(8,128)(2,1)S(1)}, bf16[3,384,128]{2,1,0:T(8,128...) custom-call(s32[16]{0:T(128)S(4)} %get-tuple-element.49.refs_0_, ...), custom_call_target="tpu_custom_call", output_to_operand_aliasing={{1}: (9, {}), {0}: (14, {})} | custom-call | flops 5000000000 | tf_op jit(solution)/shard_map/far/pallas_call | solution.py:620
  39.0 0.0 collective-permute-done.7.refs_3_
  39.0 0.0 collective-permute-done.8.refs_4_
  39.0 0.0 collective-permute-done.6.refs_2_
  39.0 0.4 collective-permute-start.9
  39.4 1.4 %collective-permute-done.9.refs_6_ = bf16[768,256]{1,0:T(8,128)(2,1)S(1)} collective-permute-done((bf16[768,256]{1,0:T(8,128)(2,1)S(1)}, bf16[768,256]{1,0:T(8,128)(2,1)S(1)}, u32[]{:S(2)}, u32[]{:S(2)}) %collective-permute-start.9) | collective-permute-done | bytes 393248 | tf_op jit(solution)/shard_map/ppermute | solution.py:664
  40.8 0.1 add_convert_fusion
  40.9 1.8 %collective-permute-start.10 = (bf16[384,256]{1,0:T(8,128)(2,1)S(1)}, bf16[384,256]{1,0:T(8,128)(2,1)S(1)}, u32[]{:S(2)}, u32[]{:S(2)}) collective-permute-start(bf16[384,256]{1,0:T(8,128)(2,1)S(1)} %add_convert_fusion), channel_id=1, source_target_pairs={{0,8},{4,12},{8,0},{12,4},{1,9},{5,13},{9,1},{13,5},{2,10},{6,14},... | collective-permute-start | bytes 589832 | tf_op jit(solution)/shard_map/ppermute | solution.py:666
  42.7 2.1 %tail.2 = (bf16[384,2048]{1,0:T(8,128)(2,1)}, f32[384,256]{1,0:T(8,128)S(1)}) custom-call(bf16[384,2048]{1,0:T(8,128)(2,1)S(1)} %get-tuple-element.54.refs_3_.refs_0_, bf16[384,2048]{1,0:T(8,128)(2,1)S(1)} %get-tuple-element.55.refs_4_.refs_1_, bf16[3,256,128]{2,1,0:T(8,128)(2,1)S(1)} %get-tuple-element.62.refs_7_.refs_2_, ...), custom_call_target="tpu_custom_call" | custom-call | flops 300000000 | tf_op jit(solution)/shard_map/tail/pallas_call | solution.py:676
  44.8 2.1 %tail.3 = (bf16[384,2048]{1,0:T(8,128)(2,1)}, f32[384,256]{1,0:T(8,128)S(1)}) custom-call(bf16[384,2048]{1,0:T(8,128)(2,1)S(1)} %get-tuple-element.54.refs_3_.refs_0_, bf16[384,2048]{1,0:T(8,128)(2,1)S(1)} %get-tuple-element.55.refs_4_.refs_1_, bf16[3,256,128]{2,1,0:T(8,128)(2,1)S(1)} %get-tuple-element.56.refs_7_.refs_2_, ...), custom_call_target="tpu_custom_call", output_to_operand_aliasing={{0}: (8, {})} | custom-call | flops 300000000 | tf_op jit(solution)/shard_map/tail/pallas_call | solution.py:676
  46.9 1.1 %collective-permute-done.10.refs_7_ = bf16[384,256]{1,0:T(8,128)(2,1)S(1)} collective-permute-done((bf16[384,256]{1,0:T(8,128)(2,1)S(1)}, bf16[384,256]{1,0:T(8,128)(2,1)S(1)}, u32[]{:S(2)}, u32[]{:S(2)}) %collective-permute-start.10) | collective-permute-done | bytes 196640 | tf_op jit(solution)/shard_map/ppermute | solution.py:666
  48.0 0.9 %finish.1 = (bf16[384,256]{1,0:T(8,128)(2,1)}, bf16[384,256]{1,0:T(8,128)(2,1)}) custom-call(s32[16]{0:T(128)S(4)} %get-tuple-element.49.refs_0_, f32[384,256]{1,0:T(8,128)S(1)} %get-tuple-element.87.refs_1_, bf16[384,256]{1,0:T(8,128)(2,1)S(1)} %collective-permute-done.6.refs_2_, bf16[256,256]{1,0:T(8,128)(2,1)S(1)} %collective-permute-done.7.refs_3_, ...), custom_call_target="tpu_custom_call" | custom-call | tf_op jit(solution)/shard_map/finish/pallas_call | solution.py:694
  (2 shorter events, 0.0 us)
Async XLA Ops:
  0.6 4.8 %copy-start = (s32[12]{0:T(128)S(1)}, s32[12]{0:T(128)}, u32[]{:S(2)}) copy-start(s32[12]{0:T(128)} %param.11) | copy-start | bytes 148
  0.6 4.8 %copy-start.1 = (s32[12]{0:T(128)S(1)}, s32[12]{0:T(128)}, u32[]{:S(2)}) copy-start(s32[12]{0:T(128)} %param.10) | copy-start | bytes 148
  1.8 9.3 %collective-permute-start.4 = (bf16[384,256]{1,0:T(8,128)(2,1)S(1)}, bf16[384,256]{1,0:T(8,128)(2,1)S(1)}, u32[]{:S(2)}, u32[]{:S(2)}) collective-permute-start(bf16[384,256]{1,0:T(8,128)(2,1)S(1)} %pad_maximum_fusion.refs_3_), channel_id=1, source_target_pairs={{0,8},{4,12},{8,0},{12,4},{1,9},{5,13},{9,1},{13,5},{2,10},{6,14},... | collective-permute-start | bytes 589832 | tf_op jit(solution)/shard_map/ppermute | solution.py:534
  4.8 1.4 %collective-permute-start = (bf16[384,256]{1,0:T(8,128)(2,1)S(1)}, bf16[384,256]{1,0:T(8,128)(2,1)S(1)}, u32[]{:S(2)}, u32[]{:S(2)}) collective-permute-start(bf16[384,256]{1,0:T(8,128)(2,1)S(1)} %pad_maximum_fusion.refs_3_), channel_id=1, source_target_pairs={{0,4},{4,0},{8,12},{12,8},{1,5},{5,1},{9,13},{13,9},{2,6},{6,2},{1... | collective-permute-start | bytes 589832 | tf_op jit(solution)/shard_map/ppermute | solution.py:533
  4.8 9.1 %collective-permute-start.2 = (bf16[384,256]{1,0:T(8,128)(2,1)S(1)}, bf16[384,256]{1,0:T(8,128)(2,1)S(1)}, u32[]{:S(2)}, u32[]{:S(2)}) collective-permute-start(bf16[384,256]{1,0:T(8,128)(2,1)S(1)} %pad_maximum_fusion.1.refs_3_), channel_id=1, source_target_pairs={{0,8},{4,12},{8,0},{12,4},{1,9},{5,13},{9,1},{13,5},{2,10},{6,14},... | collective-permute-start | bytes 589832 | tf_op jit(solution)/shard_map/ppermute | solution.py:534
  5.0 6.3 %collective-permute-start.1 = (bf16[384,256]{1,0:T(8,128)(2,1)S(1)}, bf16[384,256]{1,0:T(8,128)(2,1)S(1)}, u32[]{:S(2)}, u32[]{:S(2)}) collective-permute-start(bf16[384,256]{1,0:T(8,128)(2,1)S(1)} %pad_maximum_fusion.1.refs_3_), channel_id=1, source_target_pairs={{0,4},{4,0},{8,12},{12,8},{1,5},{5,1},{9,13},{13,9},{2,6},{6,2},{1... | collective-permute-start | bytes 589832 | tf_op jit(solution)/shard_map/ppermute | solution.py:533
  11.1 2.8 %collective-permute-start.5 = (bf16[384,256]{1,0:T(8,128)(2,1)S(1)}, bf16[384,256]{1,0:T(8,128)(2,1)S(1)}, u32[]{:S(2)}, u32[]{:S(2)}) collective-permute-start(bf16[384,256]{1,0:T(8,128)(2,1)S(1)} %collective-permute-done.4.refs_12_), channel_id=1, source_target_pairs={{0,4},{4,0},{8,12},{12,8},{1,5},{5,1},{9,13},{13,9},{2,6},{6,2},{1... | collective-permute-start | bytes 589832 | tf_op jit(solution)/shard_map/ppermute | solution.py:601
  13.9 13.6 %collective-permute-start.3 = (bf16[384,256]{1,0:T(8,128)(2,1)S(1)}, bf16[384,256]{1,0:T(8,128)(2,1)S(1)}, u32[]{:S(2)}, u32[]{:S(2)}) collective-permute-start(bf16[384,256]{1,0:T(8,128)(2,1)S(1)} %collective-permute-done.2.refs_12_), channel_id=1, source_target_pairs={{0,4},{4,0},{8,12},{12,8},{1,5},{5,1},{9,13},{13,9},{2,6},{6,2},{1... | collective-permute-start | bytes 589832 | tf_op jit(solution)/shard_map/ppermute | solution.py:606
  25.3 13.7 %collective-permute-start.7 = (bf16[256,256]{1,0:T(8,128)(2,1)S(1)}, bf16[256,256]{1,0:T(8,128)(2,1)S(1)}, u32[]{:S(2)}, u32[]{:S(2)}) collective-permute-start(bf16[256,256]{1,0:T(8,128)(2,1)S(1)} %get-tuple-element.81), channel_id=1, source_target_pairs={{0,8},{4,12},{8,0},{12,4},{1,9},{5,13},{9,1},{13,5},{2,10},{6,14},... | collective-permute-start | bytes 393224 | tf_op jit(solution)/shard_map/ppermute | solution.py:656
  27.1 11.9 %collective-permute-start.8 = (bf16[256,256]{1,0:T(8,128)(2,1)S(1)}, bf16[256,256]{1,0:T(8,128)(2,1)S(1)}, u32[]{:S(2)}, u32[]{:S(2)}) collective-permute-start(bf16[256,256]{1,0:T(8,128)(2,1)S(1)} %get-tuple-element.82), channel_id=1, source_target_pairs={{0,12},{4,8},{8,4},{12,0},{1,13},{5,9},{9,5},{13,1},{2,14},{6,10},... | collective-permute-start | bytes 393224 | tf_op jit(solution)/shard_map/ppermute | solution.py:657
  27.3 11.8 %collective-permute-start.6 = (bf16[384,256]{1,0:T(8,128)(2,1)S(1)}, bf16[384,256]{1,0:T(8,128)(2,1)S(1)}, u32[]{:S(2)}, u32[]{:S(2)}) collective-permute-start(bf16[384,256]{1,0:T(8,128)(2,1)S(1)} %get-tuple-element.80), channel_id=1, source_target_pairs={{0,4},{4,0},{8,12},{12,8},{1,5},{5,1},{9,13},{13,9},{2,6},{6,2},{1... | collective-permute-start | bytes 589832 | tf_op jit(solution)/shard_map/ppermute | solution.py:655
  39.0 1.8 %collective-permute-start.9 = (bf16[768,256]{1,0:T(8,128)(2,1)S(1)}, bf16[768,256]{1,0:T(8,128)(2,1)S(1)}, u32[]{:S(2)}, u32[]{:S(2)}) collective-permute-start(bf16[768,256]{1,0:T(8,128)(2,1)S(1)} %get-tuple-element.83), channel_id=1, source_target_pairs={{0,4},{4,0},{8,12},{12,8},{1,5},{5,1},{9,13},{13,9},{2,6},{6,2},{1... | collective-permute-start | bytes 1179656 | tf_op jit(solution)/shard_map/ppermute | solution.py:664
  40.9 7.2 %collective-permute-start.10 = (bf16[384,256]{1,0:T(8,128)(2,1)S(1)}, bf16[384,256]{1,0:T(8,128)(2,1)S(1)}, u32[]{:S(2)}, u32[]{:S(2)}) collective-permute-start(bf16[384,256]{1,0:T(8,128)(2,1)S(1)} %add_convert_fusion), channel_id=1, source_target_pairs={{0,8},{4,12},{8,0},{12,4},{1,9},{5,13},{9,1},{13,5},{2,10},{6,14},... | collective-permute-start | bytes 589832 | tf_op jit(solution)/shard_map/ppermute | solution.py:666

commit v5 on v4

--- a/solution.py
+++ b/solution.py
@@ -243,9 +243,9 @@
 
 def near_kernel(*refs, head, blocks, heads, groups, depth):
     if head == 0:
-        info, q_in, do_in, own, near = refs[:5]
-        table, top, q_v, do_v, qt, dt, kbn, vtn, pn, dpn, on = refs[5:16]
-        kv, vb, kv_sem, row_sem = refs[16:]
+        info, q_v, do_in, own, near = refs[:5]
+        table, top, do_v, qt, dt, kbn, vtn, pn, dpn, on = refs[5:15]
+        kv, vb, kv_sem, row_sem = refs[15:]
     else:
         table, qt, dt, own, near = refs[:5]
         top, kbn, vtn, pn, dpn, on = refs[5:11]
@@ -258,25 +258,14 @@
         copy.start()
     if head == 0:
 
-        def row_copies(b):
-            rows = pl.ds(b * T, T)
-            return (
-                pltpu.make_async_copy(q_in.at[rows], q_v.at[rows], row_sem.at[0, b]),
-                pltpu.make_async_copy(do_in.at[rows], do_v.at[rows], row_sem.at[1, b]),
-            )
-
-        for b in range(blocks):
-            for copy in row_copies(b):
-                copy.start()
+        do_copy = pltpu.make_async_copy(do_in, do_v, row_sem)
+        do_copy.start()
         relation_table(info, table, blocks, depth)
         highest = jnp.zeros((1, heads * groups * T), F32)
         for b in range(blocks):
-            for copy in row_copies(b):
-                copy.wait()
             for g in range(heads * groups):
                 col = pl.ds(g * D, D)
                 qt[b, :, col] = q_v[pl.ds(b * T, T), col].T
-                dt[b, :, col] = do_v[pl.ds(b * T, T), col].T
             wide = qt[b].astype(F32)
             highest = jnp.maximum(highest, jnp.sum(wide * wide, axis=0, keepdims=True))
         top[0] = jnp.max(highest)
@@ -303,19 +292,25 @@
         exps = jnp.exp2(scores * (SCALE * LOG2E))
         pn[b, :T, col] = jnp.where(tri, exps[:T], 0.0).astype(BF)
         pn[b, T:, col] = exps[T:].astype(BF)
+    if head == 0:
+        do_copy.wait()
+        for b in range(blocks):
+            for g in range(heads * groups):
+                col = pl.ds(g * D, D)
+                dt[b, :, col] = do_v[pl.ds(b * T, T), col].T
     for b, col, head_col in pieces:
         dpn[b, :, col] = jnp.dot(vb[b], dt[b, :, head_col], preferred_element_type=F32)
     for b, col, head_col in pieces:
         on[b, :, col] = jnp.dot(vtn[b], pn[b, :, col], preferred_element_type=F32)[: D + 8]
 
 
-def far_kernel(*refs, head, blocks, groups, chained, direct):
+def far_kernel(*refs, head, blocks, groups, chained):
     table, top, near_top, q_v, do_v, qt, dt, kbn, vtn, pn, dpn, on = refs[:12]
     sources = refs[12:14]
     at = 15 if chained else 14
     o_out, pn_out, dst, kb, stats = refs[at : at + 5]
-    sent = refs[at + 5 : at + (8 if direct else 7)]
-    pt, vb, vt, acc, o_buf, out_sem = refs[at + (8 if direct else 7) :]
+    sent = refs[at + 5 : at + 8]
+    pt, vb, vt, acc, o_buf, out_sem = refs[at + 8 :]
     acc[...] = jnp.zeros_like(acc)
     for b in range(blocks):
         kb[b, :T, :] = kbn[b, T:]
@@ -427,7 +422,6 @@
         )
         for r in (2, 3)
     ]
-    slots = 2 if direct else blocks
     for b in range(blocks):
         q_rows, do_rows = (stacked(ref, head, b, groups) for ref in (q_v, do_v))
         dv = jnp.dot(pt[b], do_rows, preferred_element_type=F32)
@@ -436,21 +430,14 @@
         for r, index in enumerate(places):
             slot = index
             if r:
-                if direct:
-                    slot = jnp.where(index == lows[r - 1], 0, 1)
-                slot = blocks + slot + (r - 1) * slots
-            here = row_span(jnp.where(index >= 0, slot, 3 * blocks))
+                slot = jnp.where(index == lows[r - 1], 0, 1) + blocks + (r - 1) * 2
+            here = row_span(jnp.where(index >= 0, slot, blocks + 4))
             acc[here, :D] += dk[r * T : (r + 1) * T]
             acc[here, D:] += dv[r * T : (r + 1) * T]
     tokens = blocks * T
-    ends = [0, tokens, tokens + slots * T, tokens + 2 * slots * T]
-    if direct:
-        for r in range(3):
-            sent[r][...] = acc[ends[r] : ends[r + 1]].astype(BF)
-    else:
-        sent[0][:tokens] = acc[:tokens].astype(BF)
-        sent[0][tokens:] = acc[ends[2] : ends[3]].astype(BF)
-        sent[1][...] = acc[ends[1] : ends[2]].astype(BF)
+    ends = [0, tokens, tokens + 2 * T, tokens + 4 * T]
+    for r in range(3):
+        sent[r][...] = acc[ends[r] : ends[r + 1]].astype(BF)
     for b in range(blocks):
         out_copy(b).wait()
 
@@ -498,20 +485,15 @@
     table = refs[0]
     dk_ref, dv_ref, acc = refs[-3:]
     at = 1
-    tokens = blocks * T
     for h in range(heads):
         own, core = refs[at : at + 2]
         at += 2
-        acc[...] = own[...] + core[:tokens].astype(F32)
-        if h + 1 == heads:
-            acc[...] += refs[at][...].astype(F32)
-            at += 1
-        else:
-            for r in range(2):
-                for side in range(2):
-                    index = jnp.minimum(table[blocks * LINKED + 2 * r + side], blocks - 1)
-                    acc[row_span(index)] += refs[at + r][pl.ds(side * T, T)].astype(F32)
-            at += 2
+        acc[...] = own[...] + core[...].astype(F32)
+        for r in range(2):
+            for side in range(2):
+                index = jnp.minimum(table[blocks * LINKED + 2 * r + side], blocks - 1)
+                acc[row_span(index)] += refs[at + r][pl.ds(side * T, T)].astype(F32)
+        at += 2
         dk_ref[:, pl.ds(h * D, D)] = acc[:, :D].astype(BF)
         dv_ref[:, pl.ds(h * D, D)] = acc[:, D:].astype(BF)
 
@@ -555,7 +537,6 @@
         ]
         whole = [
             kept(queries.shape, BF),
-            kept(queries.shape, BF),
             kept((blocks, D, heads * width), BF),
             kept((blocks, D, heads * width), BF),
         ]
@@ -564,11 +545,11 @@
             wide = pl.BlockSpec(memory_space=pltpu.HBM)
             operands = [
                 info,
-                pltpu.with_memory_space_constraint(queries, pltpu.HBM),
+                kept_queries,
                 pltpu.with_memory_space_constraint(output_gradient, pltpu.HBM),
             ]
-            in_specs = [smem, wide, wide]
-            out_specs = [smem, smem] + [vmem] * 9
+            in_specs = [smem, vmem, wide]
+            out_specs = [smem, smem] + [vmem] * 8
             out_shape = [table_shape, pltpu.SMEM((2,), F32)] + whole + parts
         else:
             operands = [local[0], local[4], local[5]]
@@ -587,19 +568,20 @@
                 pltpu.VMEM((blocks, 2 * T, D), BF),
                 pltpu.SemaphoreType.DMA((2,)),
             ]
-            + ([pltpu.SemaphoreType.DMA((2, blocks))] if first else []),
+            + ([pltpu.SemaphoreType.DMA] if first else []),
             compiler_params=pltpu.CompilerParams(vmem_limit_bytes=12 * 2**20),
             cost_estimate=work(4),
             name="near",
         )(*operands, packed[h], near[h])
         return [scalars(x) if x.ndim == 1 else keep(x) for x in done]
 
+    kept_queries = keep(queries)
     shared = near_work(0, None)
     table, top = shared[:2]
-    local = shared[2:6]
-    far[0], _ = lax.optimization_barrier((far[0], shared[10]))
+    local = [kept_queries] + shared[2:5]
+    far[0], _ = lax.optimization_barrier((far[0], shared[9]))
     diagonal = [lax.ppermute(far[0], "ctx", core)]
-    near_parts = [[top] + shared[6:]]
+    near_parts = [[top] + shared[5:]]
     for h in range(1, heads):
         near_parts.append(near_work(h, [table, None] + local))
         far[h], _ = lax.optimization_barrier((far[h], near_parts[h][5]))
@@ -610,16 +592,12 @@
     arrivals = []
     for h in range(heads):
         chained = attended is not None
-        direct = h + 1 < heads
-        if direct:
-            sent = [tokens, 2 * T, 2 * T]
-        else:
-            sent = [2 * tokens, tokens]
+        sent = [tokens, 2 * T, 2 * T]
         operands = [table, top, near_parts[h][0], *local, *near_parts[h][1:]]
         operands += [keep(far[h]), keep(diagonal[h])]
         done = pl.pallas_call(
             functools.partial(
-                far_kernel, head=h, blocks=blocks, groups=groups, chained=chained, direct=direct
+                far_kernel, head=h, blocks=blocks, groups=groups, chained=chained
             ),
             in_specs=[smem] * 3 + [vmem] * 11 + [hbm] * (1 if chained else 0),
             out_specs=[hbm] + [vmem] * (4 + len(sent)),
@@ -636,7 +614,7 @@
                 pltpu.VMEM((blocks, 3 * T, width), BF),
                 pltpu.VMEM((blocks, 2 * T, D), BF),
                 pltpu.VMEM((blocks, D + ONES, 2 * T), BF),
-                pltpu.VMEM((3 * tokens + T, 2 * D), F32),
+                pltpu.VMEM((tokens + 5 * T, 2 * D), F32),
                 pltpu.VMEM((blocks, T, groups * D), BF),
                 pltpu.SemaphoreType.DMA((blocks,)),
             ],
@@ -648,30 +626,22 @@
         near_probs, *rest = [keep(x) for x in done[1:5]]
         _, kbn, _, _, dpn, _ = near_parts[h]
         probs.append([kbn, near_probs, dpn, *rest])
-        if direct:
-            to_core, to_far, to_corner = done[5:]
-            arrivals.append(
-                [
-                    lax.ppermute(to_core, "ctx", core),
-                    lax.ppermute(to_far, "ctx", across),
-                    lax.ppermute(to_corner, "ctx", corner),
-                ]
-            )
-        else:
-            to_core, to_far = done[5:]
-            if arrivals:
-                to_core, arrivals[-1] = lax.optimization_barrier((to_core, arrivals[-1]))
-            received = lax.ppermute(to_core, "ctx", core)
-            sums = (to_far.astype(F32) + received[tokens:].astype(F32)).astype(BF)
-            arrivals.append([received, lax.ppermute(sums, "ctx", across)])
+        to_core, to_far, to_corner = done[5:]
+        arrivals.append(
+            [
+                lax.ppermute(to_core, "ctx", core),
+                lax.ppermute(to_far, "ctx", across),
+                lax.ppermute(to_corner, "ctx", corner),
+            ]
+        )
 
     d_queries = None
     finishing = [table]
     for h in range(heads):
         chained = d_queries is not None
         operands = [local[0], local[1], *probs[h]]
-        if not chained:
-            operands[-1], _ = lax.optimization_barrier((operands[-1], sums))
+        if not chained and heads > 1:
+            operands[-1], arrivals[0] = lax.optimization_barrier((operands[-1], arrivals[0]))
             operands[-1] = keep(operands[-1])
         done = pl.pallas_call(
             functools.partial(tail_kernel, head=h, blocks=blocks, groups=groups, chained=chained),
@@ -686,7 +656,7 @@
                 pltpu.SemaphoreType.DMA((blocks,)),
             ],
             compiler_params=pltpu.CompilerParams(vmem_limit_bytes=12 * 2**20),
-            cost_estimate=work(0.3),
+            cost_estimate=work(1),
             name="tail",
         )(*operands, *([d_queries] if chained else []))
         d_queries = done[0]

time: 49.2 us -> 48.4 us (0.984)
  Pallas kernels: 34.6 us -> 33.7 us
    ppermute x2 -> x0, waiting for transfers between devices: 2.55 us -> none  [the longest x1 1.43 us: linked_body(): received = lax.ppermute(to_core, 'ctx', core)]
    ppermute x2 -> x0, starting transfers between devices: 2.17 us -> none  [the longest x1 1.81 us: linked_body(): arrivals.append([received, lax.ppermute(sums, 'ctx', across)])]
    ppermute x1 -> x2, starting transfers between devices: 1.82 us -> 3.47 us  [linked_body(): lax.ppermute(to_far, 'ctx', across)]
    ppermute x1 -> x2, waiting for transfers between devices: 0.01 us -> 1.4 us  [linked_body(): lax.ppermute(to_corner, 'ctx', corner)]
    ppermute x2, waiting for transfers between devices: 0.84 us -> 1.91 us  [linked_body(): far = [lax.ppermute(own, 'ctx', across) for own in packed]]
    pallas_call x2, Pallas kernels: 6.6 us -> 5.73 us  [near_work(): pl.pallas_call(functools.partial(near_kernel, head=h, blocks=blocks, head...]
  transfers between devices with their start and end apart: 11 -> 12, of which waited for: 4 -> 5; matrix products, arithmetic and copies ran while one was open for 0% -> 0% of each run, Pallas kernels for 69% -> 68%
where the time goes in v5:
time: 48.4 us; the launch traced here: 48.2 us
  Pallas kernels  33.7 us (70%)
  starting transfers between devices  7.92 us (16%)
  waiting for transfers between devices  4.46 us (9%)
  local copies, waits for them, and re-layouts  1.2 us (2%)
  between operations  0.75 us (2%)
    pallas_call x2, Pallas kernels, linked_body(): pl.pallas_call(functools.partial(far_kernel, head=h, blocks=blocks, group...  22.9 us
    pallas_call x2, Pallas kernels, near_work(): pl.pallas_call(functools.partial(near_kernel, head=h, blocks=blocks, head...  5.73 us
    pallas_call x2, Pallas kernels, linked_body(): pl.pallas_call(functools.partial(tail_kernel, head=h, blocks=blocks, grou...  4.17 us
    ppermute x2, starting transfers between devices, linked_body(): lax.ppermute(to_far, 'ctx', across)  3.47 us
    ppermute x2, starting transfers between devices, linked_body(): far = [lax.ppermute(own, 'ctx', across) for own in packed]  3.19 us
    ppermute x2, waiting for transfers between devices, linked_body(): far = [lax.ppermute(own, 'ctx', across) for own in packed]  1.91 us
    ppermute x2, waiting for transfers between devices, linked_body(): lax.ppermute(to_corner, 'ctx', corner)  1.4 us
    slice x1, local copies, waits for them, and re-layouts, body(): key_states[:, h * D:(h + 1) * D]  1.18 us
  transfers between devices with their start and end apart: 12, of which 5 were waited for; matrix products, arithmetic and copies ran while one was open for 0% of the time, Pallas kernels for 68%

profile of v5, /device:TPU:0, one launch (start us, length us, event | category | flops | bytes accessed | tf_op | source)
XLA Modules:
  0.0 48.2 jit_solution(14925921690112923571)
XLA Ops:
  0.6 0.0 copy-start.1
  0.6 0.0 copy-start.2
  0.7 0.0 copy-start
  0.7 1.2 %fusion = (bf16[384,128]{1,0:T(8,128)(2,1)S(1)}, bf16[384,128]{1,0:T(8,128)(2,1)S(1)}, bf16[384,128]{1,0:T(8,128)(2,1)S(1)}, bf16[384,128]{1,0:T(8,128)(2,1)S(1)}) fusion(bf16[384,256]{1,0:T(8,128)(2,1)} %param.7, bf16[384,256]{1,0:T(8,128)(2,1)} %param.8), kind=kLoop, calls=%fused_computation.3 | loop fusion | bytes 786432 | tf_op jit(solution)/shard_map/slice | solution.py:680
  1.9 3.0 %collective-permute-start.4 = (bf16[384,256]{1,0:T(8,128)(2,1)S(1)}, bf16[384,256]{1,0:T(8,128)(2,1)S(1)}, u32[]{:S(2)}, u32[]{:S(2)}) collective-permute-start(bf16[384,256]{1,0:T(8,128)(2,1)S(1)} %pad_maximum_fusion.refs_3_), channel_id=1, source_target_pairs={{0,8},{4,12},{8,0},{12,4},{1,9},{5,13},{9,1},{13,5},{2,10},{6,14},... | collective-permute-start | bytes 589832 | tf_op jit(solution)/shard_map/ppermute | solution.py:516
  4.9 0.0 collective-permute-start
  4.9 0.2 collective-permute-start.2
  5.1 0.5 %collective-permute-start.1 = (bf16[384,256]{1,0:T(8,128)(2,1)S(1)}, bf16[384,256]{1,0:T(8,128)(2,1)S(1)}, u32[]{:S(2)}, u32[]{:S(2)}) collective-permute-start(bf16[384,256]{1,0:T(8,128)(2,1)S(1)} %pad_maximum_fusion.1.refs_3_), channel_id=1, source_target_pairs={{0,4},{4,0},{8,12},{12,8},{1,5},{5,1},{9,13},{13,9},{2,6},{6,2},{1... | collective-permute-start | bytes 589832 | tf_op jit(solution)/shard_map/ppermute | solution.py:515
  5.6 0.0 copy-done.1
  5.6 0.0 copy-done.2
  5.6 0.1 pad_add_fusion.refs_0_
  5.7 0.7 %collective-permute-done.refs_4_ = bf16[384,256]{1,0:T(8,128)(2,1)S(1)} collective-permute-done((bf16[384,256]{1,0:T(8,128)(2,1)S(1)}, bf16[384,256]{1,0:T(8,128)(2,1)S(1)}, u32[]{:S(2)}, u32[]{:S(2)}) %collective-permute-start) | collective-permute-done | bytes 196640 | tf_op jit(solution)/shard_map/ppermute | solution.py:515
  6.4 0.0 copy-done
  6.4 4.0 %near.2 = (s32[16]{0:T(128)S(4)}, f32[2]{0:T(128)S(4)}, bf16[384,2048]{1,0:T(8,128)(2,1)S(1)}, bf16[3,128,2048]{2,1,0:T(8,128)(2,1)S(1)}, bf16[3,128,2048]{2,1,0...) custom-call(s32[25]{0:T(128)S(1)} %pad_add_fusion.refs_0_, ...), custom_call_target="tpu_custom_call" | custom-call | flops 4000000000 | tf_op jit(solution)/shard_map/near/pallas_call | solution.py:559
  10.3 0.3 collective-permute-done.4.refs_12_
  10.6 0.0 collective-permute-start.5
  10.6 0.0 collective-permute-done.1.refs_4_
  10.7 1.8 %near.3 = (f32[1]{0:T(128)S(4)}, bf16[3,256,128]{2,1,0:T(8,128)(2,1)S(1)}, bf16[3,144,256]{2,1,0:T(8,128)(2,1)S(1)}, bf16[3,256,1024]{2,1,0:T(8,128)(2,1)S(1)}, ...) custom-call(s32[16]{0:T(128)S(4)} %get-tuple-element.48.refs_0_, ...), custom_call_target="tpu_custom_call" | custom-call | flops 4000000000 | tf_op jit(solution)/shard_map/near/pallas_call | solution.py:559
  12.4 1.6 %collective-permute-done.2.refs_12_ = bf16[384,256]{1,0:T(8,128)(2,1)S(1)} collective-permute-done((bf16[384,256]{1,0:T(8,128)(2,1)S(1)}, bf16[384,256]{1,0:T(8,128)(2,1)S(1)}, u32[]{:S(2)}, u32[]{:S(2)}) %collective-permute-start.2) | collective-permute-done | bytes 196640 | tf_op jit(solution)/shard_map/ppermute | solution.py:516
  14.0 0.0 collective-permute-start.3
  14.0 0.0 collective-permute-done.5.refs_13_
  14.0 11.4 %far.2 = (bf16[384,2048]{1,0:T(8,128)(2,1)}, bf16[3,256,1024]{2,1,0:T(8,128)(2,1)S(1)}, bf16[3,384,1024]{2,1,0:T(8,128)(2,1)S(1)}, bf16[3,384,128]{2,1,0:T(8,128...) custom-call(s32[16]{0:T(128)S(4)} %get-tuple-element.48.refs_0_, ...), custom_call_target="tpu_custom_call", output_to_operand_aliasing={{1}: (9, {})} | custom-call | flops 5000000000 | tf_op jit(solution)/shard_map/far/pallas_call | solution.py:598
  25.4 1.8 %collective-permute-start.7 = (bf16[256,256]{1,0:T(8,128)(2,1)S(1)}, bf16[256,256]{1,0:T(8,128)(2,1)S(1)}, u32[]{:S(2)}, u32[]{:S(2)}) collective-permute-start(bf16[256,256]{1,0:T(8,128)(2,1)S(1)} %get-tuple-element.77), channel_id=1, source_target_pairs={{0,8},{4,12},{8,0},{12,4},{1,9},{5,13},{9,1},{13,5},{2,10},{6,14},... | collective-permute-start | bytes 393224 | tf_op jit(solution)/shard_map/ppermute | solution.py:633
  27.2 0.2 collective-permute-start.8
  27.4 0.2 collective-permute-start.6
  27.6 0.0 collective-permute-done.3.refs_13_
  27.6 11.5 %far.3 = (bf16[384,2048]{1,0:T(8,128)(2,1)}, bf16[3,256,1024]{2,1,0:T(8,128)(2,1)S(1)}, bf16[3,384,1024]{2,1,0:T(8,128)(2,1)S(1)}, bf16[3,384,128]{2,1,0:T(8,128...) custom-call(s32[16]{0:T(128)S(4)} %get-tuple-element.48.refs_0_, ...), custom_call_target="tpu_custom_call", output_to_operand_aliasing={{1}: (9, {}), {0}: (14, {})} | custom-call | flops 5000000000 | tf_op jit(solution)/shard_map/far/pallas_call | solution.py:598
  39.1 0.3 collective-permute-start.9
  39.5 1.7 %collective-permute-start.10 = (bf16[256,256]{1,0:T(8,128)(2,1)S(1)}, bf16[256,256]{1,0:T(8,128)(2,1)S(1)}, u32[]{:S(2)}, u32[]{:S(2)}) collective-permute-start(bf16[256,256]{1,0:T(8,128)(2,1)S(1)} %get-tuple-element.88), channel_id=1, source_target_pairs={{0,8},{4,12},{8,0},{12,4},{1,9},{5,13},{9,1},{13,5},{2,10},{6,14},... | collective-permute-start | bytes 393224 | tf_op jit(solution)/shard_map/ppermute | solution.py:633
  41.2 0.0 collective-permute-done.7.refs_3_
  41.2 0.0 collective-permute-start.11
  41.2 0.0 collective-permute-done.8.refs_4_
  41.2 0.0 collective-permute-done.6.refs_2_
  41.2 2.1 %tail.2 = (bf16[384,2048]{1,0:T(8,128)(2,1)}, f32[384,256]{1,0:T(8,128)S(1)}) custom-call(bf16[384,2048]{1,0:T(8,128)(2,1)S(1)} %copy-done, bf16[384,2048]{1,0:T(8,128)(2,1)S(1)} %get-tuple-element.53.refs_4_.refs_1_, bf16[3,256,128]{2,1,0:T(8,128)(2,1)S(1)} %get-tuple-element.60.refs_7_.refs_2_, bf16[3,256,1024]{2,1,0:T(8,128)(2,1)S(1)} %get-tuple-element.72.refs_3_, ...), custom_call_target="tpu_custom_call" | custom-call | flops 1000000000 | tf_op jit(solution)/shard_map/tail/pallas_call | solution.py:646
  43.3 2.1 %tail.3 = (bf16[384,2048]{1,0:T(8,128)(2,1)}, f32[384,256]{1,0:T(8,128)S(1)}) custom-call(bf16[384,2048]{1,0:T(8,128)(2,1)S(1)} %copy-done, bf16[384,2048]{1,0:T(8,128)(2,1)S(1)} %get-tuple-element.53.refs_4_.refs_1_, bf16[3,256,128]{2,1,0:T(8,128)(2,1)S(1)} %get-tuple-element.54.refs_7_.refs_2_, ...), custom_call_target="tpu_custom_call", output_to_operand_aliasing={{0}: (8, {})} | custom-call | flops 1000000000 | tf_op jit(solution)/shard_map/tail/pallas_call | solution.py:646
  45.4 0.5 collective-permute-done.10.refs_7_
  45.8 1.4 %collective-permute-done.11.refs_8_ = bf16[256,256]{1,0:T(8,128)(2,1)S(1)} collective-permute-done((bf16[256,256]{1,0:T(8,128)(2,1)S(1)}, bf16[256,256]{1,0:T(8,128)(2,1)S(1)}, u32[]{:S(2)}, u32[]{:S(2)}) %collective-permute-start.11) | collective-permute-done | bytes 131104 | tf_op jit(solution)/shard_map/ppermute | solution.py:634
  47.2 0.0 collective-permute-done.9.refs_6_
  47.2 1.0 %finish.1 = (bf16[384,256]{1,0:T(8,128)(2,1)}, bf16[384,256]{1,0:T(8,128)(2,1)}) custom-call(s32[16]{0:T(128)S(4)} %get-tuple-element.48.refs_0_, f32[384,256]{1,0:T(8,128)S(1)} %get-tuple-element.82.refs_1_, bf16[384,256]{1,0:T(8,128)(2,1)S(1)} %collective-permute-done.6.refs_2_, bf16[256,256]{1,0:T(8,128)(2,1)S(1)} %collective-permute-done.7.refs_3_, ...), custom_call_target="tpu_custom_call" | custom-call | tf_op jit(solution)/shard_map/finish/pallas_call | solution.py:664
  (2 shorter events, 0.0 us)
Async XLA Ops:
  0.6 5.0 %copy-start.1 = (s32[12]{0:T(128)S(1)}, s32[12]{0:T(128)}, u32[]{:S(2)}) copy-start(s32[12]{0:T(128)} %param.11) | copy-start | bytes 148
  0.6 5.0 %copy-start.2 = (s32[12]{0:T(128)S(1)}, s32[12]{0:T(128)}, u32[]{:S(2)}) copy-start(s32[12]{0:T(128)} %param.10) | copy-start | bytes 148
  0.7 5.7 %copy-start = (bf16[384,2048]{1,0:T(8,128)(2,1)S(1)}, bf16[384,2048]{1,0:T(8,128)(2,1)}, u32[]{:S(2)}) copy-start(bf16[384,2048]{1,0:T(8,128)(2,1)} %refs_0_.3) | copy-start | bytes 4718596
  1.9 8.8 %collective-permute-start.4 = (bf16[384,256]{1,0:T(8,128)(2,1)S(1)}, bf16[384,256]{1,0:T(8,128)(2,1)S(1)}, u32[]{:S(2)}, u32[]{:S(2)}) collective-permute-start(bf16[384,256]{1,0:T(8,128)(2,1)S(1)} %pad_maximum_fusion.refs_3_), channel_id=1, source_target_pairs={{0,8},{4,12},{8,0},{12,4},{1,9},{5,13},{9,1},{13,5},{2,10},{6,14},... | collective-permute-start | bytes 589832 | tf_op jit(solution)/shard_map/ppermute | solution.py:516
  4.9 1.4 %collective-permute-start = (bf16[384,256]{1,0:T(8,128)(2,1)S(1)}, bf16[384,256]{1,0:T(8,128)(2,1)S(1)}, u32[]{:S(2)}, u32[]{:S(2)}) collective-permute-start(bf16[384,256]{1,0:T(8,128)(2,1)S(1)} %pad_maximum_fusion.refs_3_), channel_id=1, source_target_pairs={{0,4},{4,0},{8,12},{12,8},{1,5},{5,1},{9,13},{13,9},{2,6},{6,2},{1... | collective-permute-start | bytes 589832 | tf_op jit(solution)/shard_map/ppermute | solution.py:515
  4.9 9.1 %collective-permute-start.2 = (bf16[384,256]{1,0:T(8,128)(2,1)S(1)}, bf16[384,256]{1,0:T(8,128)(2,1)S(1)}, u32[]{:S(2)}, u32[]{:S(2)}) collective-permute-start(bf16[384,256]{1,0:T(8,128)(2,1)S(1)} %pad_maximum_fusion.1.refs_3_), channel_id=1, source_target_pairs={{0,8},{4,12},{8,0},{12,4},{1,9},{5,13},{9,1},{13,5},{2,10},{6,14},... | collective-permute-start | bytes 589832 | tf_op jit(solution)/shard_map/ppermute | solution.py:516
  5.1 5.5 %collective-permute-start.1 = (bf16[384,256]{1,0:T(8,128)(2,1)S(1)}, bf16[384,256]{1,0:T(8,128)(2,1)S(1)}, u32[]{:S(2)}, u32[]{:S(2)}) collective-permute-start(bf16[384,256]{1,0:T(8,128)(2,1)S(1)} %pad_maximum_fusion.1.refs_3_), channel_id=1, source_target_pairs={{0,4},{4,0},{8,12},{12,8},{1,5},{5,1},{9,13},{13,9},{2,6},{6,2},{1... | collective-permute-start | bytes 589832 | tf_op jit(solution)/shard_map/ppermute | solution.py:515
  10.6 3.4 %collective-permute-start.5 = (bf16[384,256]{1,0:T(8,128)(2,1)S(1)}, bf16[384,256]{1,0:T(8,128)(2,1)S(1)}, u32[]{:S(2)}, u32[]{:S(2)}) collective-permute-start(bf16[384,256]{1,0:T(8,128)(2,1)S(1)} %collective-permute-done.4.refs_12_), channel_id=1, source_target_pairs={{0,4},{4,0},{8,12},{12,8},{1,5},{5,1},{9,13},{13,9},{2,6},{6,2},{1... | collective-permute-start | bytes 589832 | tf_op jit(solution)/shard_map/ppermute | solution.py:583
  14.0 13.6 %collective-permute-start.3 = (bf16[384,256]{1,0:T(8,128)(2,1)S(1)}, bf16[384,256]{1,0:T(8,128)(2,1)S(1)}, u32[]{:S(2)}, u32[]{:S(2)}) collective-permute-start(bf16[384,256]{1,0:T(8,128)(2,1)S(1)} %collective-permute-done.2.refs_12_), channel_id=1, source_target_pairs={{0,4},{4,0},{8,12},{12,8},{1,5},{5,1},{9,13},{13,9},{2,6},{6,2},{1... | collective-permute-start | bytes 589832 | tf_op jit(solution)/shard_map/ppermute | solution.py:588
  25.4 15.8 %collective-permute-start.7 = (bf16[256,256]{1,0:T(8,128)(2,1)S(1)}, bf16[256,256]{1,0:T(8,128)(2,1)S(1)}, u32[]{:S(2)}, u32[]{:S(2)}) collective-permute-start(bf16[256,256]{1,0:T(8,128)(2,1)S(1)} %get-tuple-element.77), channel_id=1, source_target_pairs={{0,8},{4,12},{8,0},{12,4},{1,9},{5,13},{9,1},{13,5},{2,10},{6,14},... | collective-permute-start | bytes 393224 | tf_op jit(solution)/shard_map/ppermute | solution.py:633
  27.2 14.0 %collective-permute-start.8 = (bf16[256,256]{1,0:T(8,128)(2,1)S(1)}, bf16[256,256]{1,0:T(8,128)(2,1)S(1)}, u32[]{:S(2)}, u32[]{:S(2)}) collective-permute-start(bf16[256,256]{1,0:T(8,128)(2,1)S(1)} %get-tuple-element.78), channel_id=1, source_target_pairs={{0,12},{4,8},{8,4},{12,0},{1,13},{5,9},{9,5},{13,1},{2,14},{6,10},... | collective-permute-start | bytes 393224 | tf_op jit(solution)/shard_map/ppermute | solution.py:634
  27.4 13.8 %collective-permute-start.6 = (bf16[384,256]{1,0:T(8,128)(2,1)S(1)}, bf16[384,256]{1,0:T(8,128)(2,1)S(1)}, u32[]{:S(2)}, u32[]{:S(2)}) collective-permute-start(bf16[384,256]{1,0:T(8,128)(2,1)S(1)} %get-tuple-element.76), channel_id=1, source_target_pairs={{0,4},{4,0},{8,12},{12,8},{1,5},{5,1},{9,13},{13,9},{2,6},{6,2},{1... | collective-permute-start | bytes 589832 | tf_op jit(solution)/shard_map/ppermute | solution.py:632
  39.1 8.1 %collective-permute-start.9 = (bf16[384,256]{1,0:T(8,128)(2,1)S(1)}, bf16[384,256]{1,0:T(8,128)(2,1)S(1)}, u32[]{:S(2)}, u32[]{:S(2)}) collective-permute-start(bf16[384,256]{1,0:T(8,128)(2,1)S(1)} %get-tuple-element.87), channel_id=1, source_target_pairs={{0,4},{4,0},{8,12},{12,8},{1,5},{5,1},{9,13},{13,9},{2,6},{6,2},{1... | collective-permute-start | bytes 589832 | tf_op jit(solution)/shard_map/ppermute | solution.py:632
  39.5 6.3 %collective-permute-start.10 = (bf16[256,256]{1,0:T(8,128)(2,1)S(1)}, bf16[256,256]{1,0:T(8,128)(2,1)S(1)}, u32[]{:S(2)}, u32[]{:S(2)}) collective-permute-start(bf16[256,256]{1,0:T(8,128)(2,1)S(1)} %get-tuple-element.88), channel_id=1, source_target_pairs={{0,8},{4,12},{8,0},{12,4},{1,9},{5,13},{9,1},{13,5},{2,10},{6,14},... | collective-permute-start | bytes 393224 | tf_op jit(solution)/shard_map/ppermute | solution.py:633
  41.2 6.1 %collective-permute-start.11 = (bf16[256,256]{1,0:T(8,128)(2,1)S(1)}, bf16[256,256]{1,0:T(8,128)(2,1)S(1)}, u32[]{:S(2)}, u32[]{:S(2)}) collective-permute-start(bf16[256,256]{1,0:T(8,128)(2,1)S(1)} %get-tuple-element.89), channel_id=1, source_target_pairs={{0,12},{4,8},{8,4},{12,0},{1,13},{5,9},{9,5},{13,1},{2,14},{6,10},... | collective-permute-start | bytes 393224 | tf_op jit(solution)/shard_map/ppermute | solution.py:634

commit v6 on v5

--- a/solution.py
+++ b/solution.py
@@ -346,12 +346,14 @@
             sums = jnp.dot(vt[b], pt[b, T:, col], preferred_element_type=F32)
             sums = sums[: D + 8] + on[b, :, col]
             inverse = 1.0 / sums[D : D + 1]
-            out_t = sums[:D] * inverse
-            inner = jnp.sum(out_t * dt[b, :, head_col].astype(F32), axis=0, keepdims=True)
+            out_t = (sums[:D] * inverse).astype(BF)
+            inner = jnp.sum(
+                out_t.astype(F32) * dt[b, :, head_col].astype(F32), axis=0, keepdims=True
+            )
             stats[b, :8, col] = jnp.broadcast_to(inverse, (8, WIDE * T))
             stats[b, 8:, col] = jnp.broadcast_to(inner, (8, WIDE * T))
             for w in range(WIDE):
-                o_buf[b, :, pl.ds((j + w) * D, D)] = out_t[:, w * T : (w + 1) * T].astype(BF).T
+                o_buf[b, :, pl.ds((j + w) * D, D)] = out_t[:, w * T : (w + 1) * T].T
             if j + WIDE == groups:
                 out_copy(b).start()
         for b, j, col, head_col in pieces:
@@ -390,23 +392,25 @@
                     jnp.add, [jnp.sum(x, axis=0, keepdims=True) for x in exps]
                 )
                 inverse = 1.0 / total
-                inner = inverse * functools.reduce(
-                    jnp.add,
-                    [jnp.sum(x * y, axis=0, keepdims=True) for x, y in zip(exps, dparts)],
+                for r in range(LINKED):
+                    weights = (exps[r] * inverse).astype(BF)
+                    if r < 2:
+                        pn_out[b, pl.ds(r * T, T), col] = weights
+                    if r > 0:
+                        pt[b, pl.ds((r - 1) * T, T), col] = weights
+                out_t = jnp.dot(
+                    vtn[b], pn_out[b, :, col], preferred_element_type=F32
+                ) + jnp.dot(vt[b], pt[b, T:, col], preferred_element_type=F32)
+                out_t = out_t[:D].astype(BF)
+                inner = jnp.sum(
+                    out_t.astype(F32) * dt[b, :, head_col].astype(F32), axis=0, keepdims=True
                 )
                 stats[b, :8, col] = jnp.ones((8, T), F32)
                 stats[b, 8:, col] = jnp.broadcast_to(inner, (8, T))
-                pn_out[b, :T, col] = (exps[0] * inverse).astype(BF)
-                pn_out[b, T:, col] = (exps[1] * inverse).astype(BF)
                 for r in range(3):
-                    here = pl.ds(r * T, T)
-                    weights = exps[1 + r] * inverse
-                    pt[b, here, col] = weights.astype(BF)
-                    dst[b, here, col] = (weights * (dparts[1 + r] - inner)).astype(BF)
-                out_t = jnp.dot(
-                    vtn[b], pn_out[b, :, col], preferred_element_type=F32
-                ) + jnp.dot(vt[b], pt[b, T:, col], preferred_element_type=F32)
-                o_buf[b, :, pl.ds(g * D, D)] = out_t[:D].astype(BF).T
+                    dscores = exps[1 + r] * inverse * (dparts[1 + r] - inner)
+                    dst[b, pl.ds(r * T, T), col] = dscores.astype(BF)
+                o_buf[b, :, pl.ds(g * D, D)] = out_t.T
             out_copy(b).start()
             return carry
 

time: 48.4 us -> 48 us (level)
  no operation moved by 1% of the time
where the time goes in v6:
time: 48 us; the launch traced here: 47.7 us
  Pallas kernels  33.3 us (69%)
  starting transfers between devices  7.95 us (17%)
  waiting for transfers between devices  4.39 us (9%)
  local copies, waits for them, and re-layouts  1.2 us (2%)
  between operations  0.75 us (2%)
    pallas_call x2, Pallas kernels, linked_body(): pl.pallas_call(functools.partial(far_kernel, head=h, blocks=blocks, group...  22.5 us
    pallas_call x2, Pallas kernels, near_work(): pl.pallas_call(functools.partial(near_kernel, head=h, blocks=blocks, head...  5.73 us
    pallas_call x2, Pallas kernels, linked_body(): pl.pallas_call(functools.partial(tail_kernel, head=h, blocks=blocks, grou...  4.17 us
    ppermute x2, starting transfers between devices, linked_body(): lax.ppermute(to_far, 'ctx', across)  3.47 us
    ppermute x2, starting transfers between devices, linked_body(): far = [lax.ppermute(own, 'ctx', across) for own in packed]  3.19 us
    ppermute x2, waiting for transfers between devices, linked_body(): far = [lax.ppermute(own, 'ctx', across) for own in packed]  1.91 us
    ppermute x2, waiting for transfers between devices, linked_body(): lax.ppermute(to_corner, 'ctx', corner)  1.33 us
    slice x1, local copies, waits for them, and re-layouts, body(): key_states[:, h * D:(h + 1) * D]  1.18 us
  transfers between devices with their start and end apart: 12, of which 5 were waited for; matrix products, arithmetic and copies ran while one was open for 0% of the time, Pallas kernels for 68%

profile of v6, /device:TPU:0, one launch (start us, length us, event | category | flops | bytes accessed | tf_op | source)
XLA Modules:
  0.0 47.7 jit_solution(9697645190829642591)
XLA Ops:
  0.6 0.0 copy-start.1
  0.6 0.0 copy-start.2
  0.7 0.0 copy-start
  0.7 1.2 %fusion = (bf16[384,128]{1,0:T(8,128)(2,1)S(1)}, bf16[384,128]{1,0:T(8,128)(2,1)S(1)}, bf16[384,128]{1,0:T(8,128)(2,1)S(1)}, bf16[384,128]{1,0:T(8,128)(2,1)S(1)}) fusion(bf16[384,256]{1,0:T(8,128)(2,1)} %param.7, bf16[384,256]{1,0:T(8,128)(2,1)} %param.8), kind=kLoop, calls=%fused_computation.3 | loop fusion | bytes 786432 | tf_op jit(solution)/shard_map/slice | solution.py:684
  1.9 3.0 %collective-permute-start.4 = (bf16[384,256]{1,0:T(8,128)(2,1)S(1)}, bf16[384,256]{1,0:T(8,128)(2,1)S(1)}, u32[]{:S(2)}, u32[]{:S(2)}) collective-permute-start(bf16[384,256]{1,0:T(8,128)(2,1)S(1)} %pad_maximum_fusion.refs_3_), channel_id=1, source_target_pairs={{0,8},{4,12},{8,0},{12,4},{1,9},{5,13},{9,1},{13,5},{2,10},{6,14},... | collective-permute-start | bytes 589832 | tf_op jit(solution)/shard_map/ppermute | solution.py:520
  4.9 0.0 collective-permute-start
  4.9 0.2 collective-permute-start.2
  5.1 0.5 %collective-permute-start.1 = (bf16[384,256]{1,0:T(8,128)(2,1)S(1)}, bf16[384,256]{1,0:T(8,128)(2,1)S(1)}, u32[]{:S(2)}, u32[]{:S(2)}) collective-permute-start(bf16[384,256]{1,0:T(8,128)(2,1)S(1)} %pad_maximum_fusion.1.refs_3_), channel_id=1, source_target_pairs={{0,4},{4,0},{8,12},{12,8},{1,5},{5,1},{9,13},{13,9},{2,6},{6,2},{1... | collective-permute-start | bytes 589832 | tf_op jit(solution)/shard_map/ppermute | solution.py:519
  5.6 0.0 copy-done.1
  5.6 0.0 copy-done.2
  5.6 0.1 pad_add_fusion.refs_0_
  5.7 0.7 %collective-permute-done.refs_4_ = bf16[384,256]{1,0:T(8,128)(2,1)S(1)} collective-permute-done((bf16[384,256]{1,0:T(8,128)(2,1)S(1)}, bf16[384,256]{1,0:T(8,128)(2,1)S(1)}, u32[]{:S(2)}, u32[]{:S(2)}) %collective-permute-start) | collective-permute-done | bytes 196640 | tf_op jit(solution)/shard_map/ppermute | solution.py:519
  6.4 0.0 copy-done
  6.4 4.0 %near.2 = (s32[16]{0:T(128)S(4)}, f32[2]{0:T(128)S(4)}, bf16[384,2048]{1,0:T(8,128)(2,1)S(1)}, bf16[3,128,2048]{2,1,0:T(8,128)(2,1)S(1)}, bf16[3,128,2048]{2,1,0...) custom-call(s32[25]{0:T(128)S(1)} %pad_add_fusion.refs_0_, ...), custom_call_target="tpu_custom_call" | custom-call | flops 4000000000 | tf_op jit(solution)/shard_map/near/pallas_call | solution.py:563
  10.3 0.3 collective-permute-done.4.refs_12_
  10.6 0.0 collective-permute-start.5
  10.6 0.0 collective-permute-done.1.refs_4_
  10.7 1.8 %near.3 = (f32[1]{0:T(128)S(4)}, bf16[3,256,128]{2,1,0:T(8,128)(2,1)S(1)}, bf16[3,144,256]{2,1,0:T(8,128)(2,1)S(1)}, bf16[3,256,1024]{2,1,0:T(8,128)(2,1)S(1)}, ...) custom-call(s32[16]{0:T(128)S(4)} %get-tuple-element.48.refs_0_, ...), custom_call_target="tpu_custom_call" | custom-call | flops 4000000000 | tf_op jit(solution)/shard_map/near/pallas_call | solution.py:563
  12.4 1.6 %collective-permute-done.2.refs_12_ = bf16[384,256]{1,0:T(8,128)(2,1)S(1)} collective-permute-done((bf16[384,256]{1,0:T(8,128)(2,1)S(1)}, bf16[384,256]{1,0:T(8,128)(2,1)S(1)}, u32[]{:S(2)}, u32[]{:S(2)}) %collective-permute-start.2) | collective-permute-done | bytes 196640 | tf_op jit(solution)/shard_map/ppermute | solution.py:520
  14.0 0.0 collective-permute-start.3
  14.0 0.0 collective-permute-done.5.refs_13_
  14.0 11.2 %far.2 = (bf16[384,2048]{1,0:T(8,128)(2,1)}, bf16[3,256,1024]{2,1,0:T(8,128)(2,1)S(1)}, bf16[3,384,1024]{2,1,0:T(8,128)(2,1)S(1)}, bf16[3,384,128]{2,1,0:T(8,128...) custom-call(s32[16]{0:T(128)S(4)} %get-tuple-element.48.refs_0_, ...), custom_call_target="tpu_custom_call", output_to_operand_aliasing={{1}: (9, {})} | custom-call | flops 5000000000 | tf_op jit(solution)/shard_map/far/pallas_call | solution.py:602
  25.2 1.8 %collective-permute-start.7 = (bf16[256,256]{1,0:T(8,128)(2,1)S(1)}, bf16[256,256]{1,0:T(8,128)(2,1)S(1)}, u32[]{:S(2)}, u32[]{:S(2)}) collective-permute-start(bf16[256,256]{1,0:T(8,128)(2,1)S(1)} %get-tuple-element.77), channel_id=1, source_target_pairs={{0,8},{4,12},{8,0},{12,4},{1,9},{5,13},{9,1},{13,5},{2,10},{6,14},... | collective-permute-start | bytes 393224 | tf_op jit(solution)/shard_map/ppermute | solution.py:637
  27.0 0.2 collective-permute-start.8
  27.2 0.2 collective-permute-start.6
  27.4 0.0 collective-permute-done.3.refs_13_
  27.4 11.3 %far.3 = (bf16[384,2048]{1,0:T(8,128)(2,1)}, bf16[3,256,1024]{2,1,0:T(8,128)(2,1)S(1)}, bf16[3,384,1024]{2,1,0:T(8,128)(2,1)S(1)}, bf16[3,384,128]{2,1,0:T(8,128...) custom-call(s32[16]{0:T(128)S(4)} %get-tuple-element.48.refs_0_, ...), custom_call_target="tpu_custom_call", output_to_operand_aliasing={{1}: (9, {}), {0}: (14, {})} | custom-call | flops 5000000000 | tf_op jit(solution)/shard_map/far/pallas_call | solution.py:602
  38.7 0.4 collective-permute-start.9
  39.1 1.7 %collective-permute-start.10 = (bf16[256,256]{1,0:T(8,128)(2,1)S(1)}, bf16[256,256]{1,0:T(8,128)(2,1)S(1)}, u32[]{:S(2)}, u32[]{:S(2)}) collective-permute-start(bf16[256,256]{1,0:T(8,128)(2,1)S(1)} %get-tuple-element.88), channel_id=1, source_target_pairs={{0,8},{4,12},{8,0},{12,4},{1,9},{5,13},{9,1},{13,5},{2,10},{6,14},... | collective-permute-start | bytes 393224 | tf_op jit(solution)/shard_map/ppermute | solution.py:637
  40.8 0.0 collective-permute-done.7.refs_3_
  40.8 0.0 collective-permute-start.11
  40.8 0.0 collective-permute-done.8.refs_4_
  40.8 0.0 collective-permute-done.6.refs_2_
  40.8 2.1 %tail.2 = (bf16[384,2048]{1,0:T(8,128)(2,1)}, f32[384,256]{1,0:T(8,128)S(1)}) custom-call(bf16[384,2048]{1,0:T(8,128)(2,1)S(1)} %copy-done, bf16[384,2048]{1,0:T(8,128)(2,1)S(1)} %get-tuple-element.53.refs_4_.refs_1_, bf16[3,256,128]{2,1,0:T(8,128)(2,1)S(1)} %get-tuple-element.60.refs_7_.refs_2_, bf16[3,256,1024]{2,1,0:T(8,128)(2,1)S(1)} %get-tuple-element.72.refs_3_, ...), custom_call_target="tpu_custom_call" | custom-call | flops 1000000000 | tf_op jit(solution)/shard_map/tail/pallas_call | solution.py:650
  42.9 2.1 %tail.3 = (bf16[384,2048]{1,0:T(8,128)(2,1)}, f32[384,256]{1,0:T(8,128)S(1)}) custom-call(bf16[384,2048]{1,0:T(8,128)(2,1)S(1)} %copy-done, bf16[384,2048]{1,0:T(8,128)(2,1)S(1)} %get-tuple-element.53.refs_4_.refs_1_, bf16[3,256,128]{2,1,0:T(8,128)(2,1)S(1)} %get-tuple-element.54.refs_7_.refs_2_, ...), custom_call_target="tpu_custom_call", output_to_operand_aliasing={{0}: (8, {})} | custom-call | flops 1000000000 | tf_op jit(solution)/shard_map/tail/pallas_call | solution.py:650
  45.0 0.5 collective-permute-done.10.refs_7_
  45.5 1.3 %collective-permute-done.11.refs_8_ = bf16[256,256]{1,0:T(8,128)(2,1)S(1)} collective-permute-done((bf16[256,256]{1,0:T(8,128)(2,1)S(1)}, bf16[256,256]{1,0:T(8,128)(2,1)S(1)}, u32[]{:S(2)}, u32[]{:S(2)}) %collective-permute-start.11) | collective-permute-done | bytes 131104 | tf_op jit(solution)/shard_map/ppermute | solution.py:638
  46.8 0.0 collective-permute-done.9.refs_6_
  46.8 1.0 %finish.1 = (bf16[384,256]{1,0:T(8,128)(2,1)}, bf16[384,256]{1,0:T(8,128)(2,1)}) custom-call(s32[16]{0:T(128)S(4)} %get-tuple-element.48.refs_0_, f32[384,256]{1,0:T(8,128)S(1)} %get-tuple-element.82.refs_1_, bf16[384,256]{1,0:T(8,128)(2,1)S(1)} %collective-permute-done.6.refs_2_, bf16[256,256]{1,0:T(8,128)(2,1)S(1)} %collective-permute-done.7.refs_3_, ...), custom_call_target="tpu_custom_call" | custom-call | tf_op jit(solution)/shard_map/finish/pallas_call | solution.py:668
  (2 shorter events, 0.0 us)
Async XLA Ops:
  0.6 5.0 %copy-start.1 = (s32[12]{0:T(128)S(1)}, s32[12]{0:T(128)}, u32[]{:S(2)}) copy-start(s32[12]{0:T(128)} %param.11) | copy-start | bytes 148
  0.6 5.0 %copy-start.2 = (s32[12]{0:T(128)S(1)}, s32[12]{0:T(128)}, u32[]{:S(2)}) copy-start(s32[12]{0:T(128)} %param.10) | copy-start | bytes 148
  0.7 5.7 %copy-start = (bf16[384,2048]{1,0:T(8,128)(2,1)S(1)}, bf16[384,2048]{1,0:T(8,128)(2,1)}, u32[]{:S(2)}) copy-start(bf16[384,2048]{1,0:T(8,128)(2,1)} %refs_0_.3) | copy-start | bytes 4718596
  1.9 8.8 %collective-permute-start.4 = (bf16[384,256]{1,0:T(8,128)(2,1)S(1)}, bf16[384,256]{1,0:T(8,128)(2,1)S(1)}, u32[]{:S(2)}, u32[]{:S(2)}) collective-permute-start(bf16[384,256]{1,0:T(8,128)(2,1)S(1)} %pad_maximum_fusion.refs_3_), channel_id=1, source_target_pairs={{0,8},{4,12},{8,0},{12,4},{1,9},{5,13},{9,1},{13,5},{2,10},{6,14},... | collective-permute-start | bytes 589832 | tf_op jit(solution)/shard_map/ppermute | solution.py:520
  4.9 1.4 %collective-permute-start = (bf16[384,256]{1,0:T(8,128)(2,1)S(1)}, bf16[384,256]{1,0:T(8,128)(2,1)S(1)}, u32[]{:S(2)}, u32[]{:S(2)}) collective-permute-start(bf16[384,256]{1,0:T(8,128)(2,1)S(1)} %pad_maximum_fusion.refs_3_), channel_id=1, source_target_pairs={{0,4},{4,0},{8,12},{12,8},{1,5},{5,1},{9,13},{13,9},{2,6},{6,2},{1... | collective-permute-start | bytes 589832 | tf_op jit(solution)/shard_map/ppermute | solution.py:519
  4.9 9.1 %collective-permute-start.2 = (bf16[384,256]{1,0:T(8,128)(2,1)S(1)}, bf16[384,256]{1,0:T(8,128)(2,1)S(1)}, u32[]{:S(2)}, u32[]{:S(2)}) collective-permute-start(bf16[384,256]{1,0:T(8,128)(2,1)S(1)} %pad_maximum_fusion.1.refs_3_), channel_id=1, source_target_pairs={{0,8},{4,12},{8,0},{12,4},{1,9},{5,13},{9,1},{13,5},{2,10},{6,14},... | collective-permute-start | bytes 589832 | tf_op jit(solution)/shard_map/ppermute | solution.py:520
  5.1 5.5 %collective-permute-start.1 = (bf16[384,256]{1,0:T(8,128)(2,1)S(1)}, bf16[384,256]{1,0:T(8,128)(2,1)S(1)}, u32[]{:S(2)}, u32[]{:S(2)}) collective-permute-start(bf16[384,256]{1,0:T(8,128)(2,1)S(1)} %pad_maximum_fusion.1.refs_3_), channel_id=1, source_target_pairs={{0,4},{4,0},{8,12},{12,8},{1,5},{5,1},{9,13},{13,9},{2,6},{6,2},{1... | collective-permute-start | bytes 589832 | tf_op jit(solution)/shard_map/ppermute | solution.py:519
  10.6 3.4 %collective-permute-start.5 = (bf16[384,256]{1,0:T(8,128)(2,1)S(1)}, bf16[384,256]{1,0:T(8,128)(2,1)S(1)}, u32[]{:S(2)}, u32[]{:S(2)}) collective-permute-start(bf16[384,256]{1,0:T(8,128)(2,1)S(1)} %collective-permute-done.4.refs_12_), channel_id=1, source_target_pairs={{0,4},{4,0},{8,12},{12,8},{1,5},{5,1},{9,13},{13,9},{2,6},{6,2},{1... | collective-permute-start | bytes 589832 | tf_op jit(solution)/shard_map/ppermute | solution.py:587
  14.0 13.4 %collective-permute-start.3 = (bf16[384,256]{1,0:T(8,128)(2,1)S(1)}, bf16[384,256]{1,0:T(8,128)(2,1)S(1)}, u32[]{:S(2)}, u32[]{:S(2)}) collective-permute-start(bf16[384,256]{1,0:T(8,128)(2,1)S(1)} %collective-permute-done.2.refs_12_), channel_id=1, source_target_pairs={{0,4},{4,0},{8,12},{12,8},{1,5},{5,1},{9,13},{13,9},{2,6},{6,2},{1... | collective-permute-start | bytes 589832 | tf_op jit(solution)/shard_map/ppermute | solution.py:592
  25.2 15.6 %collective-permute-start.7 = (bf16[256,256]{1,0:T(8,128)(2,1)S(1)}, bf16[256,256]{1,0:T(8,128)(2,1)S(1)}, u32[]{:S(2)}, u32[]{:S(2)}) collective-permute-start(bf16[256,256]{1,0:T(8,128)(2,1)S(1)} %get-tuple-element.77), channel_id=1, source_target_pairs={{0,8},{4,12},{8,0},{12,4},{1,9},{5,13},{9,1},{13,5},{2,10},{6,14},... | collective-permute-start | bytes 393224 | tf_op jit(solution)/shard_map/ppermute | solution.py:637
  27.0 13.8 %collective-permute-start.8 = (bf16[256,256]{1,0:T(8,128)(2,1)S(1)}, bf16[256,256]{1,0:T(8,128)(2,1)S(1)}, u32[]{:S(2)}, u32[]{:S(2)}) collective-permute-start(bf16[256,256]{1,0:T(8,128)(2,1)S(1)} %get-tuple-element.78), channel_id=1, source_target_pairs={{0,12},{4,8},{8,4},{12,0},{1,13},{5,9},{9,5},{13,1},{2,14},{6,10},... | collective-permute-start | bytes 393224 | tf_op jit(solution)/shard_map/ppermute | solution.py:638
  27.2 13.6 %collective-permute-start.6 = (bf16[384,256]{1,0:T(8,128)(2,1)S(1)}, bf16[384,256]{1,0:T(8,128)(2,1)S(1)}, u32[]{:S(2)}, u32[]{:S(2)}) collective-permute-start(bf16[384,256]{1,0:T(8,128)(2,1)S(1)} %get-tuple-element.76), channel_id=1, source_target_pairs={{0,4},{4,0},{8,12},{12,8},{1,5},{5,1},{9,13},{13,9},{2,6},{6,2},{1... | collective-permute-start | bytes 589832 | tf_op jit(solution)/shard_map/ppermute | solution.py:636
  38.7 8.0 %collective-permute-start.9 = (bf16[384,256]{1,0:T(8,128)(2,1)S(1)}, bf16[384,256]{1,0:T(8,128)(2,1)S(1)}, u32[]{:S(2)}, u32[]{:S(2)}) collective-permute-start(bf16[384,256]{1,0:T(8,128)(2,1)S(1)} %get-tuple-element.87), channel_id=1, source_target_pairs={{0,4},{4,0},{8,12},{12,8},{1,5},{5,1},{9,13},{13,9},{2,6},{6,2},{1... | collective-permute-start | bytes 589832 | tf_op jit(solution)/shard_map/ppermute | solution.py:636
  39.1 6.3 %collective-permute-start.10 = (bf16[256,256]{1,0:T(8,128)(2,1)S(1)}, bf16[256,256]{1,0:T(8,128)(2,1)S(1)}, u32[]{:S(2)}, u32[]{:S(2)}) collective-permute-start(bf16[256,256]{1,0:T(8,128)(2,1)S(1)} %get-tuple-element.88), channel_id=1, source_target_pairs={{0,8},{4,12},{8,0},{12,4},{1,9},{5,13},{9,1},{13,5},{2,10},{6,14},... | collective-permute-start | bytes 393224 | tf_op jit(solution)/shard_map/ppermute | solution.py:637
  40.8 6.0 %collective-permute-start.11 = (bf16[256,256]{1,0:T(8,128)(2,1)S(1)}, bf16[256,256]{1,0:T(8,128)(2,1)S(1)}, u32[]{:S(2)}, u32[]{:S(2)}) collective-permute-start(bf16[256,256]{1,0:T(8,128)(2,1)S(1)} %get-tuple-element.89), channel_id=1, source_target_pairs={{0,12},{4,8},{8,4},{12,0},{1,13},{5,9},{9,5},{13,1},{2,14},{6,10},... | collective-permute-start | bytes 393224 | tf_op jit(solution)/shard_map/ppermute | solution.py:638

commit v7 on v6

--- a/solution.py
+++ b/solution.py
@@ -232,7 +232,7 @@
 
 def norm_top(rows):
     wide = rows.astype(F32)
-    return jnp.max(jnp.sum(wide * wide, axis=1, keepdims=True))
+    return jnp.sum(jnp.max(wide * wide, axis=0, keepdims=True))
 
 
 def causal(width):

time: 48 us -> 47.8 us (level)
  no operation moved by 1% of the time
where the time goes in v7:
time: 47.8 us; the launch traced here: 47.6 us
  Pallas kernels  33.1 us (69%)
  starting transfers between devices  7.92 us (17%)
  waiting for transfers between devices  4.46 us (9%)
  local copies, waits for them, and re-layouts  1.2 us (3%)
  between operations  0.75 us (2%)
    pallas_call x2, Pallas kernels, linked_body(): pl.pallas_call(functools.partial(far_kernel, head=h, blocks=blocks, group...  22.3 us
    pallas_call x2, Pallas kernels, near_work(): pl.pallas_call(functools.partial(near_kernel, head=h, blocks=blocks, head...  5.73 us
    pallas_call x2, Pallas kernels, linked_body(): pl.pallas_call(functools.partial(tail_kernel, head=h, blocks=blocks, grou...  4.17 us
    ppermute x2, starting transfers between devices, linked_body(): lax.ppermute(to_far, 'ctx', across)  3.45 us
    ppermute x2, starting transfers between devices, linked_body(): far = [lax.ppermute(own, 'ctx', across) for own in packed]  3.19 us
    ppermute x2, waiting for transfers between devices, linked_body(): far = [lax.ppermute(own, 'ctx', across) for own in packed]  1.92 us
    ppermute x2, waiting for transfers between devices, linked_body(): lax.ppermute(to_corner, 'ctx', corner)  1.39 us
    slice x1, local copies, waits for them, and re-layouts, body(): key_states[:, h * D:(h + 1) * D]  1.18 us
  transfers between devices with their start and end apart: 12, of which 5 were waited for; matrix products, arithmetic and copies ran while one was open for 0% of the time, Pallas kernels for 68%

profile of v7, /device:TPU:0, one launch (start us, length us, event | category | flops | bytes accessed | tf_op | source)
XLA Modules:
  0.0 47.6 jit_solution(5260223227973168322)
XLA Ops:
  0.6 0.0 copy-start.1
  0.6 0.0 copy-start.2
  0.7 0.0 copy-start
  0.7 1.2 %fusion = (bf16[384,128]{1,0:T(8,128)(2,1)S(1)}, bf16[384,128]{1,0:T(8,128)(2,1)S(1)}, bf16[384,128]{1,0:T(8,128)(2,1)S(1)}, bf16[384,128]{1,0:T(8,128)(2,1)S(1)}) fusion(bf16[384,256]{1,0:T(8,128)(2,1)} %param.7, bf16[384,256]{1,0:T(8,128)(2,1)} %param.8), kind=kLoop, calls=%fused_computation.3 | loop fusion | bytes 786432 | tf_op jit(solution)/shard_map/slice | solution.py:684
  1.9 3.0 %collective-permute-start.4 = (bf16[384,256]{1,0:T(8,128)(2,1)S(1)}, bf16[384,256]{1,0:T(8,128)(2,1)S(1)}, u32[]{:S(2)}, u32[]{:S(2)}) collective-permute-start(bf16[384,256]{1,0:T(8,128)(2,1)S(1)} %pad_maximum_fusion.refs_3_), channel_id=1, source_target_pairs={{0,8},{4,12},{8,0},{12,4},{1,9},{5,13},{9,1},{13,5},{2,10},{6,14},... | collective-permute-start | bytes 589832 | tf_op jit(solution)/shard_map/ppermute | solution.py:520
  4.9 0.0 collective-permute-start
  4.9 0.2 collective-permute-start.2
  5.1 0.5 %collective-permute-start.1 = (bf16[384,256]{1,0:T(8,128)(2,1)S(1)}, bf16[384,256]{1,0:T(8,128)(2,1)S(1)}, u32[]{:S(2)}, u32[]{:S(2)}) collective-permute-start(bf16[384,256]{1,0:T(8,128)(2,1)S(1)} %pad_maximum_fusion.1.refs_3_), channel_id=1, source_target_pairs={{0,4},{4,0},{8,12},{12,8},{1,5},{5,1},{9,13},{13,9},{2,6},{6,2},{1... | collective-permute-start | bytes 589832 | tf_op jit(solution)/shard_map/ppermute | solution.py:519
  5.6 0.0 copy-done.1
  5.6 0.0 copy-done.2
  5.6 0.1 pad_add_fusion.refs_0_
  5.7 0.7 %collective-permute-done.refs_4_ = bf16[384,256]{1,0:T(8,128)(2,1)S(1)} collective-permute-done((bf16[384,256]{1,0:T(8,128)(2,1)S(1)}, bf16[384,256]{1,0:T(8,128)(2,1)S(1)}, u32[]{:S(2)}, u32[]{:S(2)}) %collective-permute-start) | collective-permute-done | bytes 196640 | tf_op jit(solution)/shard_map/ppermute | solution.py:519
  6.4 0.0 copy-done
  6.4 4.0 %near.2 = (s32[16]{0:T(128)S(4)}, f32[2]{0:T(128)S(4)}, bf16[384,2048]{1,0:T(8,128)(2,1)S(1)}, bf16[3,128,2048]{2,1,0:T(8,128)(2,1)S(1)}, bf16[3,128,2048]{2,1,0...) custom-call(s32[25]{0:T(128)S(1)} %pad_add_fusion.refs_0_, ...), custom_call_target="tpu_custom_call" | custom-call | flops 4000000000 | tf_op jit(solution)/shard_map/near/pallas_call | solution.py:563
  10.3 0.3 collective-permute-done.4.refs_12_
  10.6 0.0 collective-permute-start.5
  10.6 0.0 collective-permute-done.1.refs_4_
  10.7 1.8 %near.3 = (f32[1]{0:T(128)S(4)}, bf16[3,256,128]{2,1,0:T(8,128)(2,1)S(1)}, bf16[3,144,256]{2,1,0:T(8,128)(2,1)S(1)}, bf16[3,256,1024]{2,1,0:T(8,128)(2,1)S(1)}, ...) custom-call(s32[16]{0:T(128)S(4)} %get-tuple-element.48.refs_0_, ...), custom_call_target="tpu_custom_call" | custom-call | flops 4000000000 | tf_op jit(solution)/shard_map/near/pallas_call | solution.py:563
  12.4 1.6 %collective-permute-done.2.refs_12_ = bf16[384,256]{1,0:T(8,128)(2,1)S(1)} collective-permute-done((bf16[384,256]{1,0:T(8,128)(2,1)S(1)}, bf16[384,256]{1,0:T(8,128)(2,1)S(1)}, u32[]{:S(2)}, u32[]{:S(2)}) %collective-permute-start.2) | collective-permute-done | bytes 196640 | tf_op jit(solution)/shard_map/ppermute | solution.py:520
  14.0 0.0 collective-permute-start.3
  14.0 0.0 collective-permute-done.5.refs_13_
  14.0 11.1 %far.2 = (bf16[384,2048]{1,0:T(8,128)(2,1)}, bf16[3,256,1024]{2,1,0:T(8,128)(2,1)S(1)}, bf16[3,384,1024]{2,1,0:T(8,128)(2,1)S(1)}, bf16[3,384,128]{2,1,0:T(8,128...) custom-call(s32[16]{0:T(128)S(4)} %get-tuple-element.48.refs_0_, ...), custom_call_target="tpu_custom_call", output_to_operand_aliasing={{1}: (9, {})} | custom-call | flops 5000000000 | tf_op jit(solution)/shard_map/far/pallas_call | solution.py:602
  25.1 1.8 %collective-permute-start.7 = (bf16[256,256]{1,0:T(8,128)(2,1)S(1)}, bf16[256,256]{1,0:T(8,128)(2,1)S(1)}, u32[]{:S(2)}, u32[]{:S(2)}) collective-permute-start(bf16[256,256]{1,0:T(8,128)(2,1)S(1)} %get-tuple-element.77), channel_id=1, source_target_pairs={{0,8},{4,12},{8,0},{12,4},{1,9},{5,13},{9,1},{13,5},{2,10},{6,14},... | collective-permute-start | bytes 393224 | tf_op jit(solution)/shard_map/ppermute | solution.py:637
  26.9 0.2 collective-permute-start.8
  27.1 0.2 collective-permute-start.6
  27.3 0.0 collective-permute-done.3.refs_13_
  27.3 11.2 %far.3 = (bf16[384,2048]{1,0:T(8,128)(2,1)}, bf16[3,256,1024]{2,1,0:T(8,128)(2,1)S(1)}, bf16[3,384,1024]{2,1,0:T(8,128)(2,1)S(1)}, bf16[3,384,128]{2,1,0:T(8,128...) custom-call(s32[16]{0:T(128)S(4)} %get-tuple-element.48.refs_0_, ...), custom_call_target="tpu_custom_call", output_to_operand_aliasing={{1}: (9, {}), {0}: (14, {})} | custom-call | flops 5000000000 | tf_op jit(solution)/shard_map/far/pallas_call | solution.py:602
  38.5 0.4 collective-permute-start.9
  38.9 1.7 %collective-permute-start.10 = (bf16[256,256]{1,0:T(8,128)(2,1)S(1)}, bf16[256,256]{1,0:T(8,128)(2,1)S(1)}, u32[]{:S(2)}, u32[]{:S(2)}) collective-permute-start(bf16[256,256]{1,0:T(8,128)(2,1)S(1)} %get-tuple-element.88), channel_id=1, source_target_pairs={{0,8},{4,12},{8,0},{12,4},{1,9},{5,13},{9,1},{13,5},{2,10},{6,14},... | collective-permute-start | bytes 393224 | tf_op jit(solution)/shard_map/ppermute | solution.py:637
  40.6 0.0 collective-permute-done.7.refs_3_
  40.6 0.0 collective-permute-start.11
  40.6 0.0 collective-permute-done.8.refs_4_
  40.6 0.0 collective-permute-done.6.refs_2_
  40.6 2.1 %tail.2 = (bf16[384,2048]{1,0:T(8,128)(2,1)}, f32[384,256]{1,0:T(8,128)S(1)}) custom-call(bf16[384,2048]{1,0:T(8,128)(2,1)S(1)} %copy-done, bf16[384,2048]{1,0:T(8,128)(2,1)S(1)} %get-tuple-element.53.refs_4_.refs_1_, bf16[3,256,128]{2,1,0:T(8,128)(2,1)S(1)} %get-tuple-element.60.refs_7_.refs_2_, bf16[3,256,1024]{2,1,0:T(8,128)(2,1)S(1)} %get-tuple-element.72.refs_3_, ...), custom_call_target="tpu_custom_call" | custom-call | flops 1000000000 | tf_op jit(solution)/shard_map/tail/pallas_call | solution.py:650
  42.7 2.1 %tail.3 = (bf16[384,2048]{1,0:T(8,128)(2,1)}, f32[384,256]{1,0:T(8,128)S(1)}) custom-call(bf16[384,2048]{1,0:T(8,128)(2,1)S(1)} %copy-done, bf16[384,2048]{1,0:T(8,128)(2,1)S(1)} %get-tuple-element.53.refs_4_.refs_1_, bf16[3,256,128]{2,1,0:T(8,128)(2,1)S(1)} %get-tuple-element.54.refs_7_.refs_2_, ...), custom_call_target="tpu_custom_call", output_to_operand_aliasing={{0}: (8, {})} | custom-call | flops 1000000000 | tf_op jit(solution)/shard_map/tail/pallas_call | solution.py:650
  44.8 0.5 collective-permute-done.10.refs_7_
  45.2 1.4 %collective-permute-done.11.refs_8_ = bf16[256,256]{1,0:T(8,128)(2,1)S(1)} collective-permute-done((bf16[256,256]{1,0:T(8,128)(2,1)S(1)}, bf16[256,256]{1,0:T(8,128)(2,1)S(1)}, u32[]{:S(2)}, u32[]{:S(2)}) %collective-permute-start.11) | collective-permute-done | bytes 131104 | tf_op jit(solution)/shard_map/ppermute | solution.py:638
  46.6 0.0 collective-permute-done.9.refs_6_
  46.6 1.0 %finish.1 = (bf16[384,256]{1,0:T(8,128)(2,1)}, bf16[384,256]{1,0:T(8,128)(2,1)}) custom-call(s32[16]{0:T(128)S(4)} %get-tuple-element.48.refs_0_, f32[384,256]{1,0:T(8,128)S(1)} %get-tuple-element.82.refs_1_, bf16[384,256]{1,0:T(8,128)(2,1)S(1)} %collective-permute-done.6.refs_2_, bf16[256,256]{1,0:T(8,128)(2,1)S(1)} %collective-permute-done.7.refs_3_, ...), custom_call_target="tpu_custom_call" | custom-call | tf_op jit(solution)/shard_map/finish/pallas_call | solution.py:668
  (2 shorter events, 0.0 us)
Async XLA Ops:
  0.6 5.0 %copy-start.1 = (s32[12]{0:T(128)S(1)}, s32[12]{0:T(128)}, u32[]{:S(2)}) copy-start(s32[12]{0:T(128)} %param.11) | copy-start | bytes 148
  0.6 5.0 %copy-start.2 = (s32[12]{0:T(128)S(1)}, s32[12]{0:T(128)}, u32[]{:S(2)}) copy-start(s32[12]{0:T(128)} %param.10) | copy-start | bytes 148
  0.7 5.7 %copy-start = (bf16[384,2048]{1,0:T(8,128)(2,1)S(1)}, bf16[384,2048]{1,0:T(8,128)(2,1)}, u32[]{:S(2)}) copy-start(bf16[384,2048]{1,0:T(8,128)(2,1)} %refs_0_.3) | copy-start | bytes 4718596
  1.9 8.8 %collective-permute-start.4 = (bf16[384,256]{1,0:T(8,128)(2,1)S(1)}, bf16[384,256]{1,0:T(8,128)(2,1)S(1)}, u32[]{:S(2)}, u32[]{:S(2)}) collective-permute-start(bf16[384,256]{1,0:T(8,128)(2,1)S(1)} %pad_maximum_fusion.refs_3_), channel_id=1, source_target_pairs={{0,8},{4,12},{8,0},{12,4},{1,9},{5,13},{9,1},{13,5},{2,10},{6,14},... | collective-permute-start | bytes 589832 | tf_op jit(solution)/shard_map/ppermute | solution.py:520
  4.9 1.4 %collective-permute-start = (bf16[384,256]{1,0:T(8,128)(2,1)S(1)}, bf16[384,256]{1,0:T(8,128)(2,1)S(1)}, u32[]{:S(2)}, u32[]{:S(2)}) collective-permute-start(bf16[384,256]{1,0:T(8,128)(2,1)S(1)} %pad_maximum_fusion.refs_3_), channel_id=1, source_target_pairs={{0,4},{4,0},{8,12},{12,8},{1,5},{5,1},{9,13},{13,9},{2,6},{6,2},{1... | collective-permute-start | bytes 589832 | tf_op jit(solution)/shard_map/ppermute | solution.py:519
  4.9 9.1 %collective-permute-start.2 = (bf16[384,256]{1,0:T(8,128)(2,1)S(1)}, bf16[384,256]{1,0:T(8,128)(2,1)S(1)}, u32[]{:S(2)}, u32[]{:S(2)}) collective-permute-start(bf16[384,256]{1,0:T(8,128)(2,1)S(1)} %pad_maximum_fusion.1.refs_3_), channel_id=1, source_target_pairs={{0,8},{4,12},{8,0},{12,4},{1,9},{5,13},{9,1},{13,5},{2,10},{6,14},... | collective-permute-start | bytes 589832 | tf_op jit(solution)/shard_map/ppermute | solution.py:520
  5.1 5.5 %collective-permute-start.1 = (bf16[384,256]{1,0:T(8,128)(2,1)S(1)}, bf16[384,256]{1,0:T(8,128)(2,1)S(1)}, u32[]{:S(2)}, u32[]{:S(2)}) collective-permute-start(bf16[384,256]{1,0:T(8,128)(2,1)S(1)} %pad_maximum_fusion.1.refs_3_), channel_id=1, source_target_pairs={{0,4},{4,0},{8,12},{12,8},{1,5},{5,1},{9,13},{13,9},{2,6},{6,2},{1... | collective-permute-start | bytes 589832 | tf_op jit(solution)/shard_map/ppermute | solution.py:519
  10.6 3.4 %collective-permute-start.5 = (bf16[384,256]{1,0:T(8,128)(2,1)S(1)}, bf16[384,256]{1,0:T(8,128)(2,1)S(1)}, u32[]{:S(2)}, u32[]{:S(2)}) collective-permute-start(bf16[384,256]{1,0:T(8,128)(2,1)S(1)} %collective-permute-done.4.refs_12_), channel_id=1, source_target_pairs={{0,4},{4,0},{8,12},{12,8},{1,5},{5,1},{9,13},{13,9},{2,6},{6,2},{1... | collective-permute-start | bytes 589832 | tf_op jit(solution)/shard_map/ppermute | solution.py:587
  14.0 13.3 %collective-permute-start.3 = (bf16[384,256]{1,0:T(8,128)(2,1)S(1)}, bf16[384,256]{1,0:T(8,128)(2,1)S(1)}, u32[]{:S(2)}, u32[]{:S(2)}) collective-permute-start(bf16[384,256]{1,0:T(8,128)(2,1)S(1)} %collective-permute-done.2.refs_12_), channel_id=1, source_target_pairs={{0,4},{4,0},{8,12},{12,8},{1,5},{5,1},{9,13},{13,9},{2,6},{6,2},{1... | collective-permute-start | bytes 589832 | tf_op jit(solution)/shard_map/ppermute | solution.py:592
  25.1 15.5 %collective-permute-start.7 = (bf16[256,256]{1,0:T(8,128)(2,1)S(1)}, bf16[256,256]{1,0:T(8,128)(2,1)S(1)}, u32[]{:S(2)}, u32[]{:S(2)}) collective-permute-start(bf16[256,256]{1,0:T(8,128)(2,1)S(1)} %get-tuple-element.77), channel_id=1, source_target_pairs={{0,8},{4,12},{8,0},{12,4},{1,9},{5,13},{9,1},{13,5},{2,10},{6,14},... | collective-permute-start | bytes 393224 | tf_op jit(solution)/shard_map/ppermute | solution.py:637
  26.9 13.7 %collective-permute-start.8 = (bf16[256,256]{1,0:T(8,128)(2,1)S(1)}, bf16[256,256]{1,0:T(8,128)(2,1)S(1)}, u32[]{:S(2)}, u32[]{:S(2)}) collective-permute-start(bf16[256,256]{1,0:T(8,128)(2,1)S(1)} %get-tuple-element.78), channel_id=1, source_target_pairs={{0,12},{4,8},{8,4},{12,0},{1,13},{5,9},{9,5},{13,1},{2,14},{6,10},... | collective-permute-start | bytes 393224 | tf_op jit(solution)/shard_map/ppermute | solution.py:638
  27.1 13.5 %collective-permute-start.6 = (bf16[384,256]{1,0:T(8,128)(2,1)S(1)}, bf16[384,256]{1,0:T(8,128)(2,1)S(1)}, u32[]{:S(2)}, u32[]{:S(2)}) collective-permute-start(bf16[384,256]{1,0:T(8,128)(2,1)S(1)} %get-tuple-element.76), channel_id=1, source_target_pairs={{0,4},{4,0},{8,12},{12,8},{1,5},{5,1},{9,13},{13,9},{2,6},{6,2},{1... | collective-permute-start | bytes 589832 | tf_op jit(solution)/shard_map/ppermute | solution.py:636
  38.5 8.1 %collective-permute-start.9 = (bf16[384,256]{1,0:T(8,128)(2,1)S(1)}, bf16[384,256]{1,0:T(8,128)(2,1)S(1)}, u32[]{:S(2)}, u32[]{:S(2)}) collective-permute-start(bf16[384,256]{1,0:T(8,128)(2,1)S(1)} %get-tuple-element.87), channel_id=1, source_target_pairs={{0,4},{4,0},{8,12},{12,8},{1,5},{5,1},{9,13},{13,9},{2,6},{6,2},{1... | collective-permute-start | bytes 589832 | tf_op jit(solution)/shard_map/ppermute | solution.py:636
  38.9 6.3 %collective-permute-start.10 = (bf16[256,256]{1,0:T(8,128)(2,1)S(1)}, bf16[256,256]{1,0:T(8,128)(2,1)S(1)}, u32[]{:S(2)}, u32[]{:S(2)}) collective-permute-start(bf16[256,256]{1,0:T(8,128)(2,1)S(1)} %get-tuple-element.88), channel_id=1, source_target_pairs={{0,8},{4,12},{8,0},{12,4},{1,9},{5,13},{9,1},{13,5},{2,10},{6,14},... | collective-permute-start | bytes 393224 | tf_op jit(solution)/shard_map/ppermute | solution.py:637
  40.6 6.1 %collective-permute-start.11 = (bf16[256,256]{1,0:T(8,128)(2,1)S(1)}, bf16[256,256]{1,0:T(8,128)(2,1)S(1)}, u32[]{:S(2)}, u32[]{:S(2)}) collective-permute-start(bf16[256,256]{1,0:T(8,128)(2,1)S(1)} %get-tuple-element.89), channel_id=1, source_target_pairs={{0,12},{4,8},{8,4},{12,0},{1,13},{5,9},{9,5},{13,1},{2,14},{6,10},... | collective-permute-start | bytes 393224 | tf_op jit(solution)/shard_map/ppermute | solution.py:638
